TPU v7x, 32 devices: a whole 2x2x4 slice. The times are simulated.
32 devices in a mesh: seq: 8 (over y, x, core), batch: 4 (over z).
Axes of the slice: x: 2, y: 2, z: 4, core: 2. Of those that a mesh axis runs over, the one named last changes fastest.
Arguments:
- token_ids: int32 [4, 1024], P('batch', 'seq'), may hold values from 0 to 50303
- pos_weights: int32 [4, 1024], P('batch', 'seq'), may hold values from 1 to 4, as said below
- pad_lengths: int32 [4], P('batch'), may hold values from 0 to 511, as said below
- embed_in: bfloat16 [50304, 1024], P('batch'), may hold values from -20 to 20
- w_qkv: bfloat16 [1024, 3072], P(('seq', 'batch')), may hold values from -0.1875 to 0.1875
- w_out: bfloat16 [1024, 1024], P(('seq', 'batch')), may hold values from -1.5 to 1.5
- w_fc: bfloat16 [1024, 4096], P(('seq', 'batch')), may hold values from -0.1875 to 0.1875
- w_proj: bfloat16 [4096, 1024], P(('seq', 'batch')), may hold values from -0.1875 to 0.1875
- norm_gains: float32 [3, 1024], replicated, may hold values from 0.5 to 1.5
- layer_biases: float32 [5, 1024], replicated, may hold values from -1.2 to 1.2
- wide_bias: float32 [7168], replicated, may hold values from -1.2 to 1.2
- unembed: bfloat16 [50304, 1024], P('batch'), may hold values from -0.375 to 0.375
- trans_weight: float32 [2, 1024, 1024], P(None, 'seq'), may hold values from -0.1875 to 0.1875
- trans_bias: float32 [2, 1024], P(None, 'seq'), may hold values from -0.6 to 0.6
- mom1_weight: float32 [2, 1024, 1024], P(None, 'seq'), may hold values from -4.5553006e-07 to 4.5553006e-07
- mom2_weight: float32 [2, 1024, 1024], P(None, 'seq'), may hold values from 4.7637196e-16 to 1.9054879e-15
- mom1_bias: float32 [2, 1024], P(None, 'seq'), may hold values from -1.3803941e-06 to 1.3803941e-06
- mom2_bias: float32 [2, 1024], P(None, 'seq'), may hold values from 4.7637196e-16 to 1.9054879e-15
Outputs:
- loss_sum: float32 [], replicated
- token_count: float32 [], replicated
- grad_norm: float32 [], replicated
- new_mom1_weight: float32 [2, 1024, 1024], P(None, 'seq')
- new_mom2_weight: float32 [2, 1024, 1024], P(None, 'seq')
- new_trans_weight: float32 [2, 1024, 1024], P(None, 'seq')
- new_mom1_bias: float32 [2, 1024], P(None, 'seq')
- new_mom2_bias: float32 [2, 1024], P(None, 'seq')
- new_trans_bias: float32 [2, 1024], P(None, 'seq')
Inputs may be any that keep to these rules, and one draw needn't show every extreme that they name: `pos_weights`: 1 at positions before 128; from 128 on 2 to 4. `pad_lengths`: under half of 1024; one sequence has none, another has the most.
All inputs are finite; a program needn't handle non-finite values.
Results may differ from a plain program's by a relative error of at most 0.014.
Values may be sent and summed in bfloat16 or wider, within the bound.
A program may use at most 384 MiB of HBM per device.

v0:
```python
import jax
import jax.numpy as jnp
from jax import lax
from jax.sharding import PartitionSpec as P

HEAD_DIM = 64
ROT = 16
STEP = 10


norm_eps = 1e-05
clip_max = 0.001
beta_one = 0.9
beta_two = 0.999
learn_rate = 0.03
decay_rate = 0.01
adam_eps = 1e-08


def merged(part, axis, combine):
    gathered = jax.tree.map(lambda a: lax.all_gather(a, axis), part)

    def take(source):
        return jax.tree.map(lambda a: lax.dynamic_index_in_dim(a, source, 0, False), gathered)

    return lax.fori_loop(
        1, lax.axis_size(axis), lambda source, state: combine(state, take(source)), take(0)
    )


def normalize(values, gain_row, offset_row):
    average = jnp.mean(values, axis=-1, keepdims=True)
    centered = values - average
    variance = jnp.mean(centered * centered, axis=-1, keepdims=True)
    return centered * lax.rsqrt(variance + norm_eps) * gain_row + offset_row


def norm_back(values, upstream, gain_row):
    average = jnp.mean(values, axis=-1, keepdims=True)
    centered = values - average
    variance = jnp.mean(centered * centered, axis=-1, keepdims=True)
    inverse = lax.rsqrt(variance + norm_eps)
    unit = centered * inverse
    scaled = upstream * gain_row
    return (
        scaled
        - jnp.mean(scaled, axis=-1, keepdims=True)
        - unit * jnp.mean(scaled * unit, axis=-1, keepdims=True)
    ) * inverse


def rotate(vectors, places):
    half_rot = ROT // 2
    frequency = 10000.0 ** (-2.0 * jnp.arange(half_rot, dtype=jnp.float32) / ROT)
    angles = places.astype(jnp.float32)[:, None] * frequency[None, :]
    cosine = jnp.cos(angles)[:, None, :]
    sine = jnp.sin(angles)[:, None, :]
    lower_part = vectors[..., :half_rot]
    upper_part = vectors[..., half_rot:ROT]
    return jnp.concatenate(
        [
            lower_part * cosine - upper_part * sine,
            upper_part * cosine + lower_part * sine,
            vectors[..., ROT:],
        ],
        axis=-1,
    )


def adam_update(weight, gradient, earlier, later):
    earlier = beta_one * earlier + (1.0 - beta_one) * gradient
    later = beta_two * later + (1.0 - beta_two) * gradient * gradient
    update = (
        earlier / (1.0 - beta_one**STEP) / (jnp.sqrt(later / (1.0 - beta_two**STEP)) + adam_eps)
    )
    return (earlier, later, weight * (1.0 - learn_rate * decay_rate) - learn_rate * update)


def body(
    token_ids,
    pos_weights,
    pad_lengths,
    embed_in,
    w_qkv,
    w_out,
    w_fc,
    w_proj,
    norm_gains,
    layer_biases,
    wide_bias,
    unembed,
    trans_weight,
    trans_bias,
    mom1_weight,
    mom2_weight,
    mom1_bias,
    mom2_bias,
):
    tok_rows = token_ids.shape[1]
    width = embed_in.shape[1]
    vocab_rows = unembed.shape[0]
    n_seq = lax.axis_size("seq")
    batch_index = lax.axis_index("batch")
    seq_index = lax.axis_index("seq")
    all_ids, all_weights, all_padding = (
        lax.all_gather(token_ids, "batch", axis=0, tiled=True),
        lax.all_gather(pos_weights, "batch", axis=0, tiled=True),
        lax.all_gather(pad_lengths, "batch", axis=0, tiled=True),
    )
    local_places = seq_index * tok_rows + jnp.arange(tok_rows, dtype=jnp.int32)
    living = local_places[None, :] < (tok_rows * n_seq - all_padding)[:, None]
    weight_all = jnp.where(living, all_weights, 0).astype(jnp.float32)
    weight_own = lax.dynamic_slice_in_dim(weight_all, batch_index, 1, 0)[0]
    token_count = lax.psum(jnp.sum(weight_own), ("seq", "batch"))
    flat_ids = all_ids.reshape(-1)
    vocab_start = batch_index * vocab_rows
    wanted = flat_ids - vocab_start
    inside = (wanted >= 0) & (wanted < vocab_rows)
    picked = jnp.take(embed_in, jnp.clip(wanted, 0, vocab_rows - 1), axis=0)
    stream0 = lax.psum_scatter(
        jnp.where(inside[:, None], picked.astype(jnp.float32), 0.0).astype(jnp.bfloat16),
        "batch",
        scatter_dimension=0,
        tiled=True,
    ).astype(jnp.float32)
    joined_w, out_w, fc_w, proj_w = (
        lax.all_gather(w_qkv, ("seq", "batch"), axis=0, tiled=True),
        lax.all_gather(w_out, ("seq", "batch"), axis=0, tiled=True),
        lax.all_gather(w_fc, ("seq", "batch"), axis=0, tiled=True),
        lax.all_gather(w_proj, ("seq", "batch"), axis=0, tiled=True),
    )
    trans_full, bias_full = (
        lax.all_gather(trans_weight.astype(jnp.bfloat16), "seq", axis=1, tiled=True).astype(
            trans_weight.dtype
        ),
        lax.all_gather(trans_bias.astype(jnp.bfloat16), "seq", axis=1, tiled=True).astype(
            trans_bias.dtype
        ),
    )
    head_count = width // HEAD_DIM
    x_attn = normalize(stream0, norm_gains[0], layer_biases[0]).astype(jnp.bfloat16)
    x_mlp = normalize(stream0, norm_gains[1], layer_biases[1]).astype(jnp.bfloat16)
    joined = (
        jnp.dot(x_attn, joined_w, preferred_element_type=jnp.float32) + wide_bias[: 3 * width]
    ).reshape(tok_rows, 3, head_count, HEAD_DIM)
    queries = rotate(joined[:, 0], local_places).astype(jnp.bfloat16)
    key_rows = rotate(joined[:, 1], local_places).astype(jnp.bfloat16).reshape(tok_rows, width)
    value_rows = joined[:, 2].astype(jnp.bfloat16).reshape(tok_rows, width)
    peaks = jnp.full((head_count, tok_rows), -1e30, jnp.float32)
    key_part = lax.all_gather(key_rows, "seq", axis=0, tiled=True).reshape(-1, head_count, HEAD_DIM)
    value_part = lax.all_gather(value_rows, "seq", axis=0, tiled=True).reshape(
        -1, head_count, HEAD_DIM
    )
    scores = jnp.einsum(
        "qhd,khd->hqk", queries, key_part, preferred_element_type=jnp.float32
    ) * HEAD_DIM ** (-0.5)
    key_places = jnp.arange(key_part.shape[0], dtype=jnp.int32)
    allowed = (key_places[None, :] <= local_places[:, None])[None]
    scores = jnp.where(allowed, scores, -1e30)
    new_peaks = jnp.maximum(peaks, jnp.max(scores, axis=-1))
    exponent = jnp.where(allowed, jnp.exp(scores - new_peaks[..., None]), 0.0)
    weighted = jnp.einsum(
        "hqk,khd->hqd",
        exponent.astype(jnp.bfloat16),
        value_part,
        preferred_element_type=jnp.float32,
    )
    weighted, peaks, summed = (weighted, new_peaks, jnp.sum(exponent, axis=-1))
    attended = (
        jnp.transpose(weighted / summed[..., None], (1, 0, 2))
        .reshape(tok_rows, width)
        .astype(jnp.bfloat16)
    )
    attn = jnp.dot(attended, out_w, preferred_element_type=jnp.float32) + layer_biases[2]
    hidden = jax.nn.gelu(
        jnp.dot(x_mlp, fc_w, preferred_element_type=jnp.float32) + wide_bias[3 * width :],
        approximate=False,
    ).astype(jnp.bfloat16)
    stream1 = (
        stream0
        + attn
        + jnp.dot(hidden, proj_w, preferred_element_type=jnp.float32)
        + layer_biases[3]
    )
    gain_final = norm_gains[2]
    offset_final = layer_biases[4]
    probe_in = (stream0, stream1)
    probe_low = (stream0.astype(jnp.bfloat16), stream1.astype(jnp.bfloat16))
    trans_low = trans_full.astype(jnp.bfloat16)
    translated = [
        probe_in[index]
        + jnp.dot(probe_low[index], trans_low[index], preferred_element_type=jnp.float32)
        + bias_full[index]
        for index in range(2)
    ]
    states = jnp.stack(
        [
            normalize(stream1, gain_final, offset_final),
            normalize(translated[0], gain_final, offset_final),
            normalize(translated[1], gain_final, offset_final),
        ]
    ).astype(jnp.bfloat16)
    gathered = lax.all_gather(states, "batch", axis=1, tiled=True)
    all_rows = gathered.shape[1]

    def block_size():
        return 512

    def block_stats(offset):
        portion = lax.dynamic_slice_in_dim(gathered, offset, block_size(), 1)
        logits = jnp.einsum("std,vd->stv", portion, unembed, preferred_element_type=jnp.float32)
        peak_rows = jnp.max(logits, axis=-1)
        exponent = jnp.exp(logits - peak_rows[..., None])
        crossing = jnp.sum(exponent[0][None] * (logits[0][None] - logits[1:]), axis=-1)
        return (peak_rows, jnp.sum(exponent, axis=-1), crossing)

    stat_offsets = jnp.arange(all_rows // block_size(), dtype=jnp.int32) * block_size()
    peak_all, sums_all, cross_all = lax.map(block_stats, stat_offsets)
    peak_all = jnp.transpose(peak_all, (1, 0, 2)).reshape(3, all_rows)
    sums_all = jnp.transpose(sums_all, (1, 0, 2)).reshape(3, all_rows)
    cross_all = jnp.transpose(cross_all, (1, 0, 2)).reshape(2, all_rows)

    def combine(earlier, later):
        peak_a, sums_a, cross_a = earlier
        peak_b, sums_b, cross_b = later
        peak_new = jnp.maximum(peak_a, peak_b)
        factor_a = jnp.exp(peak_a - peak_new)
        factor_b = jnp.exp(peak_b - peak_new)
        return (
            peak_new,
            sums_a * factor_a + sums_b * factor_b,
            cross_a * factor_a[0] + cross_b * factor_b[0],
        )

    peak_all, sums_all, cross_all = merged((peak_all, sums_all, cross_all), "batch", combine)
    log_totals = peak_all + jnp.log(sums_all)
    diverge = cross_all / sums_all[0] - log_totals[0] + log_totals[1:]
    diverge_own = lax.dynamic_slice_in_dim(diverge, batch_index * tok_rows, tok_rows, 1)
    loss_local = jnp.sum(weight_own * (diverge_own[0] + diverge_own[1]))
    token_coef = weight_all.reshape(-1) / token_count
    size = block_size()

    def block_grads(inner):
        portion = lax.dynamic_slice_in_dim(gathered, inner, size, 1)
        totals_part = lax.dynamic_slice_in_dim(log_totals, inner, size, 1)
        coef_part = lax.dynamic_slice_in_dim(token_coef, inner, size, 0)
        logits = jnp.einsum("std,vd->stv", portion, unembed, preferred_element_type=jnp.float32)
        probs = jnp.exp(logits - totals_part[..., None])
        dlogits = (coef_part[None, :, None] * (probs[1:] - probs[0][None])).astype(jnp.bfloat16)
        return jnp.einsum(
            "sbv,vd->bsd", dlogits, unembed, preferred_element_type=jnp.float32
        ).reshape(size, 2 * width)

    inner_offsets = jnp.arange(tok_rows * lax.axis_size("batch") // size, dtype=jnp.int32) * size
    dstates = (
        lax.psum_scatter(
            lax.map(block_grads, inner_offsets)
            .reshape(tok_rows * lax.axis_size("batch"), 2 * width)
            .astype(jnp.bfloat16),
            "batch",
            scatter_dimension=0,
            tiled=True,
        )
        .astype(jnp.float32)
        .reshape(tok_rows, 2, width)
    )
    grad_w_list = []
    grad_b_list = []
    for index in range(2):
        delta = norm_back(translated[index], dstates[:, index], gain_final)
        grad_w_list.append(
            jnp.einsum(
                "td,te->de",
                probe_low[index],
                delta.astype(jnp.bfloat16),
                preferred_element_type=jnp.float32,
            )
        )
        grad_b_list.append(jnp.sum(delta, axis=0))
    grad_w = jnp.stack(grad_w_list)
    grad_b = jnp.stack(grad_b_list)
    grad_w, grad_b = (
        lax.psum(grad_w.astype(jnp.bfloat16), "batch").astype(jnp.float32),
        lax.psum(grad_b.astype(jnp.bfloat16), "batch").astype(jnp.float32),
    )
    grad_w, grad_b = (
        lax.psum_scatter(
            grad_w.astype(jnp.bfloat16), "seq", scatter_dimension=1, tiled=True
        ).astype(jnp.float32),
        lax.psum_scatter(
            grad_b.astype(jnp.bfloat16), "seq", scatter_dimension=1, tiled=True
        ).astype(jnp.float32),
    )
    squares = jnp.sum(grad_w * grad_w) + jnp.sum(grad_b * grad_b)
    first_copy = (batch_index == 0).astype(jnp.float32)
    loss_sum, norm_square = lax.psum((loss_local, squares * first_copy), ("seq", "batch"))
    grad_norm = jnp.sqrt(norm_square)
    factor = jnp.minimum(1.0, clip_max / (grad_norm + 1e-06))
    first_w, second_w, new_w = adam_update(trans_weight, grad_w * factor, mom1_weight, mom2_weight)
    first_b, second_b, new_b = adam_update(trans_bias, grad_b * factor, mom1_bias, mom2_bias)
    return (loss_sum, token_count, grad_norm, first_w, second_w, new_w, first_b, second_b, new_b)


def solution(mesh):
    return jax.shard_map(
        body,
        mesh=mesh,
        in_specs=(
            P("batch", "seq"),
            P("batch", "seq"),
            P("batch"),
            P("batch", None),
            P(("seq", "batch"), None),
            P(("seq", "batch"), None),
            P(("seq", "batch"), None),
            P(("seq", "batch"), None),
            P(),
            P(),
            P(),
            P("batch", None),
            P(None, "seq", None),
            P(None, "seq"),
            P(None, "seq", None),
            P(None, "seq", None),
            P(None, "seq"),
            P(None, "seq"),
        ),
        out_specs=(
            P(),
            P(),
            P(),
            P(None, "seq", None),
            P(None, "seq", None),
            P(None, "seq", None),
            P(None, "seq"),
            P(None, "seq"),
            P(None, "seq"),
        ),
        check_vma=False,
    )
```

profile of v0, /device:TPU:0, one launch (start us, length us, event | category | flops | bytes accessed | tf_op | source)
XLA Modules:
  0.0 1074.4 jit_solution(2313814447790069991)
XLA Ops:
  8.1 12.7 %all-gather.4 = s32[4,1,128]{2,1,0:T(1,128)S(1)} all-gather(s32[1,1,128]{2,1,0:T(1,128)} %bitcast.190), channel_id=1, replica_groups=mesh['seq'=8,'batch'=4] {'batch'}, dimensions={0}, use_global_device_ids=true | all-gather | bytes 2560 | tf_op jit(solution)/shard_map/all_gather | solution.py:106
  20.8 14.4 %gather_fusion = bf16[512,1024]{1,0:T(8,128)(2,1)S(1)} fusion(bf16[12576,1024]{1,0:T(8,128)(2,1)} %param.23, s32[1024]{0:T(1024)S(1)} %pad_clamp_fusion), kind=kCustom, calls=%fused_computation | custom fusion | bytes 2099200 | tf_op jit(solution)/shard_map/jit(_take)/gather | solution.py:119
  38.4 26.5 %reduce-scatter.9.cloned.1.call-done = bf16[128,1024]{1,0:T(8,128)(2,1)} async-done(((bf16[512,1024]{1,0:T(8,128)(2,1)}), bf16[128,1024]{1,0:T(8,128)(2,1)}) %reduce-scatter.9.cloned.1.call-update) | async-done | bytes 262160 | tf_op jit(solution)/shard_map/reduce_scatter | solution.py:120
  67.2 47.8 %all-gather.17.cloned.1.call-done = bf16[1024,3072]{1,0:T(8,128)(2,1)} async-done(((bf16[32,3072]{1,0:T(8,128)(2,1)}), bf16[1024,3072]{1,0:T(8,128)(2,1)}) %all-gather.17.cloned.1.call-update) | async-done | bytes 6291472 | tf_op jit(solution)/shard_map/all_gather | solution.py:127
  123.6 8.9 all_gather.55
  132.5 20.1 %all-gather.29.cloned.1.call-done = bf16[2,1024,1024]{2,1,0:T(8,128)(2,1)} async-done(((bf16[2,128,1024]{2,1,0:T(8,128)(2,1)}), bf16[2,1024,1024]{2,1,0:T(8,128)(2,1)}) %all-gather.29.cloned.1.call-update) | async-done | bytes 4194320 | tf_op jit(solution)/shard_map/all_gather | solution.py:133
  154.8 28.3 %all-gather.19.cloned.1.call-done = bf16[1024,1024]{0,1:T(8,128)(2,1)} async-done(((bf16[128,1024]{0,1:T(8,128)(2,1)}), bf16[1024,1024]{0,1:T(8,128)(2,1)}) %all-gather.19.cloned.1.call-update) | async-done | bytes 2097168 | tf_op jit(solution)/shard_map/all_gather | solution.py:150
  192.2 21.6 %all-gather.21.cloned.1.call-done = bf16[1024,1024]{0,1:T(8,128)(2,1)} async-done(((bf16[128,1024]{0,1:T(8,128)(2,1)}), bf16[1024,1024]{0,1:T(8,128)(2,1)}) %all-gather.21.cloned.1.call-update) | async-done | bytes 2097168 | tf_op jit(solution)/shard_map/all_gather | solution.py:151
  220.1 74.5 %all-gather.25.cloned.1.call-done = bf16[1024,4096]{1,0:T(8,128)(2,1)} async-done(((bf16[32,4096]{1,0:T(8,128)(2,1)}), bf16[1024,4096]{1,0:T(8,128)(2,1)}) %all-gather.25.cloned.1.call-update) | async-done | bytes 8388624 | tf_op jit(solution)/shard_map/all_gather | solution.py:129
  294.6 79.4 %all-gather.27.cloned.1.call-done = bf16[4096,1024]{1,0:T(8,128)(2,1)} async-done(((bf16[128,1024]{1,0:T(8,128)(2,1)}), bf16[4096,1024]{1,0:T(8,128)(2,1)}) %all-gather.27.cloned.1.call-update) | async-done | bytes 8388624 | tf_op jit(solution)/shard_map/all_gather | solution.py:130
  374.0 10.9 %fusion.47 = f32[128,1024]{1,0:T(8,128)S(1)} fusion(bf16[4096,1024]{1,0:T(8,128)(2,1)} %all-gather.27.cloned.1.call-done, bf16[1024,4096]{1,0:T(8,128)(2,1)} %all-gather.25.cloned.1.call-done, f32[4096]{0:T(1024)S(1)} %slice-done.2, bf16[128,1024]{1,0:T(8,128)(2,1)S(1)} %copy-done.1, f32[1024]{0:T(1024)S(1)} %bitcast.184, f32[1024]{0:T(1024)S(1)} %bitcast.185, ...), kind=kOutput, calls=%fused_computation.76 | convolution fusion | flops 2182873088 | bytes 17589248 | tf_op jit(solution)/shard_map/dot_general | solution.py:182
  384.9 47.6 %all-gather.23.cloned.1.call-done = bf16[1024,1024]{1,0:T(8,128)(2,1)} async-done(((bf16[32,1024]{1,0:T(8,128)(2,1)}), bf16[1024,1024]{1,0:T(8,128)(2,1)}) %all-gather.23.cloned.1.call-update) | async-done | bytes 2097168 | tf_op jit(solution)/shard_map/all_gather | solution.py:128
  441.1 6.6 all-reduce
  447.7 10.1 all-gather.3
  459.1 42.5 %all-gather.31.cloned.1.call-done = bf16[3,512,1024]{2,1,0:T(8,128)(2,1)} async-done(((bf16[3,128,1024]{2,1,0:T(8,128)(2,1)}), bf16[3,512,1024]{2,1,0:T(8,128)(2,1)}) %all-gather.31.cloned.1.call-update) | async-done | bytes 3145744 | tf_op jit(solution)/shard_map/all_gather | solution.py:203
  501.6 49.4 %fusion.183 = (f32[3,512]{1,0:T(4,128)S(1)}, f32[3,512,12576]{1,2,0:T(8,128)}) fusion(bf16[3,512,1024]{2,1,0:T(8,128)(2,1)} %all-gather.31.cloned.1.call-done, bf16[12576,1024]{1,0:T(8,128)(2,1)} %param.31), kind=kOutput, calls=%fused_computation.264 | convolution fusion | flops 39579992064 | bytes 106174464 | tf_op jit(solution)/shard_map/while/body/eval_jaxpr/std,vd->stv/dot_general | solution.py:211
  550.9 17.5 %slice_bitcast_fusion.1 = f32[512,12576]{0,1:T(8,128)} fusion(f32[3,512,12576]{1,2,0:T(8,128)} %get-tuple-element.304), kind=kLoop, calls=%fused_computation.19 | loop fusion | bytes 51511296 | tf_op jit(solution)/shard_map/while/body/eval_jaxpr/sub | solution.py:214
  568.5 52.0 %fusion.175 = (f32[3,512]{1,0:T(4,128)S(1)}, f32[3,512,12576]{1,2,0:T(8,128)}) fusion(f32[3,512,12576]{1,2,0:T(8,128)} %get-tuple-element.304, f32[3,512]{1,0:T(4,128)S(1)} %get-tuple-element.303), kind=kLoop, calls=%fused_computation.256 | loop fusion | flops 38631936 | bytes 154546176 | tf_op jit(solution)/shard_map/while/body/eval_jaxpr/reduce_sum | solution.py:215
  620.5 17.6 %slice_bitcast_fusion.2 = f32[512,12576]{0,1:T(8,128)} fusion(f32[3,512,12576]{1,2,0:T(8,128)} %get-tuple-element.265), kind=kLoop, calls=%fused_computation.20 | loop fusion | bytes 51511296 | tf_op jit(solution)/shard_map/while/body/eval_jaxpr/mul | solution.py:214
  638.1 31.8 %fusion.6 = f32[2,512]{1,0:T(2,128)S(1)} fusion(f32[3,512,12576]{1,2,0:T(8,128)} %get-tuple-element.304, f32[512,12576]{0,1:T(8,128)} %slice_bitcast_fusion.1, f32[512,12576]{0,1:T(8,128)} %slice_bitcast_fusion.2), kind=kLoop, calls=%fused_computation.16 | loop fusion | flops 38632448 | bytes 103026688 | tf_op jit(solution)/shard_map/while/body/eval_jaxpr/reduce_sum | solution.py:214
  669.9 13.1 %all-gather.7 = f32[4,2,512]{2,1,0:T(2,128)S(1)} all-gather(f32[1,2,512]{2,1,0:T(2,128)S(1)} %bitcast.178), channel_id=4, replica_groups=mesh['seq'=8,'batch'=4] {'batch'}, dimensions={0}, use_global_device_ids=true | all-gather | bytes 20480 | tf_op jit(solution)/shard_map/all_gather | solution.py:21
  683.0 13.1 %all-gather.6 = f32[4,3,512]{2,1,0:T(4,128)S(1)} all-gather(f32[1,3,512]{2,1,0:T(4,128)S(1)} %bitcast.173), channel_id=3, replica_groups=mesh['seq'=8,'batch'=4] {'batch'}, dimensions={0}, use_global_device_ids=true | all-gather | bytes 30720 | tf_op jit(solution)/shard_map/all_gather | solution.py:21
  696.1 13.1 %all-gather.5 = f32[4,3,512]{2,1,0:T(4,128)S(1)} all-gather(f32[1,3,512]{2,1,0:T(4,128)S(1)} %bitcast.172), channel_id=2, replica_groups=mesh['seq'=8,'batch'=4] {'batch'}, dimensions={0}, use_global_device_ids=true | all-gather | bytes 30720 | tf_op jit(solution)/shard_map/all_gather | solution.py:21
  709.5 52.1 %subtract_exponential_fusion.1 = f32[3,512,12576]{1,2,0:T(8,128)} fusion(f32[3,512,12576]{1,2,0:T(8,128)} %get-tuple-element.304, f32[3,512]{1,0:T(4,128)S(1)} %log_add_fusion), kind=kLoop, calls=%fused_computation.9 | loop fusion | flops 19316736 | bytes 154540032 | tf_op jit(solution)/shard_map/while/body/eval_jaxpr/exp | solution.py:248
  761.7 17.6 %slice_bitcast_fusion = f32[512,12576]{0,1:T(8,128)} fusion(f32[3,512,12576]{1,2,0:T(8,128)} %subtract_exponential_fusion.1), kind=kLoop, calls=%fused_computation.18 | loop fusion | bytes 51511296 | tf_op jit(solution)/shard_map/while/body/eval_jaxpr/sub | solution.py:249
  780.7 38.9 %psum.36 = f32[]{:T(128)} all-reduce(f32[]{:T(128)} %get-tuple-element.232), channel_id=1, replica_groups=mesh['seq'=8,'batch'=4] {'seq','batch'}, use_global_device_ids=true, to_apply=%region_19.20 | all-reduce | flops 1 | bytes 8 | tf_op jit(solution)/shard_map/psum | solution.py:114
  820.3 42.1 %convert_bitcast_fusion.2 = bf16[512,2,1024]{2,0,1:T(8,128)(2,1)} fusion(bf16[12576,1024]{1,0:T(8,128)(2,1)} %param.31, f32[3,512,12576]{1,2,0:T(8,128)} %subtract_exponential_fusion.1, f32[512,12576]{0,1:T(8,128)} %slice_bitcast_fusion, f32[512]{0:T(512)S(1)} %divide_bitcast_fusion), kind=kOutput, calls=%fused_computation.46 | convolution fusion | flops 26413465600 | bytes 105121792 | tf_op jit(solution)/shard_map/while/body/eval_jaxpr/sbv,vd->bsd/dot_general | solution.py:250
  867.9 44.0 %reduce-scatter.13.cloned.1.call-done = bf16[128,2048]{1,0:T(8,128)(2,1)} async-done(((bf16[512,2048]{1,0:T(8,128)(2,1)}), bf16[128,2048]{1,0:T(8,128)(2,1)}) %reduce-scatter.13.cloned.1.call-update) | async-done | bytes 524304
  920.3 49.6 %reduce-scatter.11.cloned.1.call-done = bf16[2,128,1024]{2,1,0:T(8,128)(2,1)} async-done(((bf16[2,1024,1024]{2,1,0:T(8,128)(2,1)}), bf16[2,128,1024]{2,1,0:T(8,128)(2,1)}) %reduce-scatter.11.cloned.1.call-update) | async-done | bytes 524304 | tf_op jit(solution)/shard_map/reduce_scatter | solution.py:287
  970.0 37.4 %reduce-scatter.15.cloned.1.call-done = bf16[128,2]{1,0:T(8,128)(2,1)} async-done(((bf16[1024,2]{1,0:T(8,128)(2,1)}), bf16[128,2]{1,0:T(8,128)(2,1)}) %reduce-scatter.15.cloned.1.call-update) | async-done | bytes 528
  1008.2 11.7 %psum.41 = bf16[2,128]{1,0:T(2,128)(2,1)S(1)} all-reduce(bf16[2,128]{1,0:T(2,128)(2,1)S(1)} %copy.41), channel_id=1, replica_groups=mesh['seq'=8,'batch'=4] {'batch'}, use_global_device_ids=true, to_apply=%region_30.31 | all-reduce | flops 256 | bytes 1024 | tf_op jit(solution)/shard_map/psum | solution.py:284
  1023.7 37.2 %all-reduce.1 = (f32[]{:T(128)}, f32[]{:T(128)}) all-reduce(f32[]{:T(128)} %get-tuple-element.233, f32[]{:T(128)S(6)} %mul.538), channel_id=1, replica_groups=mesh['seq'=8,'batch'=4] {'seq','batch'}, use_global_device_ids=true, to_apply=%region_17.18 | all-reduce | flops 2 | bytes 16 | tf_op jit(solution)/shard_map/psum | solution.py:296
  (206 shorter events, 63.7 us)
Async XLA Ops:
  8.0 56.9 %reduce-scatter.9.cloned.1.call-start = ((), (), s32[]{:S(2)}) async-start(), calls=%async_computation.4 | async-start | bytes 1310720 | tf_op jit(solution)/shard_map/reduce_scatter | solution.py:120
  36.6 78.4 %slice-start.1 = ((f32[7168]{0:T(1024)}), f32[3072]{0:T(1024)S(1)}, s32[]{:S(2)}) async-start(f32[7168]{0:T(1024)} %param.30), calls=%async_computation.18 | async-start | bytes 24576 | tf_op jit(solution)/shard_map/slice | solution.py:144
  36.6 78.4 %all-gather.17.cloned.1.call-start = ((), (), s32[]{:S(2)}) async-start(), calls=%async_computation.5 | async-start | bytes 6488064 | tf_op jit(solution)/shard_map/all_gather | solution.py:127
  37.2 115.4 %all-gather.29.cloned.1.call-start = ((), (), s32[]{:S(2)}) async-start(), calls=%async_computation.11 | async-start | bytes 4718592 | tf_op jit(solution)/shard_map/all_gather | solution.py:133
  38.2 145.0 %all-gather.19.cloned.1.call-start = ((), (), s32[]{:S(2)}) async-start(), calls=%async_computation.6 | async-start | bytes 2359296 | tf_op jit(solution)/shard_map/all_gather | solution.py:150
  38.4 399.3 %copy-start.13 = (f32[1,1024]{1,0:T(1,128)}, f32[1,1024]{1,0:T(1,128)S(1)}, u32[]{:S(2)}) copy-start(f32[1,1024]{1,0:T(1,128)S(1)} %get-tuple-element.281) | copy-start | bytes 12292
  119.6 4.0 copy-start.32
  119.6 33.0 %copy-start.1 = (bf16[128,1024]{1,0:T(8,128)(2,1)S(1)}, bf16[128,1024]{1,0:T(8,128)(2,1)}, u32[]{:S(2)}) copy-start(bf16[128,1024]{1,0:T(8,128)(2,1)} %reduce-scatter.9.cloned.1.call-done) | copy-start | bytes 786436
  120.4 93.4 %all-gather.21.cloned.1.call-start = ((), (), s32[]{:S(2)}) async-start(), calls=%async_computation.7 | async-start | bytes 2359296 | tf_op jit(solution)/shard_map/all_gather | solution.py:151
  121.3 173.3 %all-gather.25.cloned.1.call-start = ((), (), s32[]{:S(2)}) async-start(), calls=%async_computation.9 | async-start | bytes 8650752 | tf_op jit(solution)/shard_map/all_gather | solution.py:129
  122.0 252.0 %all-gather.27.cloned.1.call-start = ((), (), s32[]{:S(2)}) async-start(), calls=%async_computation.10 | async-start | bytes 8650752 | tf_op jit(solution)/shard_map/all_gather | solution.py:130
  122.8 309.7 %all-gather.23.cloned.1.call-start = ((), (), s32[]{:S(2)}) async-start(), calls=%async_computation.8 | async-start | bytes 2162688 | tf_op jit(solution)/shard_map/all_gather | solution.py:128
  123.3 378.2 %all-gather.31.cloned.1.call-start = ((), (), s32[]{:S(2)}) async-start(), calls=%async_computation.12 | async-start | bytes 3932160 | tf_op jit(solution)/shard_map/all_gather | solution.py:203
  123.4 334.4 %copy-start.26 = (s32[128]{0:T(128)}, s32[128]{0:T(128)S(1)}, u32[]{:S(2)}) copy-start(s32[128]{0:T(128)S(1)} %iota_add_fusion) | copy-start | bytes 1540
  154.7 282.9 %copy-start.3 = (f32[128,1024]{1,0:T(8,128)}, f32[128,1024]{1,0:T(8,128)S(1)}, u32[]{:S(2)}) copy-start(f32[128,1024]{1,0:T(8,128)S(1)} %get-tuple-element.300) | copy-start | bytes 1572868
  213.8 160.2 %slice-start.2 = ((f32[7168]{0:T(1024)}), f32[4096]{0:T(1024)S(1)}, s32[]{:S(2)}) async-start(f32[7168]{0:T(1024)} %param.30), calls=%async_computation.19 | async-start | bytes 32768 | tf_op jit(solution)/shard_map/slice | solution.py:176
  437.7 10.0 copy-start.36
  439.0 472.8 %reduce-scatter.13.cloned.1.call-start = ((), (), s32[]{:S(2)}) async-start(), calls=%async_computation.15 | async-start | bytes 2621440
  709.5 52.1 %copy-start.15 = (f32[3,512]{1,0:T(4,128)}, f32[3,512]{1,0:T(4,128)S(1)}, u32[]{:S(2)}) copy-start(f32[3,512]{1,0:T(4,128)S(1)} %log_add_fusion) | copy-start | bytes 18436
  761.6 17.7 %slice-start = ((f32[3,512]{1,0:T(4,128)}), f32[1,512]{1,0:T(1,128)S(1)}, s32[]{:S(2)}) async-start(f32[3,512]{1,0:T(4,128)} %copy-done.15), calls=%async_computation.17 | async-start | bytes 4096 | tf_op jit(solution)/shard_map/slice | solution.py:237
  761.6 58.0 %copy-start.17 = (s32[4,1,128]{2,1,0:T(1,128)S(1)}, s32[4,1,128]{2,1,0:T(1,128)}, u32[]{:S(2)}) copy-start(s32[4,1,128]{2,1,0:T(1,128)} %copy-done.16) | copy-start | bytes 6148
  761.7 57.9 %copy-start.27 = (s32[128]{0:T(128)S(1)}, s32[128]{0:T(128)}, u32[]{:S(2)}) copy-start(s32[128]{0:T(128)} %copy-done.26) | copy-start | bytes 1540
  761.7 57.9 %copy-start.31 = (s32[4]{0:T(128)S(1)}, s32[4]{0:T(128)}, u32[]{:S(2)}) copy-start(s32[4]{0:T(128)} %copy-done.30) | copy-start | bytes 52
  867.8 102.1 %reduce-scatter.11.cloned.1.call-start = ((), (), s32[]{:S(2)}) async-start(), calls=%async_computation.13 | async-start | bytes 4718592 | tf_op jit(solution)/shard_map/reduce_scatter | solution.py:287
  919.2 142.4 %copy-start.33 = (f32[2,128]{1,0:T(2,128)S(1)}, f32[2,128]{1,0:T(2,128)}, u32[]{:S(2)}) copy-start(f32[2,128]{1,0:T(2,128)} %param.33) | copy-start | bytes 3076
  919.2 142.4 %copy-start.34 = (f32[2,128]{1,0:T(2,128)S(1)}, f32[2,128]{1,0:T(2,128)}, u32[]{:S(2)}) copy-start(f32[2,128]{1,0:T(2,128)} %param.37) | copy-start | bytes 3076
  919.2 142.4 %copy-start.35 = (f32[2,128]{1,0:T(2,128)S(1)}, f32[2,128]{1,0:T(2,128)}, u32[]{:S(2)}) copy-start(f32[2,128]{1,0:T(2,128)} %param.36) | copy-start | bytes 3076
  919.2 143.0 %copy-start.10 = (f32[2,128,1024]{2,1,0:T(8,128)S(1)}, f32[2,128,1024]{2,1,0:T(8,128)}, u32[]{:S(2)}) copy-start(f32[2,128,1024]{2,1,0:T(8,128)} %param.32) | copy-start | bytes 3145732
  919.2 143.0 %copy-start.11 = (f32[2,128,1024]{2,1,0:T(8,128)S(1)}, f32[2,128,1024]{2,1,0:T(8,128)}, u32[]{:S(2)}) copy-start(f32[2,128,1024]{2,1,0:T(8,128)} %param.35) | copy-start | bytes 3145732
  919.2 143.0 %copy-start.12 = (f32[2,128,1024]{2,1,0:T(8,128)S(1)}, f32[2,128,1024]{2,1,0:T(8,128)}, u32[]{:S(2)}) copy-start(f32[2,128,1024]{2,1,0:T(8,128)} %param.34) | copy-start | bytes 3145732
  919.3 88.1 %reduce-scatter.15.cloned.1.call-start = ((), (), s32[]{:S(2)}) async-start(), calls=%async_computation.16 | async-start | bytes 294912
  920.3 100.2 %all-reduce.4.cloned.1.call-start = ((), (), s32[]{:S(2)}) async-start(), calls=%async_computation.14 | async-start | bytes 1048576 | tf_op jit(solution)/shard_map/psum | solution.py:283
  (22 other events, 33.6 us)
Sparse Core Ops, SparseCore 0:
  36.7 28.1 reduce-scatter.8
  439.2 62.3 all-gather.30
  867.9 43.8 reduce-scatter.12
  970.1 38.2 all-reduce.3
Sparse Core Ops, SparseCore 1:
  40.4 74.6 all-gather.16
  117.5 35.0 all-gather.28
  155.1 28.0 all-gather.18
  185.8 28.0 all-gather.20
  217.2 77.3 all-gather.24
  298.0 76.0 all-gather.26
  377.2 55.2 all-gather.22
  919.4 50.5 reduce-scatter.10
  973.7 33.6 reduce-scatter.14
where the time goes:
time: 1080 us; the launch traced here: 1070 us
  waiting for transfers between devices  522 us (48%)
  blocking collectives  165 us (15%)
  other arithmetic  158 us (15%)
  matrix products  124 us (11%)
  local copies, waits for them, and re-layouts  83.7 us (8%)
  between operations  20.6 us (2%)
    unnamed x15, waiting for transfers between devices  84 us
    all_gather x1, waiting for transfers between devices, body(): lax.all_gather(w_proj, ('seq', 'batch'), axis=0, tiled=True)  79.4 us
    all_gather x1, waiting for transfers between devices, body(): lax.all_gather(w_fc, ('seq', 'batch'), axis=0, tiled=True)  74.5 us
    exp x1, other arithmetic, block_grads(): probs = jnp.exp(logits - totals_part[..., None])  52.1 us
    reduce_sum x1, other arithmetic, block_stats(): return (peak_rows, jnp.sum(exponent, axis=-1), crossing)  52 us
    reduce_scatter x1, waiting for transfers between devices, body(): lax.psum_scatter(grad_w.astype(jnp.bfloat16), 'seq', scatter_dimension=1,...  49.6 us
    dot_general x1, matrix products, block_stats(): jnp.einsum('std,vd->stv', portion, unembed, preferred_element_type=jnp.fl...  49.4 us
    all_gather x1, waiting for transfers between devices, body(): lax.all_gather(w_qkv, ('seq', 'batch'), axis=0, tiled=True)  47.8 us
  transfers between devices with their start and end apart: 13, of which 12 were waited for; matrix products, arithmetic and copies ran while one was open for 4% of the time, Pallas kernels for 0%

commit v1 on v0

--- a/solution.py
+++ b/solution.py
@@ -1,6 +1,10 @@
+import functools
+
 import jax
 import jax.numpy as jnp
 from jax import lax
+from jax.experimental import pallas as pl
+from jax.experimental.pallas import tpu as pltpu
 from jax.sharding import PartitionSpec as P
 
 HEAD_DIM = 64
@@ -8,6 +12,10 @@
 STEP = 10
 
 
+VOCAB_TILE = 1280
+LANES = 128
+NEGATIVE = -1e30
+VMEM_BYTES = 60 * 1024 * 1024
 norm_eps = 1e-05
 clip_max = 0.001
 beta_one = 0.9
@@ -74,6 +82,231 @@
         earlier / (1.0 - beta_one**STEP) / (jnp.sqrt(later / (1.0 - beta_two**STEP)) + adam_eps)
     )
     return (earlier, later, weight * (1.0 - learn_rate * decay_rate) - learn_rate * update)
+
+
+def forward_kernel(vocab, states_ref, table_ref, exps_ref, cols_ref, sums_ref, cross_ref, left, right, peak):
+    tile = pl.program_id(0)
+    rows = states_ref.shape[1]
+    width = table_ref.shape[0]
+    chunk = left.shape[0] // 3
+    group = 16
+    piece = 256
+    limit = vocab - tile * width
+    last = vocab - (pl.cdiv(vocab, width) - 1) * width
+    lane = lax.broadcasted_iota(jnp.int32, (group, LANES), 1)
+
+    @pl.when(tile == 0)
+    def _():
+        peak[...] = jnp.full_like(peak, NEGATIVE)
+        cols_ref[...] = jnp.zeros_like(cols_ref)
+        sums_ref[...] = jnp.zeros_like(sums_ref)
+        cross_ref[...] = jnp.zeros_like(cross_ref)
+
+    def multiply(index, target, start):
+        table = table_ref[start : start + piece, :]
+        for state in range(3):
+            target[state * chunk : (state + 1) * chunk, start : start + piece] = lax.dot_general(
+                states_ref[state, index * chunk : (index + 1) * chunk, :],
+                table,
+                (((1,), (1,)), ((), ())),
+                preferred_element_type=jnp.float32,
+            )
+
+    def reduce_rows(index, source, part):
+        begin = index * chunk + part * group
+        span = slice(begin, begin + group)
+
+        def logits(state, block):
+            value = source[
+                state * chunk + part * group : state * chunk + (part + 1) * group,
+                block * LANES : (block + 1) * LANES,
+            ]
+            if (block + 1) * LANES > last:
+                value = jnp.where(lane + block * LANES < limit, value, NEGATIVE)
+            return value
+
+        blocks = width // LANES
+        tops = []
+        totals = []
+        for state in range(3):
+            top = logits(state, 0)
+            for block in range(1, blocks):
+                top = jnp.maximum(top, logits(state, block))
+            before = peak[state, span, :]
+            now = jnp.maximum(before, jnp.max(top, axis=-1, keepdims=True))
+            peak[state, span, :] = now
+            cols_ref[state, span, :] = jnp.where(lane == tile, now, cols_ref[state, span, :])
+            fade = jnp.exp(before - now)
+            tops.append(now)
+            totals.append(sums_ref[state, span, :] * fade)
+            if state == 0:
+                crossing = [cross_ref[other, span, :] * fade for other in range(2)]
+        for block in range(blocks):
+            place = slice(block * LANES, (block + 1) * LANES)
+            base = logits(0, block)
+            base_exp = jnp.exp(base - tops[0])
+            totals[0] += base_exp
+            exps_ref[0, 0, span, place] = base_exp.astype(jnp.bfloat16)
+            for state in range(1, 3):
+                value = logits(state, block)
+                value_exp = jnp.exp(value - tops[state])
+                totals[state] += value_exp
+                exps_ref[0, state, span, place] = value_exp.astype(jnp.bfloat16)
+                crossing[state - 1] += base_exp * (base - value)
+        for state in range(3):
+            sums_ref[state, span, :] = totals[state]
+        for other in range(2):
+            cross_ref[other, span, :] = crossing[other]
+
+    count = rows // chunk
+    groups = chunk // group
+    pieces = width // piece
+    buffers = (left, right)
+    for index in range(count + 1):
+        done = 0
+        for step in range(pieces):
+            if index < count:
+                multiply(index, buffers[index % 2], step * piece)
+            if index > 0:
+                upto = (step + 1) * groups // pieces
+                for part in range(done, upto):
+                    reduce_rows(index - 1, buffers[(index - 1) % 2], part)
+                done = upto
+
+
+def vocab_forward(states, table):
+    _, rows, depth = states.shape
+    vocab = table.shape[0]
+    tiles = pl.cdiv(vocab, VOCAB_TILE)
+    chunk = 128
+    stat = lambda count: pl.BlockSpec((count, rows, LANES), lambda i: (0, 0, 0))
+    return pl.pallas_call(
+        functools.partial(forward_kernel, vocab),
+        grid=(tiles,),
+        in_specs=[
+            pl.BlockSpec((3, rows, depth), lambda i: (0, 0, 0)),
+            pl.BlockSpec((VOCAB_TILE, depth), lambda i: (i, 0)),
+        ],
+        out_specs=[
+            pl.BlockSpec((1, 3, rows, VOCAB_TILE), lambda i: (i, 0, 0, 0)),
+            stat(3),
+            stat(3),
+            stat(2),
+        ],
+        out_shape=[
+            jax.ShapeDtypeStruct((tiles, 3, rows, VOCAB_TILE), jnp.bfloat16),
+            jax.ShapeDtypeStruct((3, rows, LANES), jnp.float32),
+            jax.ShapeDtypeStruct((3, rows, LANES), jnp.float32),
+            jax.ShapeDtypeStruct((2, rows, LANES), jnp.float32),
+        ],
+        scratch_shapes=[
+            pltpu.VMEM((3 * chunk, VOCAB_TILE), jnp.float32),
+            pltpu.VMEM((3 * chunk, VOCAB_TILE), jnp.float32),
+            pltpu.VMEM((3, rows, LANES), jnp.float32),
+        ],
+        compiler_params=pltpu.CompilerParams(vmem_limit_bytes=VMEM_BYTES),
+        cost_estimate=pl.CostEstimate(
+            flops=6 * rows * depth * vocab,
+            bytes_accessed=2 * vocab * (depth + 3 * rows),
+            transcendentals=3 * rows * vocab,
+        ),
+        name="vocab_forward",
+    )(states, table)
+
+
+def backward_kernel(vocab, exps_ref, scales_ref, table_ref, out_ref, left, right, tail):
+    tile = pl.program_id(0)
+    rows = exps_ref.shape[2]
+    width, depth = table_ref.shape
+    chunk = left.shape[0] // 2
+    group = 16
+    piece = 256
+    limit = vocab - tile * width
+    last = vocab - (pl.cdiv(vocab, width) - 1) * width
+    whole = last // piece * piece
+    lane = lax.broadcasted_iota(jnp.int32, (group, LANES), 1)
+
+    @pl.when(tile == 0)
+    def _():
+        out_ref[...] = jnp.zeros_like(out_ref)
+
+    below = lax.broadcasted_iota(jnp.int32, (width - whole, depth), 0) + whole < limit
+    tail[...] = jnp.where(below, table_ref[whole:, :], jnp.zeros((), tail.dtype))
+
+    def differences(index, target, part):
+        begin = index * chunk + part * group
+        span = slice(begin, begin + group)
+        factors = [
+            jnp.sum(jnp.where(lane == tile, scales_ref[state, span, :], 0.0), axis=-1, keepdims=True)
+            for state in range(3)
+        ]
+        factors = [jnp.broadcast_to(factor, (group, LANES)) for factor in factors]
+        for block in range(width // LANES):
+            place = slice(block * LANES, (block + 1) * LANES)
+            base = exps_ref[0, 0, span, place].astype(jnp.float32) * factors[0]
+            for state in range(1, 3):
+                value = exps_ref[0, state, span, place].astype(jnp.float32) * factors[state]
+                target[
+                    (state - 1) * chunk + part * group : (state - 1) * chunk + (part + 1) * group, place
+                ] = (value - base).astype(jnp.bfloat16)
+
+    def multiply(index, source, start):
+        place = slice(start, start + piece)
+        span = slice(index * chunk, (index + 1) * chunk)
+        part = jnp.dot(
+            source[:, whole:], tail[:, place], preferred_element_type=jnp.float32
+        )
+        if whole > 0:
+            part += jnp.dot(
+                source[:, :whole], table_ref[:whole, place], preferred_element_type=jnp.float32
+            )
+        for probe in range(2):
+            out_ref[probe, span, place] += part[probe * chunk : (probe + 1) * chunk]
+
+    count = rows // chunk
+    groups = chunk // group
+    pieces = depth // piece
+    buffers = (left, right)
+    for index in range(count + 1):
+        done = 0
+        for step in range(pieces):
+            if index > 0:
+                multiply(index - 1, buffers[(index - 1) % 2], step * piece)
+            if index < count:
+                upto = (step + 1) * groups // pieces
+                for part in range(done, upto):
+                    differences(index, buffers[index % 2], part)
+                done = upto
+
+
+def vocab_backward(exps, scales, table):
+    tiles, _, rows, _ = exps.shape
+    vocab, depth = table.shape
+    chunk = 256
+    last = vocab - (tiles - 1) * VOCAB_TILE
+    return pl.pallas_call(
+        functools.partial(backward_kernel, vocab),
+        grid=(tiles,),
+        in_specs=[
+            pl.BlockSpec((1, 3, rows, VOCAB_TILE), lambda i: (i, 0, 0, 0)),
+            pl.BlockSpec((3, rows, LANES), lambda i: (0, 0, 0)),
+            pl.BlockSpec((VOCAB_TILE, depth), lambda i: (i, 0)),
+        ],
+        out_specs=pl.BlockSpec((2, rows, depth), lambda i: (0, 0, 0)),
+        out_shape=jax.ShapeDtypeStruct((2, rows, depth), jnp.float32),
+        scratch_shapes=[
+            pltpu.VMEM((2 * chunk, VOCAB_TILE), jnp.bfloat16),
+            pltpu.VMEM((2 * chunk, VOCAB_TILE), jnp.bfloat16),
+            pltpu.VMEM((VOCAB_TILE - last // 256 * 256, depth), jnp.bfloat16),
+        ],
+        compiler_params=pltpu.CompilerParams(vmem_limit_bytes=VMEM_BYTES),
+        cost_estimate=pl.CostEstimate(
+            flops=4 * rows * depth * vocab,
+            bytes_accessed=2 * vocab * (depth + 3 * rows),
+            transcendentals=0,
+        ),
+        name="vocab_backward",
+    )(exps, scales, table)
 
 
 def body(
@@ -203,22 +436,11 @@
     gathered = lax.all_gather(states, "batch", axis=1, tiled=True)
     all_rows = gathered.shape[1]
 
-    def block_size():
-        return 512
-
-    def block_stats(offset):
-        portion = lax.dynamic_slice_in_dim(gathered, offset, block_size(), 1)
-        logits = jnp.einsum("std,vd->stv", portion, unembed, preferred_element_type=jnp.float32)
-        peak_rows = jnp.max(logits, axis=-1)
-        exponent = jnp.exp(logits - peak_rows[..., None])
-        crossing = jnp.sum(exponent[0][None] * (logits[0][None] - logits[1:]), axis=-1)
-        return (peak_rows, jnp.sum(exponent, axis=-1), crossing)
-
-    stat_offsets = jnp.arange(all_rows // block_size(), dtype=jnp.int32) * block_size()
-    peak_all, sums_all, cross_all = lax.map(block_stats, stat_offsets)
-    peak_all = jnp.transpose(peak_all, (1, 0, 2)).reshape(3, all_rows)
-    sums_all = jnp.transpose(sums_all, (1, 0, 2)).reshape(3, all_rows)
-    cross_all = jnp.transpose(cross_all, (1, 0, 2)).reshape(2, all_rows)
+    exps, peak_cols, sums_lane, cross_lane = vocab_forward(gathered, unembed)
+    tiles = exps.shape[0]
+    peak_all = peak_cols[:, :, tiles - 1]
+    sums_all = jnp.sum(sums_lane, axis=-1)
+    cross_all = jnp.sum(cross_lane, axis=-1)
 
     def combine(earlier, later):
         peak_a, sums_a, cross_a = earlier
@@ -238,25 +460,11 @@
     diverge_own = lax.dynamic_slice_in_dim(diverge, batch_index * tok_rows, tok_rows, 1)
     loss_local = jnp.sum(weight_own * (diverge_own[0] + diverge_own[1]))
     token_coef = weight_all.reshape(-1) / token_count
-    size = block_size()
-
-    def block_grads(inner):
-        portion = lax.dynamic_slice_in_dim(gathered, inner, size, 1)
-        totals_part = lax.dynamic_slice_in_dim(log_totals, inner, size, 1)
-        coef_part = lax.dynamic_slice_in_dim(token_coef, inner, size, 0)
-        logits = jnp.einsum("std,vd->stv", portion, unembed, preferred_element_type=jnp.float32)
-        probs = jnp.exp(logits - totals_part[..., None])
-        dlogits = (coef_part[None, :, None] * (probs[1:] - probs[0][None])).astype(jnp.bfloat16)
-        return jnp.einsum(
-            "sbv,vd->bsd", dlogits, unembed, preferred_element_type=jnp.float32
-        ).reshape(size, 2 * width)
-
-    inner_offsets = jnp.arange(tok_rows * lax.axis_size("batch") // size, dtype=jnp.int32) * size
+    scales = token_coef[None, :, None] * jnp.exp(peak_cols - log_totals[:, :, None])
+    partial = vocab_backward(exps, scales, unembed)
     dstates = (
         lax.psum_scatter(
-            lax.map(block_grads, inner_offsets)
-            .reshape(tok_rows * lax.axis_size("batch"), 2 * width)
-            .astype(jnp.bfloat16),
+            jnp.transpose(partial, (1, 0, 2)).reshape(all_rows, 2 * width).astype(jnp.bfloat16),
             "batch",
             scatter_dimension=0,
             tiled=True,

time: 1080 us -> 972 us (0.900)
  Pallas kernels: 0 us -> 163 us
  other arithmetic: 158 us -> 26.4 us
  matrix products: 124 us -> 32.4 us
  local copies, waits for them, and re-layouts: 83.7 us -> 32.7 us
    pallas_call x0 -> x2, Pallas kernels: none -> 163 us  [the longest x1 121 us: vocab_forward(): pl.pallas_call(functools.partial(forward_kernel, vocab), grid=(tiles,), i...]
    dot_general x2 -> x0, matrix products: 91.5 us -> none  [the longest x1 49.4 us: block_stats(): jnp.einsum('std,vd->stv', portion, unembed, preferred_element_type=jnp.fl...]
    reduce_sum x2, other arithmetic: 83.8 us -> 1.63 us  [the longest x1 1.41 us: body(): sums_all = jnp.sum(sums_lane, axis=-1)]
    exp x1 -> x0, other arithmetic: 52.1 us -> none  [block_grads(): probs = jnp.exp(logits - totals_part[..., None])]
    sub x2 -> x0, local copies, waits for them, and re-layouts: 35.1 us -> none  [the longest x1 17.6 us: block_grads(): probs[1:] - probs[0][None]]
    mul x1 -> x0, local copies, waits for them, and re-layouts: 17.6 us -> none  [block_stats(): exponent[0][None] * (logits[0][None] - logits[1:])]
where the time goes in v1:
time: 972 us; the launch traced here: 964 us
  waiting for transfers between devices  523 us (54%)
  blocking collectives  165 us (17%)
  Pallas kernels  163 us (17%)
  local copies, waits for them, and re-layouts  32.7 us (3%)
  matrix products  32.4 us (3%)
  other arithmetic  26.4 us (3%)
  between operations  20.4 us (2%)
    pallas_call x1, Pallas kernels, vocab_forward(): pl.pallas_call(functools.partial(forward_kernel, vocab), grid=(tiles,), i...  121 us
    unnamed x15, waiting for transfers between devices  83.9 us
    all_gather x1, waiting for transfers between devices, body(): lax.all_gather(w_proj, ('seq', 'batch'), axis=0, tiled=True)  79.4 us
    all_gather x1, waiting for transfers between devices, body(): lax.all_gather(w_fc, ('seq', 'batch'), axis=0, tiled=True)  74.5 us
    reduce_scatter x1, waiting for transfers between devices, body(): lax.psum_scatter(grad_w.astype(jnp.bfloat16), 'seq', scatter_dimension=1,...  49.6 us
    all_gather x1, waiting for transfers between devices, body(): lax.all_gather(w_qkv, ('seq', 'batch'), axis=0, tiled=True)  47.8 us
    all_gather x1, waiting for transfers between devices, body(): lax.all_gather(w_out, ('seq', 'batch'), axis=0, tiled=True)  47.6 us
    all_gather x1, waiting for transfers between devices, body(): gathered = lax.all_gather(states, 'batch', axis=1, tiled=True)  43.7 us
  transfers between devices with their start and end apart: 13, of which 12 were waited for; matrix products, arithmetic and copies ran while one was open for 4% of the time, Pallas kernels for 0%

profile of v1, /device:TPU:0, one launch (start us, length us, event | category | flops | bytes accessed | tf_op | source)
XLA Modules:
  0.0 964.0 jit_solution(17215587333985583126)
XLA Ops:
  8.1 12.7 %all-gather.4 = s32[4,1,128]{2,1,0:T(1,128)S(1)} all-gather(s32[1,1,128]{2,1,0:T(1,128)} %bitcast.174), channel_id=1, replica_groups=mesh['seq'=8,'batch'=4] {'batch'}, dimensions={0}, use_global_device_ids=true | all-gather | bytes 2560 | tf_op jit(solution)/shard_map/all_gather | solution.py:339
  20.8 14.4 %gather_fusion = bf16[512,1024]{1,0:T(8,128)(2,1)S(1)} fusion(bf16[12576,1024]{1,0:T(8,128)(2,1)} %param.23, s32[1024]{0:T(1024)S(1)} %pad_clamp_fusion), kind=kCustom, calls=%fused_computation | custom fusion | bytes 2099200 | tf_op jit(solution)/shard_map/jit(_take)/gather | solution.py:352
  38.4 26.5 %reduce-scatter.9.cloned.1.call-done = bf16[128,1024]{1,0:T(8,128)(2,1)} async-done(((bf16[512,1024]{1,0:T(8,128)(2,1)}), bf16[128,1024]{1,0:T(8,128)(2,1)}) %reduce-scatter.9.cloned.1.call-update) | async-done | bytes 262160 | tf_op jit(solution)/shard_map/reduce_scatter | solution.py:353
  67.1 47.8 %all-gather.16.cloned.1.call-done = bf16[1024,3072]{1,0:T(8,128)(2,1)} async-done(((bf16[32,3072]{1,0:T(8,128)(2,1)}), bf16[1024,3072]{1,0:T(8,128)(2,1)}) %all-gather.16.cloned.1.call-update) | async-done | bytes 6291472 | tf_op jit(solution)/shard_map/all_gather | solution.py:360
  115.0 4.0 convolution_add_fusion.1
  123.5 8.9 all_gather.61
  132.4 20.1 %all-gather.28.cloned.1.call-done = bf16[2,1024,1024]{2,1,0:T(8,128)(2,1)} async-done(((bf16[2,128,1024]{2,1,0:T(8,128)(2,1)}), bf16[2,1024,1024]{2,1,0:T(8,128)(2,1)}) %all-gather.28.cloned.1.call-update) | async-done | bytes 4194320 | tf_op jit(solution)/shard_map/all_gather | solution.py:366
  154.7 28.4 %all-gather.18.cloned.1.call-done = bf16[1024,1024]{0,1:T(8,128)(2,1)} async-done(((bf16[128,1024]{0,1:T(8,128)(2,1)}), bf16[1024,1024]{0,1:T(8,128)(2,1)}) %all-gather.18.cloned.1.call-update) | async-done | bytes 2097168 | tf_op jit(solution)/shard_map/all_gather | solution.py:383
  183.1 3.2 fusion.3
  186.3 3.2 copy-done
  192.1 21.7 %all-gather.20.cloned.1.call-done = bf16[1024,1024]{0,1:T(8,128)(2,1)} async-done(((bf16[128,1024]{0,1:T(8,128)(2,1)}), bf16[1024,1024]{0,1:T(8,128)(2,1)}) %all-gather.20.cloned.1.call-update) | async-done | bytes 2097168 | tf_op jit(solution)/shard_map/all_gather | solution.py:384
  213.8 6.3 fusion.71
  220.0 74.5 %all-gather.24.cloned.1.call-done = bf16[1024,4096]{1,0:T(8,128)(2,1)} async-done(((bf16[32,4096]{1,0:T(8,128)(2,1)}), bf16[1024,4096]{1,0:T(8,128)(2,1)}) %all-gather.24.cloned.1.call-update) | async-done | bytes 8388624 | tf_op jit(solution)/shard_map/all_gather | solution.py:362
  294.5 79.4 %all-gather.26.cloned.1.call-done = bf16[4096,1024]{1,0:T(8,128)(2,1)} async-done(((bf16[128,1024]{1,0:T(8,128)(2,1)}), bf16[4096,1024]{1,0:T(8,128)(2,1)}) %all-gather.26.cloned.1.call-update) | async-done | bytes 8388624 | tf_op jit(solution)/shard_map/all_gather | solution.py:363
  373.9 10.9 %fusion.32 = f32[128,1024]{1,0:T(8,128)S(1)} fusion(bf16[4096,1024]{1,0:T(8,128)(2,1)} %all-gather.26.cloned.1.call-done, bf16[1024,4096]{1,0:T(8,128)(2,1)} %all-gather.24.cloned.1.call-done, f32[4096]{0:T(1024)S(1)} %slice-done.1, bf16[128,1024]{1,0:T(8,128)(2,1)S(1)} %copy-done.1, f32[1024]{0:T(1024)S(1)} %bitcast.167, f32[1024]{0:T(1024)S(1)} %bitcast.168, ...), kind=kOutput, calls=%fused_computation.59 | convolution fusion | flops 2182873088 | bytes 17589248 | tf_op jit(solution)/shard_map/dot_general | solution.py:415
  384.8 47.6 %all-gather.22.cloned.1.call-done = bf16[1024,1024]{1,0:T(8,128)(2,1)} async-done(((bf16[32,1024]{1,0:T(8,128)(2,1)}), bf16[1024,1024]{1,0:T(8,128)(2,1)}) %all-gather.22.cloned.1.call-update) | async-done | bytes 2097168 | tf_op jit(solution)/shard_map/all_gather | solution.py:361
  441.0 6.6 all-reduce
  447.6 10.1 %all-gather.3 = s32[4,1,128]{2,1,0:T(1,128)S(1)} all-gather(s32[1,1,128]{2,1,0:T(1,128)S(1)} %bitcast.175), channel_id=1, replica_groups=mesh['seq'=8,'batch'=4] {'batch'}, dimensions={0}, use_global_device_ids=true | all-gather | bytes 2560 | tf_op jit(solution)/shard_map/all_gather | solution.py:340
  457.8 43.7 %all-gather.30.cloned.1.call-done.states_ref = bf16[3,512,1024]{2,1,0:T(8,128)(2,1)} async-done(((bf16[3,128,1024]{2,1,0:T(8,128)(2,1)}), bf16[3,512,1024]{2,1,0:T(8,128)(2,1)}) %all-gather.30.cloned.1.call-update) | async-done | bytes 3145744 | tf_op jit(solution)/shard_map/all_gather | solution.py:436
  501.4 121.2 %vocab_forward.1 = (bf16[10,3,512,1280]{3,2,1,0:T(8,128)(2,1)}, f32[3,512,128]{2,1,0:T(8,128)}, f32[3,512,128]{2,1,0:T(8,128)}, f32[2,512,128]{2,1,0:T(8,128)}) custom-call(bf16[3,512,1024]{2,1,0:T(8,128)(2,1)} %all-gather.30.cloned.1.call-done.states_ref, bf16[12576,1024]{1,0:T(8,128)(2,1)} %table_ref.3), custom_call_target="tpu_custom_call" | custom-call | flops 39560675328 | bytes 64389120 | tf_op jit(solution)/shard_map/vocab_forward/pallas_call | solution.py:183
  624.4 13.1 %all-gather = f32[12,512,1]{1,2,0:T(1,128)S(1)} all-gather(f32[3,512,1]{1,2,0:T(1,128)S(1)} %copy.35), channel_id=2, replica_groups=mesh['seq'=8,'batch'=4] {'batch'}, dimensions={0}, use_global_device_ids=true | all-gather | bytes 30720 | tf_op jit(solution)/shard_map/all_gather | solution.py:29
  639.1 13.1 %all-gather.5 = f32[4,3,512]{2,1,0:T(4,128)S(1)} all-gather(f32[1,3,512]{2,1,0:T(4,128)S(1)} %bitcast.156), channel_id=3, replica_groups=mesh['seq'=8,'batch'=4] {'batch'}, dimensions={0}, use_global_device_ids=true | all-gather | bytes 30720 | tf_op jit(solution)/shard_map/all_gather | solution.py:29
  652.4 13.1 %all-gather.6 = f32[4,2,512]{2,1,0:T(2,128)S(1)} all-gather(f32[1,2,512]{2,1,0:T(2,128)S(1)} %bitcast.161), channel_id=4, replica_groups=mesh['seq'=8,'batch'=4] {'batch'}, dimensions={0}, use_global_device_ids=true | all-gather | bytes 20480 | tf_op jit(solution)/shard_map/all_gather | solution.py:29
  666.6 38.9 %psum.36 = f32[]{:T(128)} all-reduce(f32[]{:T(128)} %get-tuple-element.204), channel_id=1, replica_groups=mesh['seq'=8,'batch'=4] {'seq','batch'}, use_global_device_ids=true, to_apply=%region_18.19 | all-reduce | flops 1 | bytes 8 | tf_op jit(solution)/shard_map/psum | solution.py:347
  707.5 41.7 %vocab_backward.1 = f32[2,512,1024]{2,1,0:T(8,128)} custom-call(bf16[10,3,512,1280]{3,2,1,0:T(8,128)(2,1)} %get-tuple-element.197.exps_ref, f32[3,512,128]{2,1,0:T(8,128)} %exponential_multiply_fusion.scales_ref, bf16[12576,1024]{1,0:T(8,128)(2,1)} %table_ref.3), custom_call_target="tpu_custom_call" | custom-call | flops 26373783552 | bytes 64389120 | tf_op jit(solution)/shard_map/vocab_backward/pallas_call | solution.py:287
  754.3 4.0 copy.39
  758.3 43.9 %reduce-scatter.13.cloned.1.call-done = bf16[128,2048]{1,0:T(8,128)(2,1)} async-done(((bf16[512,2048]{1,0:T(8,128)(2,1)}), bf16[128,2048]{1,0:T(8,128)(2,1)}) %reduce-scatter.13.cloned.1.call-update) | async-done | bytes 524304
  810.0 49.6 %reduce-scatter.11.cloned.1.call-done = bf16[2,128,1024]{2,1,0:T(8,128)(2,1)} async-done(((bf16[2,1024,1024]{2,1,0:T(8,128)(2,1)}), bf16[2,128,1024]{2,1,0:T(8,128)(2,1)}) %reduce-scatter.11.cloned.1.call-update) | async-done | bytes 524304 | tf_op jit(solution)/shard_map/reduce_scatter | solution.py:495
  859.6 37.4 %reduce-scatter.15.cloned.1.call-done = bf16[128,2]{1,0:T(8,128)(2,1)} async-done(((bf16[1024,2]{1,0:T(8,128)(2,1)}), bf16[128,2]{1,0:T(8,128)(2,1)}) %reduce-scatter.15.cloned.1.call-update) | async-done | bytes 528
  897.8 11.7 %psum.41 = bf16[2,128]{1,0:T(2,128)(2,1)S(1)} all-reduce(bf16[2,128]{1,0:T(2,128)(2,1)S(1)} %copy.42), channel_id=1, replica_groups=mesh['seq'=8,'batch'=4] {'batch'}, use_global_device_ids=true, to_apply=%region_29.30 | all-reduce | flops 256 | bytes 1024 | tf_op jit(solution)/shard_map/psum | solution.py:492
  913.4 37.1 %all-reduce.1 = (f32[]{:T(128)}, f32[]{:T(128)}) all-reduce(f32[]{:T(128)} %get-tuple-element.205, f32[]{:T(128)S(6)} %mul.517), channel_id=1, replica_groups=mesh['seq'=8,'batch'=4] {'seq','batch'}, use_global_device_ids=true, to_apply=%region_16.17 | all-reduce | flops 2 | bytes 16 | tf_op jit(solution)/shard_map/psum | solution.py:504
  951.9 3.2 multiply_subtract_fusion
  (166 shorter events, 45.8 us)
Async XLA Ops:
  8.0 56.9 %reduce-scatter.9.cloned.1.call-start = ((), (), s32[]{:S(2)}) async-start(), calls=%async_computation.4 | async-start | bytes 1310720 | tf_op jit(solution)/shard_map/reduce_scatter | solution.py:353
  35.2 2.0 copy-start.4
  36.5 1.8 copy-start.11
  36.6 1.8 copy-start.10
  36.6 78.4 %slice-start = ((f32[7168]{0:T(1024)}), f32[3072]{0:T(1024)S(1)}, s32[]{:S(2)}) async-start(f32[7168]{0:T(1024)} %param.30), calls=%async_computation.17 | async-start | bytes 24576 | tf_op jit(solution)/shard_map/slice | solution.py:377
  36.6 78.4 %all-gather.16.cloned.1.call-start = ((), (), s32[]{:S(2)}) async-start(), calls=%async_computation.5 | async-start | bytes 6488064 | tf_op jit(solution)/shard_map/all_gather | solution.py:360
  37.2 115.4 %all-gather.28.cloned.1.call-start = ((), (), s32[]{:S(2)}) async-start(), calls=%async_computation.11 | async-start | bytes 4718592 | tf_op jit(solution)/shard_map/all_gather | solution.py:366
  38.1 145.0 %all-gather.18.cloned.1.call-start = ((), (), s32[]{:S(2)}) async-start(), calls=%async_computation.6 | async-start | bytes 2359296 | tf_op jit(solution)/shard_map/all_gather | solution.py:383
  119.5 4.0 copy-start.12
  119.5 33.0 %copy-start.1 = (bf16[128,1024]{1,0:T(8,128)(2,1)S(1)}, bf16[128,1024]{1,0:T(8,128)(2,1)}, u32[]{:S(2)}) copy-start(bf16[128,1024]{1,0:T(8,128)(2,1)} %reduce-scatter.9.cloned.1.call-done) | copy-start | bytes 786436
  120.4 93.4 %all-gather.20.cloned.1.call-start = ((), (), s32[]{:S(2)}) async-start(), calls=%async_computation.7 | async-start | bytes 2359296 | tf_op jit(solution)/shard_map/all_gather | solution.py:384
  121.2 173.3 %all-gather.24.cloned.1.call-start = ((), (), s32[]{:S(2)}) async-start(), calls=%async_computation.9 | async-start | bytes 8650752 | tf_op jit(solution)/shard_map/all_gather | solution.py:362
  122.0 252.0 %all-gather.26.cloned.1.call-start = ((), (), s32[]{:S(2)}) async-start(), calls=%async_computation.10 | async-start | bytes 8650752 | tf_op jit(solution)/shard_map/all_gather | solution.py:363
  122.7 309.7 %all-gather.22.cloned.1.call-start = ((), (), s32[]{:S(2)}) async-start(), calls=%async_computation.8 | async-start | bytes 2162688 | tf_op jit(solution)/shard_map/all_gather | solution.py:361
  123.3 378.1 %all-gather.30.cloned.1.call-start = ((), (), s32[]{:S(2)}) async-start(), calls=%async_computation.12 | async-start | bytes 3932160 | tf_op jit(solution)/shard_map/all_gather | solution.py:436
  186.3 3.2 copy-start
  213.8 160.2 %slice-start.1 = ((f32[7168]{0:T(1024)}), f32[4096]{0:T(1024)S(1)}, s32[]{:S(2)}) async-start(f32[7168]{0:T(1024)} %param.30), calls=%async_computation.18 | async-start | bytes 32768 | tf_op jit(solution)/shard_map/slice | solution.py:409
  434.6 3.0 copy-start.2
  437.6 2.1 copy-start.16
  437.6 10.0 %copy-start.15 = (s32[1,128]{1,0:T(1,128)S(1)}, s32[1,128]{1,0:T(1,128)}, u32[]{:S(2)}) copy-start(s32[1,128]{1,0:T(1,128)} %param.21) | copy-start | bytes 1540
  438.9 363.4 %reduce-scatter.13.cloned.1.call-start = ((), (), s32[]{:S(2)}) async-start(), calls=%async_computation.15 | async-start | bytes 2621440
  622.6 29.5 %copy-start.9 = (f32[2,512,128]{2,1,0:T(8,128)S(1)}, f32[2,512,128]{2,1,0:T(8,128)}, u32[]{:S(2)}) copy-start(f32[2,512,128]{2,1,0:T(8,128)} %get-tuple-element.193) | copy-start | bytes 1572868
  622.6 83.6 %copy-start.6 = (f32[3,512,128]{2,1,0:T(8,128)S(1)}, f32[3,512,128]{2,1,0:T(8,128)}, u32[]{:S(2)}) copy-start(f32[3,512,128]{2,1,0:T(8,128)} %get-tuple-element.191) | copy-start | bytes 2359300
  758.3 101.3 %reduce-scatter.11.cloned.1.call-start = ((), (), s32[]{:S(2)}) async-start(), calls=%async_computation.13 | async-start | bytes 4718592 | tf_op jit(solution)/shard_map/reduce_scatter | solution.py:495
  804.1 1.0 copy-start.3
  808.9 142.4 %copy-start.13 = (f32[2,128]{1,0:T(2,128)S(1)}, f32[2,128]{1,0:T(2,128)}, u32[]{:S(2)}) copy-start(f32[2,128]{1,0:T(2,128)} %param.37) | copy-start | bytes 3076
  808.9 142.4 %copy-start.14 = (f32[2,128]{1,0:T(2,128)S(1)}, f32[2,128]{1,0:T(2,128)}, u32[]{:S(2)}) copy-start(f32[2,128]{1,0:T(2,128)} %param.36) | copy-start | bytes 3076
  808.9 143.0 %copy-start.5 = (f32[2,128,1024]{2,1,0:T(8,128)S(1)}, f32[2,128,1024]{2,1,0:T(8,128)}, u32[]{:S(2)}) copy-start(f32[2,128,1024]{2,1,0:T(8,128)} %param.32) | copy-start | bytes 3145732
  808.9 143.0 %copy-start.7 = (f32[2,128,1024]{2,1,0:T(8,128)S(1)}, f32[2,128,1024]{2,1,0:T(8,128)}, u32[]{:S(2)}) copy-start(f32[2,128,1024]{2,1,0:T(8,128)} %param.35) | copy-start | bytes 3145732
  808.9 143.0 %copy-start.8 = (f32[2,128,1024]{2,1,0:T(8,128)S(1)}, f32[2,128,1024]{2,1,0:T(8,128)}, u32[]{:S(2)}) copy-start(f32[2,128,1024]{2,1,0:T(8,128)} %param.34) | copy-start | bytes 3145732
  809.0 88.1 %reduce-scatter.15.cloned.1.call-start = ((), (), s32[]{:S(2)}) async-start(), calls=%async_computation.16 | async-start | bytes 294912
  810.0 100.2 %all-reduce.4.cloned.1.call-start = ((), (), s32[]{:S(2)}) async-start(), calls=%async_computation.14 | async-start | bytes 1048576 | tf_op jit(solution)/shard_map/psum | solution.py:491
Sparse Core Ops, SparseCore 0:
  36.7 28.1 reduce-scatter.8
  439.0 62.3 all-gather.29
  758.4 43.8 reduce-scatter.12
  859.7 38.2 all-reduce.3
Sparse Core Ops, SparseCore 1:
  40.4 74.5 all-gather.15
  117.5 35.0 all-gather.27
  155.0 28.0 all-gather.17
  185.7 28.0 all-gather.19
  217.2 77.3 all-gather.23
  297.9 76.0 all-gather.25
  377.2 55.2 all-gather.21
  809.0 50.5 reduce-scatter.10
  863.3 33.6 reduce-scatter.14

commit v2 on v0

--- a/solution.py
+++ b/solution.py
@@ -1,6 +1,10 @@
+import functools
+
 import jax
 import jax.numpy as jnp
 from jax import lax
+from jax.experimental import pallas as pl
+from jax.experimental.pallas import tpu as pltpu
 from jax.sharding import PartitionSpec as P
 
 HEAD_DIM = 64
@@ -8,6 +12,10 @@
 STEP = 10
 
 
+VOCAB_TILE = 1280
+LANES = 128
+NEGATIVE = -1e30
+VMEM_BYTES = 60 * 1024 * 1024
 norm_eps = 1e-05
 clip_max = 0.001
 beta_one = 0.9
@@ -74,6 +82,273 @@
         earlier / (1.0 - beta_one**STEP) / (jnp.sqrt(later / (1.0 - beta_two**STEP)) + adam_eps)
     )
     return (earlier, later, weight * (1.0 - learn_rate * decay_rate) - learn_rate * update)
+
+
+def forward_kernel(vocab, states_ref, table_ref, first_ref, second_ref, peaks_ref, sums_ref, cross_ref, turned, left, right, peak):
+    step = pl.program_id(0)
+    steps = pl.num_programs(0) - 1
+    width = table_ref.shape[0]
+    half = left.shape[1] // 3
+    group = 16
+    last = vocab - (pl.cdiv(vocab, width) - 1) * width
+    row = lax.broadcasted_iota(jnp.int32, (group, LANES), 0)
+
+    def reset(part):
+        span = slice(part * half, (part + 1) * half)
+        peak[:, span] = jnp.full((8, half), NEGATIVE, jnp.float32)
+        sums_ref[:, :, span] = jnp.zeros((3, 8, half), jnp.float32)
+        cross_ref[:, :, span] = jnp.zeros((2, 8, half), jnp.float32)
+
+    @pl.when(step == 0)
+    def _():
+        reset(0)
+        for state in range(3):
+            for part in range(2):
+                turned[part, :, state * half : (state + 1) * half] = jnp.transpose(
+                    states_ref[state, part * half : (part + 1) * half, :]
+                )
+
+    @pl.when(step <= 1)
+    def _():
+        reset(1)
+
+    def multiply(part, target, state):
+        place = slice(state * half, (state + 1) * half)
+        target[:, place] = jnp.dot(
+            table_ref[...], turned[part, :, place], preferred_element_type=jnp.float32
+        )
+
+    def units(part, source, target, tile):
+        limit = vocab - tile * width
+        blocks = width // group
+        result = []
+        for lanes in range(half // LANES):
+            span = slice(part * half + lanes * LANES, part * half + (lanes + 1) * LANES)
+            local = slice(lanes * LANES, (lanes + 1) * LANES)
+            held = {}
+
+            def logits(state, block, lanes=lanes):
+                begin = state * half + lanes * LANES
+                value = source[block * group : (block + 1) * group, begin : begin + LANES]
+                if (block + 1) * group > last:
+                    value = jnp.where(row + block * group < limit, value, NEGATIVE)
+                return value
+
+            def tops(span=span, held=held, logits=logits):
+                held["top"], held["sum"], held["cross"] = [], [], []
+                for state in range(3):
+                    top = logits(state, 0)
+                    for block in range(1, blocks):
+                        top = jnp.maximum(top, logits(state, block))
+                    before = peak[state : state + 1, span]
+                    now = jnp.maximum(before, jnp.max(top, axis=0, keepdims=True))
+                    peak[state : state + 1, span] = now
+                    peaks_ref[pl.ds(tile, 1), state, span] = now
+                    fade = jnp.exp(before - now)
+                    held["top"].append(jnp.broadcast_to(now, (group, LANES)))
+                    held["sum"].append(sums_ref[state, :, span] * fade)
+                    if state == 0:
+                        held["cross"] = [cross_ref[other, :, span] * fade for other in range(2)]
+
+            def fold(value):
+                return value[:8] + value[8:]
+
+            def powers(begin, end, held=held, logits=logits, local=local, fold=fold):
+                for block in range(begin, end):
+                    place = slice(block * group, (block + 1) * group)
+                    base = logits(0, block)
+                    base_exp = jnp.exp(base - held["top"][0])
+                    held["sum"][0] += fold(base_exp)
+                    target[0, 0, place, local] = base_exp.astype(jnp.bfloat16)
+                    for state in range(1, 3):
+                        value = logits(state, block)
+                        value_exp = jnp.exp(value - held["top"][state])
+                        held["sum"][state] += fold(value_exp)
+                        target[0, state, place, local] = value_exp.astype(jnp.bfloat16)
+                        held["cross"][state - 1] += fold(base_exp * (base - value))
+
+            def finish(span=span, held=held):
+                for state in range(3):
+                    sums_ref[state, :, span] = held["sum"][state]
+                for other in range(2):
+                    cross_ref[other, :, span] = held["cross"][other]
+
+            result.append(tops)
+            cuts = 5
+            for cut in range(cuts):
+                result.append(
+                    functools.partial(powers, cut * blocks // cuts, (cut + 1) * blocks // cuts)
+                )
+            result.append(finish)
+        return result
+
+    def stage(part, target, work):
+        done = 0
+        for state in range(3):
+            multiply(part, target, state)
+            upto = (state + 1) * len(work) // 3
+            for unit in work[done:upto]:
+                unit()
+            done = upto
+
+    before = jnp.maximum(step - 1, 0)
+
+    @pl.when(step < steps)
+    def _():
+        stage(0, left, units(1, right, second_ref, before))
+        stage(1, right, units(0, left, first_ref, step))
+
+    @pl.when(step == steps)
+    def _():
+        for unit in units(1, right, second_ref, before):
+            unit()
+
+
+def vocab_forward(states, table):
+    _, rows, depth = states.shape
+    vocab = table.shape[0]
+    tiles = pl.cdiv(vocab, VOCAB_TILE)
+    half = rows // 2
+    kept = jax.ShapeDtypeStruct((tiles, 3, VOCAB_TILE, half), jnp.bfloat16)
+    block = (1, 3, VOCAB_TILE, half)
+    whole = lambda *shape: pl.BlockSpec(shape, lambda i: (0,) * len(shape))
+    return pl.pallas_call(
+        functools.partial(forward_kernel, vocab),
+        grid=(tiles + 1,),
+        in_specs=[
+            whole(3, rows, depth),
+            pl.BlockSpec((VOCAB_TILE, depth), lambda i: (jnp.minimum(i, tiles - 1), 0)),
+        ],
+        out_specs=[
+            pl.BlockSpec(block, lambda i: (jnp.minimum(i, tiles - 1), 0, 0, 0)),
+            pl.BlockSpec(block, lambda i: (jnp.maximum(i - 1, 0), 0, 0, 0)),
+            whole(tiles, 3, rows),
+            whole(3, 8, rows),
+            whole(2, 8, rows),
+        ],
+        out_shape=[
+            kept,
+            kept,
+            jax.ShapeDtypeStruct((tiles, 3, rows), jnp.float32),
+            jax.ShapeDtypeStruct((3, 8, rows), jnp.float32),
+            jax.ShapeDtypeStruct((2, 8, rows), jnp.float32),
+        ],
+        scratch_shapes=[
+            pltpu.VMEM((2, depth, 3 * half), jnp.bfloat16),
+            pltpu.VMEM((VOCAB_TILE, 3 * half), jnp.float32),
+            pltpu.VMEM((VOCAB_TILE, 3 * half), jnp.float32),
+            pltpu.VMEM((8, rows), jnp.float32),
+        ],
+        compiler_params=pltpu.CompilerParams(vmem_limit_bytes=VMEM_BYTES),
+        cost_estimate=pl.CostEstimate(
+            flops=6 * rows * depth * vocab,
+            bytes_accessed=2 * vocab * (depth + 3 * rows),
+            transcendentals=3 * rows * vocab,
+        ),
+        name="vocab_forward",
+    )(states, table)
+
+
+def backward_kernel(vocab, first_ref, second_ref, scales_ref, table_ref, out_ref, left, right, tail):
+    step = pl.program_id(0)
+    tiles = pl.num_programs(0) - 1
+    width, depth = table_ref.shape
+    half = first_ref.shape[3]
+    piece = 256
+    last = vocab - (pl.cdiv(vocab, width) - 1) * width
+    whole = last // piece * piece
+    tile = jnp.maximum(step - 1, 0)
+    limit = vocab - tile * width
+
+    def units(part, source, target, index):
+        result = []
+
+        def turn(lanes, block):
+            begin = part * half + lanes * LANES
+            span = slice(begin, begin + LANES)
+            place = slice(block * LANES, (block + 1) * LANES)
+            local = slice(lanes * LANES, (lanes + 1) * LANES)
+            factors = scales_ref[pl.ds(index, 1), :, span][0]
+            base = source[0, 0, place, local].astype(jnp.float32) * factors[0:1]
+            for state in range(1, 3):
+                value = source[0, state, place, local].astype(jnp.float32) * factors[state : state + 1]
+                first = (state - 1) * half + lanes * LANES
+                target[first : first + LANES, place] = jnp.transpose(
+                    (value - base).astype(jnp.bfloat16)
+                )
+
+        for lanes in range(half // LANES):
+            for block in range(width // LANES):
+                result.append(functools.partial(turn, lanes, block))
+        return result
+
+    def multiply(part, source, start):
+        place = slice(start, start + piece)
+        span = slice(part * half, (part + 1) * half)
+        partial = jnp.dot(source[:, whole:], tail[:, place], preferred_element_type=jnp.float32)
+        if whole > 0:
+            partial += jnp.dot(
+                source[:, :whole], table_ref[:whole, place], preferred_element_type=jnp.float32
+            )
+        for probe in range(2):
+            out_ref[probe, span, place] += partial[probe * half : (probe + 1) * half]
+
+    def stage(part, source, work):
+        done = 0
+        pieces = depth // piece
+        for index in range(pieces):
+            multiply(part, source, index * piece)
+            upto = (index + 1) * len(work) // pieces
+            for unit in work[done:upto]:
+                unit()
+            done = upto
+
+    ahead = jnp.minimum(step, tiles - 1)
+
+    @pl.when(step == 0)
+    def _():
+        out_ref[...] = jnp.zeros_like(out_ref)
+        for unit in units(0, first_ref, left, ahead):
+            unit()
+
+    @pl.when(step > 0)
+    def _():
+        below = lax.broadcasted_iota(jnp.int32, (width - whole, depth), 0) + whole < limit
+        tail[...] = jnp.where(below, table_ref[whole:, :], jnp.zeros((), tail.dtype))
+        stage(0, left, units(1, second_ref, right, tile))
+        stage(1, right, units(0, first_ref, left, ahead))
+
+
+def vocab_backward(first, second, scales, table):
+    tiles, _, _, half = first.shape
+    vocab, depth = table.shape
+    rows = 2 * half
+    last = vocab - (tiles - 1) * VOCAB_TILE
+    block = (1, 3, VOCAB_TILE, half)
+    return pl.pallas_call(
+        functools.partial(backward_kernel, vocab),
+        grid=(tiles + 1,),
+        in_specs=[
+            pl.BlockSpec(block, lambda i: (jnp.minimum(i, tiles - 1), 0, 0, 0)),
+            pl.BlockSpec(block, lambda i: (jnp.maximum(i - 1, 0), 0, 0, 0)),
+            pl.BlockSpec((tiles, 3, rows), lambda i: (0, 0, 0)),
+            pl.BlockSpec((VOCAB_TILE, depth), lambda i: (jnp.maximum(i - 1, 0), 0)),
+        ],
+        out_specs=pl.BlockSpec((2, rows, depth), lambda i: (0, 0, 0)),
+        out_shape=jax.ShapeDtypeStruct((2, rows, depth), jnp.float32),
+        scratch_shapes=[
+            pltpu.VMEM((2 * half, VOCAB_TILE), jnp.bfloat16),
+            pltpu.VMEM((2 * half, VOCAB_TILE), jnp.bfloat16),
+            pltpu.VMEM((VOCAB_TILE - last // 256 * 256, depth), jnp.bfloat16),
+        ],
+        compiler_params=pltpu.CompilerParams(vmem_limit_bytes=VMEM_BYTES),
+        cost_estimate=pl.CostEstimate(
+            flops=4 * rows * depth * vocab,
+            bytes_accessed=2 * vocab * (depth + 3 * rows),
+            transcendentals=0,
+        ),
+        name="vocab_backward",
+    )(first, second, scales, table)
 
 
 def body(
@@ -203,22 +478,10 @@
     gathered = lax.all_gather(states, "batch", axis=1, tiled=True)
     all_rows = gathered.shape[1]
 
-    def block_size():
-        return 512
-
-    def block_stats(offset):
-        portion = lax.dynamic_slice_in_dim(gathered, offset, block_size(), 1)
-        logits = jnp.einsum("std,vd->stv", portion, unembed, preferred_element_type=jnp.float32)
-        peak_rows = jnp.max(logits, axis=-1)
-        exponent = jnp.exp(logits - peak_rows[..., None])
-        crossing = jnp.sum(exponent[0][None] * (logits[0][None] - logits[1:]), axis=-1)
-        return (peak_rows, jnp.sum(exponent, axis=-1), crossing)
-
-    stat_offsets = jnp.arange(all_rows // block_size(), dtype=jnp.int32) * block_size()
-    peak_all, sums_all, cross_all = lax.map(block_stats, stat_offsets)
-    peak_all = jnp.transpose(peak_all, (1, 0, 2)).reshape(3, all_rows)
-    sums_all = jnp.transpose(sums_all, (1, 0, 2)).reshape(3, all_rows)
-    cross_all = jnp.transpose(cross_all, (1, 0, 2)).reshape(2, all_rows)
+    first, second, peaks, sums_part, cross_part = vocab_forward(gathered, unembed)
+    peak_all = peaks[-1]
+    sums_all = jnp.sum(sums_part, axis=1)
+    cross_all = jnp.sum(cross_part, axis=1)
 
     def combine(earlier, later):
         peak_a, sums_a, cross_a = earlier
@@ -238,25 +501,11 @@
     diverge_own = lax.dynamic_slice_in_dim(diverge, batch_index * tok_rows, tok_rows, 1)
     loss_local = jnp.sum(weight_own * (diverge_own[0] + diverge_own[1]))
     token_coef = weight_all.reshape(-1) / token_count
-    size = block_size()
-
-    def block_grads(inner):
-        portion = lax.dynamic_slice_in_dim(gathered, inner, size, 1)
-        totals_part = lax.dynamic_slice_in_dim(log_totals, inner, size, 1)
-        coef_part = lax.dynamic_slice_in_dim(token_coef, inner, size, 0)
-        logits = jnp.einsum("std,vd->stv", portion, unembed, preferred_element_type=jnp.float32)
-        probs = jnp.exp(logits - totals_part[..., None])
-        dlogits = (coef_part[None, :, None] * (probs[1:] - probs[0][None])).astype(jnp.bfloat16)
-        return jnp.einsum(
-            "sbv,vd->bsd", dlogits, unembed, preferred_element_type=jnp.float32
-        ).reshape(size, 2 * width)
-
-    inner_offsets = jnp.arange(tok_rows * lax.axis_size("batch") // size, dtype=jnp.int32) * size
+    scales = token_coef[None, None, :] * jnp.exp(peaks - log_totals[None])
+    partial = vocab_backward(first, second, scales, unembed)
     dstates = (
         lax.psum_scatter(
-            lax.map(block_grads, inner_offsets)
-            .reshape(tok_rows * lax.axis_size("batch"), 2 * width)
-            .astype(jnp.bfloat16),
+            jnp.transpose(partial, (1, 0, 2)).reshape(all_rows, 2 * width).astype(jnp.bfloat16),
             "batch",
             scatter_dimension=0,
             tiled=True,

time: 1080 us -> 909 us (0.84)
  other arithmetic: 158 us -> 26.7 us
  Pallas kernels: 0 us -> 101 us
  matrix products: 124 us -> 32.4 us
  local copies, waits for them, and re-layouts: 83.7 us -> 31.6 us
    pallas_call x0 -> x2, Pallas kernels: none -> 101 us  [the longest x1 65.3 us: vocab_forward(): pl.pallas_call(functools.partial(forward_kernel, vocab), grid=(tiles + 1,...]
    dot_general x2 -> x0, matrix products: 91.5 us -> none  [the longest x1 49.4 us: block_stats(): jnp.einsum('std,vd->stv', portion, unembed, preferred_element_type=jnp.fl...]
    reduce_sum x2, other arithmetic: 83.8 us -> 1.6 us  [the longest x1 0.82 us: body(): sums_all = jnp.sum(sums_part, axis=1)]
    exp x1 -> x0, other arithmetic: 52.1 us -> none  [block_grads(): probs = jnp.exp(logits - totals_part[..., None])]
    sub x2 -> x0, local copies, waits for them, and re-layouts: 35.1 us -> none  [the longest x1 17.6 us: block_grads(): probs[1:] - probs[0][None]]
    mul x1 -> x0, local copies, waits for them, and re-layouts: 17.6 us -> none  [block_stats(): exponent[0][None] * (logits[0][None] - logits[1:])]
where the time goes in v2:
time: 909 us; the launch traced here: 902 us
  waiting for transfers between devices  523 us (58%)
  blocking collectives  165 us (18%)
  Pallas kernels  101 us (11%)
  matrix products  32.4 us (4%)
  local copies, waits for them, and re-layouts  31.6 us (3%)
  other arithmetic  26.7 us (3%)
  between operations  20.4 us (2%)
    unnamed x15, waiting for transfers between devices  84 us
    all_gather x1, waiting for transfers between devices, body(): lax.all_gather(w_proj, ('seq', 'batch'), axis=0, tiled=True)  79.4 us
    all_gather x1, waiting for transfers between devices, body(): lax.all_gather(w_fc, ('seq', 'batch'), axis=0, tiled=True)  74.5 us
    pallas_call x1, Pallas kernels, vocab_forward(): pl.pallas_call(functools.partial(forward_kernel, vocab), grid=(tiles + 1,...  65.3 us
    reduce_scatter x1, waiting for transfers between devices, body(): lax.psum_scatter(grad_w.astype(jnp.bfloat16), 'seq', scatter_dimension=1,...  49.6 us
    all_gather x1, waiting for transfers between devices, body(): lax.all_gather(w_qkv, ('seq', 'batch'), axis=0, tiled=True)  47.8 us
    all_gather x1, waiting for transfers between devices, body(): lax.all_gather(w_out, ('seq', 'batch'), axis=0, tiled=True)  47.6 us
    all_gather x1, waiting for transfers between devices, body(): gathered = lax.all_gather(states, 'batch', axis=1, tiled=True)  43.7 us
  transfers between devices with their start and end apart: 13, of which 12 were waited for; matrix products, arithmetic and copies ran while one was open for 4% of the time, Pallas kernels for 0%

profile of v2, /device:TPU:0, one launch (start us, length us, event | category | flops | bytes accessed | tf_op | source)
XLA Modules:
  0.0 901.5 jit_solution(865059048983285315)
XLA Ops:
  8.1 12.7 %all-gather.3 = s32[4,1,128]{2,1,0:T(1,128)S(1)} all-gather(s32[1,1,128]{2,1,0:T(1,128)} %bitcast.172), channel_id=1, replica_groups=mesh['seq'=8,'batch'=4] {'batch'}, dimensions={0}, use_global_device_ids=true | all-gather | bytes 2560 | tf_op jit(solution)/shard_map/all_gather | solution.py:381
  20.8 14.4 %gather_fusion = bf16[512,1024]{1,0:T(8,128)(2,1)S(1)} fusion(bf16[12576,1024]{1,0:T(8,128)(2,1)} %param.23, s32[1024]{0:T(1024)S(1)} %pad_clamp_fusion), kind=kCustom, calls=%fused_computation | custom fusion | bytes 2099200 | tf_op jit(solution)/shard_map/jit(_take)/gather | solution.py:394
  38.4 26.5 %reduce-scatter.9.cloned.1.call-done = bf16[128,1024]{1,0:T(8,128)(2,1)} async-done(((bf16[512,1024]{1,0:T(8,128)(2,1)}), bf16[128,1024]{1,0:T(8,128)(2,1)}) %reduce-scatter.9.cloned.1.call-update) | async-done | bytes 262160 | tf_op jit(solution)/shard_map/reduce_scatter | solution.py:395
  67.1 47.8 %all-gather.15.cloned.1.call-done = bf16[1024,3072]{1,0:T(8,128)(2,1)} async-done(((bf16[32,3072]{1,0:T(8,128)(2,1)}), bf16[1024,3072]{1,0:T(8,128)(2,1)}) %all-gather.15.cloned.1.call-update) | async-done | bytes 6291472 | tf_op jit(solution)/shard_map/all_gather | solution.py:402
  115.0 4.0 convolution_add_fusion.1
  123.4 8.9 all_gather.61
  132.4 20.1 %all-gather.27.cloned.1.call-done = bf16[2,1024,1024]{2,1,0:T(8,128)(2,1)} async-done(((bf16[2,128,1024]{2,1,0:T(8,128)(2,1)}), bf16[2,1024,1024]{2,1,0:T(8,128)(2,1)}) %all-gather.27.cloned.1.call-update) | async-done | bytes 4194320 | tf_op jit(solution)/shard_map/all_gather | solution.py:408
  154.7 28.4 %all-gather.17.cloned.1.call-done = bf16[1024,1024]{0,1:T(8,128)(2,1)} async-done(((bf16[128,1024]{0,1:T(8,128)(2,1)}), bf16[1024,1024]{0,1:T(8,128)(2,1)}) %all-gather.17.cloned.1.call-update) | async-done | bytes 2097168 | tf_op jit(solution)/shard_map/all_gather | solution.py:425
  183.1 3.2 fusion.3
  186.3 3.2 copy-done
  192.1 21.7 %all-gather.19.cloned.1.call-done = bf16[1024,1024]{0,1:T(8,128)(2,1)} async-done(((bf16[128,1024]{0,1:T(8,128)(2,1)}), bf16[1024,1024]{0,1:T(8,128)(2,1)}) %all-gather.19.cloned.1.call-update) | async-done | bytes 2097168 | tf_op jit(solution)/shard_map/all_gather | solution.py:426
  213.8 6.3 fusion.71
  220.0 74.5 %all-gather.23.cloned.1.call-done = bf16[1024,4096]{1,0:T(8,128)(2,1)} async-done(((bf16[32,4096]{1,0:T(8,128)(2,1)}), bf16[1024,4096]{1,0:T(8,128)(2,1)}) %all-gather.23.cloned.1.call-update) | async-done | bytes 8388624 | tf_op jit(solution)/shard_map/all_gather | solution.py:404
  294.5 79.4 %all-gather.25.cloned.1.call-done = bf16[4096,1024]{1,0:T(8,128)(2,1)} async-done(((bf16[128,1024]{1,0:T(8,128)(2,1)}), bf16[4096,1024]{1,0:T(8,128)(2,1)}) %all-gather.25.cloned.1.call-update) | async-done | bytes 8388624 | tf_op jit(solution)/shard_map/all_gather | solution.py:405
  373.9 10.9 %fusion.32 = f32[128,1024]{1,0:T(8,128)S(1)} fusion(bf16[4096,1024]{1,0:T(8,128)(2,1)} %all-gather.25.cloned.1.call-done, bf16[1024,4096]{1,0:T(8,128)(2,1)} %all-gather.23.cloned.1.call-done, f32[4096]{0:T(1024)S(1)} %slice-done.1, bf16[128,1024]{1,0:T(8,128)(2,1)S(1)} %copy-done.1, f32[1024]{0:T(1024)S(1)} %bitcast.165, f32[1024]{0:T(1024)S(1)} %bitcast.166, ...), kind=kOutput, calls=%fused_computation.59 | convolution fusion | flops 2182873088 | bytes 17589248 | tf_op jit(solution)/shard_map/dot_general | solution.py:457
  384.8 47.6 %all-gather.21.cloned.1.call-done = bf16[1024,1024]{1,0:T(8,128)(2,1)} async-done(((bf16[32,1024]{1,0:T(8,128)(2,1)}), bf16[1024,1024]{1,0:T(8,128)(2,1)}) %all-gather.21.cloned.1.call-update) | async-done | bytes 2097168 | tf_op jit(solution)/shard_map/all_gather | solution.py:403
  441.0 6.6 all-reduce
  447.6 10.1 %all-gather.2 = s32[4,1,128]{2,1,0:T(1,128)S(1)} all-gather(s32[1,1,128]{2,1,0:T(1,128)S(1)} %bitcast.173), channel_id=1, replica_groups=mesh['seq'=8,'batch'=4] {'batch'}, dimensions={0}, use_global_device_ids=true | all-gather | bytes 2560 | tf_op jit(solution)/shard_map/all_gather | solution.py:382
  457.8 43.7 %all-gather.29.cloned.1.call-done.states_ref = bf16[3,512,1024]{2,1,0:T(8,128)(2,1)} async-done(((bf16[3,128,1024]{2,1,0:T(8,128)(2,1)}), bf16[3,512,1024]{2,1,0:T(8,128)(2,1)}) %all-gather.29.cloned.1.call-update) | async-done | bytes 3145744 | tf_op jit(solution)/shard_map/all_gather | solution.py:478
  501.4 65.3 %vocab_forward.1 = (bf16[10,3,1280,256]{3,2,1,0:T(8,128)(2,1)}, bf16[10,3,1280,256]{3,2,1,0:T(8,128)(2,1)}, f32[10,3,512]{2,1,0:T(4,128)}, f32[3,8,512]{2,1,0:T(8,128)}, f32[2,8,512]{2,1,0:T(8,128)}) custom-call(bf16[3,512,1024]{2,1,0:T(8,128)(2,1)} %all-gather.29.cloned.1.call-done.states_ref, bf16[12576,1024]{1,0:T(8,128)(2,1)} %table_ref.3), custom_call_target="tpu_custom_call" | custom-call | flops 39560675328 | bytes 64389120 | tf_op jit(solution)/shard_map/vocab_forward/pallas_call | solution.py:215
  569.1 13.1 %all-gather.5 = f32[4,2,512]{2,1,0:T(2,128)S(1)} all-gather(f32[1,2,512]{2,1,0:T(2,128)S(1)} %bitcast.159), channel_id=3, replica_groups=mesh['seq'=8,'batch'=4] {'batch'}, dimensions={0}, use_global_device_ids=true | all-gather | bytes 20480 | tf_op jit(solution)/shard_map/all_gather | solution.py:29
  582.2 13.1 %all_gather.63 = f32[4,3,512]{2,1,0:T(4,128)S(1)} all-gather(f32[1,3,512]{2,1,0:T(4,128)S(1)} %slice.142), channel_id=1, replica_groups=mesh['seq'=8,'batch'=4] {'batch'}, dimensions={0}, use_global_device_ids=true | all-gather | bytes 30720 | tf_op jit(solution)/shard_map/all_gather | solution.py:29
  595.3 13.1 %all-gather.4 = f32[4,3,512]{2,1,0:T(4,128)S(1)} all-gather(f32[1,3,512]{2,1,0:T(4,128)S(1)} %bitcast.154), channel_id=2, replica_groups=mesh['seq'=8,'batch'=4] {'batch'}, dimensions={0}, use_global_device_ids=true | all-gather | bytes 30720 | tf_op jit(solution)/shard_map/all_gather | solution.py:29
  609.5 38.9 %psum.36 = f32[]{:T(128)} all-reduce(f32[]{:T(128)} %get-tuple-element.206), channel_id=1, replica_groups=mesh['seq'=8,'batch'=4] {'seq','batch'}, use_global_device_ids=true, to_apply=%region_18.19 | all-reduce | flops 1 | bytes 8 | tf_op jit(solution)/shard_map/psum | solution.py:389
  650.6 36.0 %vocab_backward.1 = f32[2,512,1024]{2,1,0:T(8,128)} custom-call(bf16[10,3,1280,256]{3,2,1,0:T(8,128)(2,1)} %get-tuple-element.198.first_ref, bf16[10,3,1280,256]{3,2,1,0:T(8,128)(2,1)} %get-tuple-element.199.second_ref, f32[10,3,512]{2,1,0:T(4,128)} %exponential_multiply_fusion.scales_ref, bf16[12576,1024]{1,0:T(8,128)(2,1)} %table_ref.3), custom_call_target="tpu_custom_call" | custom-call | flops 26373783552 | bytes 64389120 | tf_op jit(solution)/shard_map/vocab_backward/pallas_call | solution.py:328
  691.7 4.0 copy.38
  695.7 44.0 %reduce-scatter.13.cloned.1.call-done = bf16[128,2048]{1,0:T(8,128)(2,1)} async-done(((bf16[512,2048]{1,0:T(8,128)(2,1)}), bf16[128,2048]{1,0:T(8,128)(2,1)}) %reduce-scatter.13.cloned.1.call-update) | async-done | bytes 524304
  747.5 49.6 %reduce-scatter.11.cloned.1.call-done = bf16[2,128,1024]{2,1,0:T(8,128)(2,1)} async-done(((bf16[2,1024,1024]{2,1,0:T(8,128)(2,1)}), bf16[2,128,1024]{2,1,0:T(8,128)(2,1)}) %reduce-scatter.11.cloned.1.call-update) | async-done | bytes 524304 | tf_op jit(solution)/shard_map/reduce_scatter | solution.py:536
  797.1 37.4 %reduce-scatter.15.cloned.1.call-done = bf16[128,2]{1,0:T(8,128)(2,1)} async-done(((bf16[1024,2]{1,0:T(8,128)(2,1)}), bf16[128,2]{1,0:T(8,128)(2,1)}) %reduce-scatter.15.cloned.1.call-update) | async-done | bytes 528
  835.3 11.7 %psum.41 = bf16[2,128]{1,0:T(2,128)(2,1)S(1)} all-reduce(bf16[2,128]{1,0:T(2,128)(2,1)S(1)} %copy.41), channel_id=1, replica_groups=mesh['seq'=8,'batch'=4] {'batch'}, use_global_device_ids=true, to_apply=%region_29.30 | all-reduce | flops 256 | bytes 1024 | tf_op jit(solution)/shard_map/psum | solution.py:533
  850.9 37.2 %all-reduce.1 = (f32[]{:T(128)}, f32[]{:T(128)}) all-reduce(f32[]{:T(128)} %get-tuple-element.207, f32[]{:T(128)S(6)} %mul.517), channel_id=1, replica_groups=mesh['seq'=8,'batch'=4] {'seq','batch'}, use_global_device_ids=true, to_apply=%region_16.17 | all-reduce | flops 2 | bytes 16 | tf_op jit(solution)/shard_map/psum | solution.py:545
  889.4 3.2 multiply_subtract_fusion
  (158 shorter events, 44.9 us)
Async XLA Ops:
  8.0 56.9 %reduce-scatter.9.cloned.1.call-start = ((), (), s32[]{:S(2)}) async-start(), calls=%async_computation.4 | async-start | bytes 1310720 | tf_op jit(solution)/shard_map/reduce_scatter | solution.py:395
  35.2 2.0 copy-start.4
  36.6 1.8 copy-start.9
  36.6 1.8 copy-start.8
  36.6 78.4 %slice-start = ((f32[7168]{0:T(1024)}), f32[3072]{0:T(1024)S(1)}, s32[]{:S(2)}) async-start(f32[7168]{0:T(1024)} %param.30), calls=%async_computation.17 | async-start | bytes 24576 | tf_op jit(solution)/shard_map/slice | solution.py:419
  36.6 78.4 %all-gather.15.cloned.1.call-start = ((), (), s32[]{:S(2)}) async-start(), calls=%async_computation.5 | async-start | bytes 6488064 | tf_op jit(solution)/shard_map/all_gather | solution.py:402
  37.2 115.4 %all-gather.27.cloned.1.call-start = ((), (), s32[]{:S(2)}) async-start(), calls=%async_computation.11 | async-start | bytes 4718592 | tf_op jit(solution)/shard_map/all_gather | solution.py:408
  38.1 145.0 %all-gather.17.cloned.1.call-start = ((), (), s32[]{:S(2)}) async-start(), calls=%async_computation.6 | async-start | bytes 2359296 | tf_op jit(solution)/shard_map/all_gather | solution.py:425
  119.4 3.9 copy-start.10
  119.5 33.0 %copy-start.1 = (bf16[128,1024]{1,0:T(8,128)(2,1)S(1)}, bf16[128,1024]{1,0:T(8,128)(2,1)}, u32[]{:S(2)}) copy-start(bf16[128,1024]{1,0:T(8,128)(2,1)} %reduce-scatter.9.cloned.1.call-done) | copy-start | bytes 786436
  120.4 93.4 %all-gather.19.cloned.1.call-start = ((), (), s32[]{:S(2)}) async-start(), calls=%async_computation.7 | async-start | bytes 2359296 | tf_op jit(solution)/shard_map/all_gather | solution.py:426
  121.2 173.3 %all-gather.23.cloned.1.call-start = ((), (), s32[]{:S(2)}) async-start(), calls=%async_computation.9 | async-start | bytes 8650752 | tf_op jit(solution)/shard_map/all_gather | solution.py:404
  122.0 252.0 %all-gather.25.cloned.1.call-start = ((), (), s32[]{:S(2)}) async-start(), calls=%async_computation.10 | async-start | bytes 8650752 | tf_op jit(solution)/shard_map/all_gather | solution.py:405
  122.7 309.7 %all-gather.21.cloned.1.call-start = ((), (), s32[]{:S(2)}) async-start(), calls=%async_computation.8 | async-start | bytes 2162688 | tf_op jit(solution)/shard_map/all_gather | solution.py:403
  123.3 378.1 %all-gather.29.cloned.1.call-start = ((), (), s32[]{:S(2)}) async-start(), calls=%async_computation.12 | async-start | bytes 3932160 | tf_op jit(solution)/shard_map/all_gather | solution.py:478
  186.3 3.2 copy-start
  213.8 160.2 %slice-start.1 = ((f32[7168]{0:T(1024)}), f32[4096]{0:T(1024)S(1)}, s32[]{:S(2)}) async-start(f32[7168]{0:T(1024)} %param.30), calls=%async_computation.18 | async-start | bytes 32768 | tf_op jit(solution)/shard_map/slice | solution.py:451
  434.6 3.0 copy-start.2
  437.6 2.0 copy-start.14
  437.6 10.0 %copy-start.13 = (s32[1,128]{1,0:T(1,128)S(1)}, s32[1,128]{1,0:T(1,128)}, u32[]{:S(2)}) copy-start(s32[1,128]{1,0:T(1,128)} %param.21) | copy-start | bytes 1540
  438.9 300.9 %reduce-scatter.13.cloned.1.call-start = ((), (), s32[]{:S(2)}) async-start(), calls=%async_computation.15 | async-start | bytes 2621440
  695.7 101.4 %reduce-scatter.11.cloned.1.call-start = ((), (), s32[]{:S(2)}) async-start(), calls=%async_computation.13 | async-start | bytes 4718592 | tf_op jit(solution)/shard_map/reduce_scatter | solution.py:536
  741.6 1.0 copy-start.3
  746.4 142.4 %copy-start.11 = (f32[2,128]{1,0:T(2,128)S(1)}, f32[2,128]{1,0:T(2,128)}, u32[]{:S(2)}) copy-start(f32[2,128]{1,0:T(2,128)} %param.37) | copy-start | bytes 3076
  746.4 142.4 %copy-start.12 = (f32[2,128]{1,0:T(2,128)S(1)}, f32[2,128]{1,0:T(2,128)}, u32[]{:S(2)}) copy-start(f32[2,128]{1,0:T(2,128)} %param.36) | copy-start | bytes 3076
  746.4 143.0 %copy-start.5 = (f32[2,128,1024]{2,1,0:T(8,128)S(1)}, f32[2,128,1024]{2,1,0:T(8,128)}, u32[]{:S(2)}) copy-start(f32[2,128,1024]{2,1,0:T(8,128)} %param.32) | copy-start | bytes 3145732
  746.4 143.0 %copy-start.6 = (f32[2,128,1024]{2,1,0:T(8,128)S(1)}, f32[2,128,1024]{2,1,0:T(8,128)}, u32[]{:S(2)}) copy-start(f32[2,128,1024]{2,1,0:T(8,128)} %param.35) | copy-start | bytes 3145732
  746.4 143.0 %copy-start.7 = (f32[2,128,1024]{2,1,0:T(8,128)S(1)}, f32[2,128,1024]{2,1,0:T(8,128)}, u32[]{:S(2)}) copy-start(f32[2,128,1024]{2,1,0:T(8,128)} %param.34) | copy-start | bytes 3145732
  746.4 88.1 %reduce-scatter.15.cloned.1.call-start = ((), (), s32[]{:S(2)}) async-start(), calls=%async_computation.16 | async-start | bytes 294912
  747.4 100.2 %all-reduce.4.cloned.1.call-start = ((), (), s32[]{:S(2)}) async-start(), calls=%async_computation.14 | async-start | bytes 1048576 | tf_op jit(solution)/shard_map/psum | solution.py:532
Sparse Core Ops, SparseCore 0:
  36.7 28.1 reduce-scatter.8
  439.0 62.3 all-gather.28
  695.8 43.9 reduce-scatter.12
  797.2 38.2 all-reduce.3
Sparse Core Ops, SparseCore 1:
  40.4 74.5 all-gather.14
  117.5 35.0 all-gather.26
  155.0 28.0 all-gather.16
  185.7 28.0 all-gather.18
  217.2 77.3 all-gather.22
  297.9 76.0 all-gather.24
  377.2 55.2 all-gather.20
  746.5 50.5 reduce-scatter.10
  800.8 33.6 reduce-scatter.14

commit v3 on v2

--- a/solution.py
+++ b/solution.py
@@ -23,17 +23,6 @@
 learn_rate = 0.03
 decay_rate = 0.01
 adam_eps = 1e-08
-
-
-def merged(part, axis, combine):
-    gathered = jax.tree.map(lambda a: lax.all_gather(a, axis), part)
-
-    def take(source):
-        return jax.tree.map(lambda a: lax.dynamic_index_in_dim(a, source, 0, False), gathered)
-
-    return lax.fori_loop(
-        1, lax.axis_size(axis), lambda source, state: combine(state, take(source)), take(0)
-    )
 
 
 def normalize(values, gain_row, offset_row):
@@ -349,6 +338,731 @@
         ),
         name="vocab_backward",
     )(first, second, scales, table)
+
+
+def plane_place(place):
+    core = lax.rem(place, 2)
+    return core, lax.rem(place // 2, 2), place // 4
+
+
+def plane_index(core, column, line):
+    return (line * 2 + column) * 2 + core
+
+
+def greet(partners):
+    barrier = pltpu.get_barrier_semaphore()
+    for partner in partners:
+        pl.semaphore_signal(barrier, inc=1, device_id=partner, device_id_type=pl.DeviceIdType.MESH)
+    pl.semaphore_wait(barrier, len(partners))
+
+
+def push(source, target, send, receive, partner):
+    copy = pltpu.make_async_remote_copy(
+        src_ref=source,
+        dst_ref=target,
+        send_sem=send,
+        recv_sem=receive,
+        device_id=partner,
+        device_id_type=pl.DeviceIdType.MESH,
+    )
+    copy.start()
+    return copy
+
+
+def arrived(target, receive, partner):
+    pltpu.make_async_remote_copy(
+        src_ref=target,
+        dst_ref=target,
+        send_sem=receive,
+        recv_sem=receive,
+        device_id=partner,
+        device_id_type=pl.DeviceIdType.MESH,
+    ).wait_recv()
+
+
+def departed(source, send, partner):
+    pltpu.make_async_remote_copy(
+        src_ref=source,
+        dst_ref=source,
+        send_sem=send,
+        recv_sem=send,
+        device_id=partner,
+        device_id_type=pl.DeviceIdType.MESH,
+    ).wait_send()
+
+
+class LineSum:
+    def __init__(self, count, size, own, land, held, total, inner_sem, outer_sem, receive_sem):
+        lines = lax.axis_size("batch")
+        place = lax.axis_index("batch")
+        near = place < lines // 2
+        self.count, self.size = count, size
+        self.own, self.land, self.held, self.total = own, land, held, total
+        self.inner_sem, self.outer_sem, self.receive_sem = inner_sem, outer_sem, receive_sem
+        self.middle = (place == lines // 2 - 1) | (place == lines // 2)
+        self.end = (place == 0) | (place == lines - 1)
+        self.inner = {"batch": jnp.where(near, place + 1, place - 1)}
+        self.outer = {"batch": jnp.where(near, place - 1, place + 1)}
+        self.slot = jnp.where(self.middle, 1, 0)
+
+    def rows(self, index):
+        return pl.ds(index * self.size, self.size)
+
+    def send_in(self, index):
+        rows = self.rows(index)
+        push(
+            self.held.at[rows],
+            self.land.at[self.slot, rows],
+            self.inner_sem.at[index],
+            self.receive_sem.at[self.slot, index],
+            self.inner,
+        )
+
+    def begin(self, indices):
+        @pl.when(self.end)
+        def _():
+            for index in indices:
+                rows = self.rows(index)
+                self.held[rows, :] = self.own(rows).astype(jnp.bfloat16)
+                self.send_in(index)
+
+    def gather(self, index):
+        rows = self.rows(index)
+
+        @pl.when(jnp.logical_not(self.end))
+        def _():
+            arrived(self.land.at[0, rows], self.receive_sem.at[0, index], self.outer)
+            own = self.own(rows).astype(jnp.float32)
+            self.held[rows, :] = (own + self.land[0, rows, :].astype(jnp.float32)).astype(jnp.bfloat16)
+            self.send_in(index)
+
+    def spread(self, index):
+        rows = self.rows(index)
+
+        @pl.when(self.middle)
+        def _():
+            arrived(self.land.at[1, rows], self.receive_sem.at[1, index], self.inner)
+            both = self.held[rows, :].astype(jnp.float32) + self.land[1, rows, :].astype(jnp.float32)
+            self.total[rows, :] = both.astype(jnp.bfloat16)
+
+        @pl.when(jnp.logical_not(self.middle))
+        def _():
+            arrived(self.total.at[rows], self.receive_sem.at[2, index], self.inner)
+
+        @pl.when(jnp.logical_not(self.end))
+        def _():
+            push(
+                self.total.at[rows],
+                self.total.at[rows],
+                self.outer_sem.at[index],
+                self.receive_sem.at[2, index],
+                self.outer,
+            )
+
+    def finish(self):
+        for index in range(self.count):
+            rows = self.rows(index)
+            departed(self.held.at[rows], self.inner_sem.at[index], self.inner)
+
+            @pl.when(jnp.logical_not(self.end))
+            def _(rows=rows, index=index):
+                departed(self.total.at[rows], self.outer_sem.at[index], self.outer)
+
+    @staticmethod
+    def scratch(count, rows, depth):
+        return [
+            pltpu.VMEM((2, rows, depth), jnp.bfloat16),
+            pltpu.VMEM((rows, depth), jnp.bfloat16),
+            pltpu.SemaphoreType.DMA((count,)),
+            pltpu.SemaphoreType.DMA((count,)),
+            pltpu.SemaphoreType.DMA((3, count)),
+        ]
+
+
+def others(axis):
+    size = lax.axis_size(axis)
+    place = lax.axis_index(axis)
+    return [lax.rem(place + step, size) for step in range(1, size)]
+
+
+def share_kernel(axis, tile_ref, out_ref, local_sem, send_sem, receive_sem):
+    place = lax.axis_index(axis)
+    peers = others(axis)
+    local = pltpu.make_async_copy(tile_ref, out_ref.at[place], local_sem)
+    local.start()
+    greet([{axis: peer} for peer in peers])
+    copies = [
+        push(tile_ref, out_ref.at[place], send_sem.at[index], receive_sem.at[place], {axis: peer})
+        for index, peer in enumerate(peers)
+    ]
+    for peer in peers:
+        arrived(out_ref.at[peer], receive_sem.at[peer], {axis: peer})
+    for copy in copies:
+        copy.wait_send()
+    local.wait()
+
+
+def share(tile, axis, identity, name):
+    size = lax.axis_size(axis)
+    space = pl.BlockSpec(memory_space=pltpu.VMEM)
+    return pl.pallas_call(
+        functools.partial(share_kernel, axis),
+        in_specs=[space],
+        out_specs=space,
+        out_shape=jax.ShapeDtypeStruct((size,) + tile.shape, tile.dtype),
+        scratch_shapes=[
+            pltpu.SemaphoreType.DMA,
+            pltpu.SemaphoreType.DMA((size - 1,)),
+            pltpu.SemaphoreType.DMA((size,)),
+        ],
+        compiler_params=pltpu.CompilerParams(collective_id=identity, has_side_effects=True),
+        name=name,
+    )(tile)
+
+
+def swap_kernel(send_ref, out_ref, local_sem, send_sem, receive_sem):
+    place = lax.axis_index("seq")
+    peers = others("seq")
+    local = pltpu.make_async_copy(send_ref.at[place], out_ref.at[place], local_sem)
+    local.start()
+    greet([{"seq": peer} for peer in peers])
+    copies = [
+        push(send_ref.at[peer], out_ref.at[place], send_sem.at[index], receive_sem.at[place], {"seq": peer})
+        for index, peer in enumerate(peers)
+    ]
+    for peer in peers:
+        arrived(out_ref.at[peer], receive_sem.at[peer], {"seq": peer})
+    for copy in copies:
+        copy.wait_send()
+    local.wait()
+
+
+def swap(blocks, identity, name):
+    size = lax.axis_size("seq")
+    space = pl.BlockSpec(memory_space=pltpu.VMEM)
+    return pl.pallas_call(
+        swap_kernel,
+        in_specs=[space],
+        out_specs=space,
+        out_shape=jax.ShapeDtypeStruct(blocks.shape, blocks.dtype),
+        scratch_shapes=[
+            pltpu.SemaphoreType.DMA,
+            pltpu.SemaphoreType.DMA((size - 1,)),
+            pltpu.SemaphoreType.DMA((size,)),
+        ],
+        compiler_params=pltpu.CompilerParams(
+            collective_id=identity, has_side_effects=True, vmem_limit_bytes=VMEM_BYTES
+        ),
+        name=name,
+    )(blocks)
+
+
+def lookup_kernel(ids_ref, table_ref, out_ref, window, rows_f32, sems):
+    rows, depth = out_ref.shape
+    vocab = table_ref.shape[0]
+    ring = window.shape[0]
+    group = window.shape[1]
+    rows_f32[...] = jnp.zeros_like(rows_f32)
+    line = lax.broadcasted_iota(jnp.int32, (group, depth), 0)
+
+    def fetch(index, slot):
+        base = pl.multiple_of(ids_ref[index] // group * group, group)
+        return pltpu.make_async_copy(table_ref.at[pl.ds(base, group)], window.at[slot], sems.at[slot])
+
+    def inside(index):
+        value = ids_ref[index]
+        return (value >= 0) & (value < vocab)
+
+    def loop(index, carry):
+        slot = lax.rem(index, ring)
+        late = jnp.maximum(index - ring, 0)
+
+        @pl.when((index >= ring) & inside(late))
+        def _():
+            fetch(late, slot).wait()
+            place = lax.rem(ids_ref[late], group)
+            block = window[slot].astype(jnp.float32)
+            rows_f32[pl.ds(late, 1), :] = jnp.sum(jnp.where(line == place, block, 0.0), axis=0, keepdims=True)
+
+        now = jnp.minimum(index, rows - 1)
+
+        @pl.when((index < rows) & inside(now))
+        def _():
+            fetch(now, slot).start()
+
+        return carry
+
+    lax.fori_loop(0, rows + ring, loop, 0)
+    out_ref[...] = rows_f32[...].astype(jnp.bfloat16)
+
+
+def lookup(ids, table):
+    rows = ids.shape[0]
+    depth = table.shape[1]
+    return pl.pallas_call(
+        lookup_kernel,
+        in_specs=[pl.BlockSpec(memory_space=pltpu.SMEM), pl.BlockSpec(memory_space=pl.ANY)],
+        out_specs=pl.BlockSpec(memory_space=pltpu.VMEM),
+        out_shape=jax.ShapeDtypeStruct((rows, depth), jnp.bfloat16),
+        scratch_shapes=[
+            pltpu.VMEM((64, 16, depth), jnp.bfloat16),
+            pltpu.VMEM((rows, depth), jnp.float32),
+            pltpu.SemaphoreType.DMA((64,)),
+        ],
+        compiler_params=pltpu.CompilerParams(vmem_limit_bytes=VMEM_BYTES),
+        name="lookup",
+    )(ids, table)
+
+
+def front_kernel(
+    count,
+    picked_ref, joined_ref, fc_ref, proj_ref, bias_ref,
+    stream_ref, joined_out, fc_out, proj_out, bias_out,
+    land, held, inner_sem, outer_sem, receive_sem,
+    local_sem, cross_send, cross_receive, plane_send, plane_receive, bias_send, bias_receive,
+):
+    lines = lax.axis_size("batch")
+    place = lax.axis_index("batch")
+    size = lax.axis_size("seq")
+    spot = lax.axis_index("seq")
+    core, column, line = plane_place(spot)
+    rows = size // 4
+    beside = plane_index(core, 1 - column, line)
+    sibling = plane_index(1 - core, column, line)
+    across = [plane_index(core, column, lax.rem(line + step, rows)) for step in range(1, rows)]
+    corners = [plane_index(core, 1 - column, lax.rem(line + step, rows)) for step in range(1, rows)]
+    planes = others("batch")
+    peers = others("seq")
+    outs = (joined_out, fc_out, proj_out)
+    proj_rows = proj_ref.shape[0]
+
+    def piece(array, half, slot):
+        if array < 2:
+            return outs[array].at[slot, pl.ds(half * (lines // 2), lines // 2)]
+        return outs[array].at[slot, pl.ds(half * (proj_rows // 2), proj_rows // 2)]
+
+    started = []
+
+    def send(array, half, slot, way, index, target):
+        view = piece(array, half, slot)
+        started.append(
+            push(view, view, plane_send.at[array, half, way, index], plane_receive.at[array, half, slot], {"seq": target})
+        )
+
+    def await_piece(array, half, slot):
+        arrived(piece(array, half, slot), plane_receive.at[array, half, slot], {"seq": slot})
+
+    def own(array):
+        for half in range(2):
+            send(array, half, spot, 0, 0, beside)
+            for index, target in enumerate(across):
+                send(array, half, spot, 1 + index, 0, target)
+            send(array, half, spot, rows, 0, sibling)
+
+    def relay_side(array):
+        await_piece(array, 0, beside)
+        for index, target in enumerate(across):
+            send(array, 0, beside, 1 + index, 1, target)
+        for index, source in enumerate(across):
+            await_piece(array, 1, source)
+            send(array, 1, source, 0, 1 + index, beside)
+
+    def relay_core(array):
+        send(array, 0, beside, rows, 1, sibling)
+        await_piece(array, 1, beside)
+        send(array, 1, beside, rows, 1, sibling)
+        for index, source in enumerate(across):
+            send(array, 1, source, rows, 2 + index, sibling)
+            await_piece(array, 0, source)
+            send(array, 0, source, rows, 2 + index, sibling)
+        for index, source in enumerate(corners):
+            for half in range(2):
+                await_piece(array, half, source)
+                send(array, half, source, rows, 1 + rows + index, sibling)
+
+    def receive_core(array):
+        for step in range(rows):
+            for side in range(2):
+                source = plane_index(1 - core, side, lax.rem(line + step, rows))
+                for half in range(2):
+                    await_piece(array, half, source)
+
+    proj_copy = pltpu.make_async_copy(proj_ref, proj_out.at[spot], local_sem.at[0])
+    proj_copy.start()
+    locals_ = [
+        pltpu.make_async_copy(source.at[place], out.at[spot, place], local_sem.at[1 + index])
+        for index, (source, out) in enumerate(((joined_ref, joined_out), (fc_ref, fc_out)))
+    ]
+    for copy in locals_:
+        copy.start()
+    bias_copy = pltpu.make_async_copy(bias_ref, bias_out.at[spot], local_sem.at[3])
+    bias_copy.start()
+    greet([{"batch": plane} for plane in planes] + [{"seq": peer} for peer in peers])
+    line_sum = LineSum(
+        count, stream_ref.shape[0] // count, lambda at: picked_ref[at, :],
+        land, held, stream_ref, inner_sem, outer_sem, receive_sem,
+    )
+    line_sum.begin(range(count))
+    crossing = []
+    for array, source, out in ((0, joined_ref, joined_out), (1, fc_ref, fc_out)):
+        for index, plane in enumerate(planes):
+            crossing.append(
+                push(source.at[plane], out.at[spot, place], cross_send.at[array, index], cross_receive.at[array, place], {"batch": plane})
+            )
+    bias_copies = [
+        push(bias_ref, bias_out.at[spot], bias_send.at[index], bias_receive.at[spot], {"seq": peer})
+        for index, peer in enumerate(peers)
+    ]
+    proj_copy.wait()
+    own(2)
+    for copy in locals_:
+        copy.wait()
+
+    def receive_cross(array):
+        for plane in planes:
+            arrived(outs[array].at[spot, plane], cross_receive.at[array, plane], {"batch": plane})
+
+    def turn(array):
+        receive_cross(array)
+        own(array)
+
+    todo = [
+        lambda: turn(0),
+        lambda: relay_side(2),
+        lambda: turn(1),
+        lambda: relay_core(2),
+        lambda: relay_side(0),
+        lambda: relay_core(0),
+        lambda: relay_side(1),
+        lambda: relay_core(1),
+        lambda: receive_core(2),
+        lambda: receive_core(0),
+        lambda: receive_core(1),
+    ]
+    for index in range(count + 1):
+        if index < count:
+            line_sum.gather(index)
+        if index >= 1:
+            line_sum.spread(index - 1)
+        if todo:
+            todo.pop(0)()
+    for work in todo:
+        work()
+    for peer in peers:
+        arrived(bias_out.at[peer], bias_receive.at[peer], {"seq": peer})
+    bias_copy.wait()
+    for copy in started + crossing + bias_copies:
+        copy.wait_send()
+    line_sum.finish()
+
+
+def front(picked, joined, fc, proj, bias):
+    size = lax.axis_size("seq")
+    lines = lax.axis_size("batch")
+    rows, depth = picked.shape
+    count = 8
+    vmem = pl.BlockSpec(memory_space=pltpu.VMEM)
+    anywhere = pl.BlockSpec(memory_space=pl.ANY)
+    dma = pltpu.SemaphoreType.DMA
+    chips = size // 2
+    return pl.pallas_call(
+        functools.partial(front_kernel, count),
+        in_specs=[vmem, anywhere, anywhere, anywhere, vmem],
+        out_specs=[vmem, anywhere, anywhere, anywhere, vmem],
+        out_shape=[
+            jax.ShapeDtypeStruct((rows, depth), jnp.bfloat16),
+            jax.ShapeDtypeStruct((size,) + joined.shape, jnp.bfloat16),
+            jax.ShapeDtypeStruct((size,) + fc.shape, jnp.bfloat16),
+            jax.ShapeDtypeStruct((size,) + proj.shape, jnp.bfloat16),
+            jax.ShapeDtypeStruct((size,) + bias.shape, jnp.float32),
+        ],
+        scratch_shapes=LineSum.scratch(count, rows, depth) + [
+            dma((4,)),
+            dma((2, lines - 1)),
+            dma((2, lines)),
+            dma((3, 2, size // 4 + 1, chips + 1)),
+            dma((3, 2, size)),
+            dma((size - 1,)),
+            dma((size,)),
+        ],
+        compiler_params=pltpu.CompilerParams(
+            collective_id=1, has_side_effects=True, vmem_limit_bytes=VMEM_BYTES
+        ),
+        name="front",
+    )(picked, joined, fc, proj, bias)
+
+
+def layer_sum_kernel(count, part_ref, total_ref, land, held, inner_sem, outer_sem, receive_sem):
+    line_sum = LineSum(
+        count, part_ref.shape[0] // count, lambda at: part_ref[at, :],
+        land, held, total_ref, inner_sem, outer_sem, receive_sem,
+    )
+    greet([{"batch": plane} for plane in others("batch")])
+    line_sum.begin(range(count))
+    for index in range(count + 1):
+        if index < count:
+            line_sum.gather(index)
+        if index >= 1:
+            line_sum.spread(index - 1)
+    line_sum.finish()
+
+
+def layer_sum(part):
+    rows, depth = part.shape
+    count = 8
+    vmem = pl.BlockSpec(memory_space=pltpu.VMEM)
+    return pl.pallas_call(
+        functools.partial(layer_sum_kernel, count),
+        in_specs=[vmem],
+        out_specs=vmem,
+        out_shape=jax.ShapeDtypeStruct((rows, depth), jnp.bfloat16),
+        scratch_shapes=LineSum.scratch(count, rows, depth),
+        compiler_params=pltpu.CompilerParams(
+            collective_id=4, has_side_effects=True, vmem_limit_bytes=VMEM_BYTES
+        ),
+        name="layer_sum",
+    )(part)
+
+
+def attention_kernel(heads, in_ref, out_ref):
+    sources, _, tokens, columns = in_ref.shape
+    length = sources * tokens
+    head_dim = columns // heads
+    block = 2 * tokens
+    lane = lax.broadcasted_iota(jnp.int32, (block, columns), 1) // head_dim
+    keys = jnp.concatenate([in_ref[source, 1] for source in range(sources)], axis=0)
+    values = jnp.concatenate([in_ref[source, 2] for source in range(sources)], axis=0)
+    for first in range(0, length, block):
+        end = first + block
+        queries = jnp.concatenate([in_ref[source, 0] for source in range(first // tokens, end // tokens)], axis=0)
+        allowed = lax.broadcasted_iota(jnp.int32, (block, end), 1) <= (
+            lax.broadcasted_iota(jnp.int32, (block, end), 0) + first
+        )
+        mixed = None
+        for head in range(heads):
+            chosen = jnp.where(lane == head, queries, jnp.zeros((), queries.dtype))
+            scores = lax.dot_general(
+                chosen, keys[:end], (((1,), (1,)), ((), ())), preferred_element_type=jnp.float32
+            ) * head_dim ** (-0.5)
+            scores = jnp.where(allowed, scores, NEGATIVE)
+            exponent = jnp.exp(scores - jnp.max(scores, axis=-1, keepdims=True))
+            result = jnp.dot(
+                exponent.astype(jnp.bfloat16), values[:end], preferred_element_type=jnp.float32
+            ) / jnp.sum(exponent, axis=-1, keepdims=True)
+            mixed = result if mixed is None else jnp.where(lane == head, result, mixed)
+        mixed = mixed.astype(jnp.bfloat16)
+        for index in range(block // tokens):
+            out_ref[first // tokens + index] = mixed[index * tokens : (index + 1) * tokens]
+
+
+def attention(blocks, heads):
+    sources, _, tokens, columns = blocks.shape
+    vmem = pl.BlockSpec(memory_space=pltpu.VMEM)
+    return pl.pallas_call(
+        functools.partial(attention_kernel, heads),
+        in_specs=[vmem],
+        out_specs=vmem,
+        out_shape=jax.ShapeDtypeStruct((sources, tokens, columns), jnp.bfloat16),
+        compiler_params=pltpu.CompilerParams(vmem_limit_bytes=VMEM_BYTES),
+        name="attention",
+    )(blocks)
+
+
+def reduce_kernel(
+    count,
+    grad_ref, bias_ref, note_ref,
+    total_ref, bias_out, note_out,
+    mine, sibling_land, side_land, line_land, side_sum, line_sum_ref, last_land, own_sum,
+    land, held, inner_sem, outer_sem, receive_sem,
+    tile_land, tile_line, tile_out,
+    local_sem, core_send, core_receive, side_send, side_receive, line_send, line_receive,
+    last_send, last_receive, bias_send, bias_receive, plane_send, plane_receive, note_send, note_receive,
+):
+    size = lax.axis_size("seq")
+    spot = lax.axis_index("seq")
+    place = lax.axis_index("batch")
+    core, column, line = plane_place(spot)
+    rows = size // 4
+    width = total_ref.shape[0] // 2
+    beside = {"seq": plane_index(core, 1 - column, line)}
+    sibling = {"seq": plane_index(1 - core, column, line)}
+    across = [{"seq": plane_index(core, column, lax.rem(line + step, rows))} for step in range(1, rows)]
+    peers = others("seq")
+    planes = others("batch")
+    f32 = jnp.float32
+    order = [(lax.rem(line + step, rows), side) for step in range(rows) for side in (1 - column, column)]
+    places = [(step, side) for step in range(rows) for side in range(2)]
+
+    loads = [
+        pltpu.make_async_copy(
+            grad_ref.at[:, plane_index(core, side, at)], mine.at[step, index], local_sem.at[step, index]
+        )
+        for (step, index), (at, side) in zip(places, order)
+    ]
+    for copy in loads:
+        copy.start()
+    tile_land[spot] = bias_ref[spot]
+    greet([{"batch": plane} for plane in planes] + [{"seq": peer} for peer in peers])
+    sent = []
+    for (step, index), (at, side) in zip(places, order):
+        sent.append(
+            push(
+                grad_ref.at[:, plane_index(1 - core, side, at)], sibling_land.at[step, index],
+                core_send.at[step, index], core_receive.at[step, index], sibling,
+            )
+        )
+    for index, peer in enumerate(peers):
+        sent.append(
+            push(bias_ref.at[peer], tile_land.at[spot], bias_send.at[index], bias_receive.at[spot], {"seq": peer})
+        )
+    for (step, index), copy in zip(places, loads):
+        copy.wait()
+        arrived(sibling_land.at[step, index], core_receive.at[step, index], sibling)
+        mine[step, index] = (
+            mine[step, index].astype(f32) + sibling_land[step, index].astype(f32)
+        ).astype(jnp.bfloat16)
+        if index == 0:
+            sent.append(
+                push(mine.at[step, 0, 0], side_land.at[step], side_send.at[step], side_receive.at[step], beside)
+            )
+        if step > 0:
+            sent.append(
+                push(
+                    mine.at[step, index, 1], line_land.at[step - 1, index],
+                    line_send.at[step - 1, index], line_receive.at[step - 1, index], across[step - 1],
+                )
+            )
+    for step in list(range(1, rows)) + [0]:
+        arrived(side_land.at[step], side_receive.at[step], beside)
+        both = mine[step, 1, 0].astype(f32) + side_land[step].astype(f32)
+        if step > 0:
+            side_sum[step - 1] = both.astype(jnp.bfloat16)
+            sent.append(
+                push(
+                    side_sum.at[step - 1], last_land.at[step], last_send.at[step], last_receive.at[step],
+                    across[step - 1],
+                )
+            )
+        else:
+            own_sum[0:width, :] = both
+    for index in range(2):
+        both = mine[0, index, 1].astype(f32)
+        for step in range(1, rows):
+            arrived(line_land.at[step - 1, index], line_receive.at[step - 1, index], across[-step])
+            both += line_land[step - 1, index].astype(f32)
+        if index == 0:
+            line_sum_ref[...] = both.astype(jnp.bfloat16)
+            sent.append(push(line_sum_ref, last_land.at[0], last_send.at[0], last_receive.at[0], beside))
+        else:
+            own_sum[width:, :] = both
+    for step in range(1, rows):
+        arrived(last_land.at[step], last_receive.at[step], across[-step])
+        own_sum[0:width, :] += last_land[step].astype(f32)
+    line_sum = LineSum(
+        count, 2 * width // count, lambda at: own_sum[at, :],
+        land, held, total_ref, inner_sem, outer_sem, receive_sem,
+    )
+    line_sum.begin(range(count // 2))
+    for index in range(count // 2):
+        line_sum.gather(index)
+    arrived(last_land.at[0], last_receive.at[0], beside)
+    own_sum[width:, :] += last_land[0].astype(f32)
+    line_sum.begin(range(count // 2, count))
+    for index in range(count // 2, count):
+        line_sum.gather(index)
+        line_sum.spread(index - count // 2)
+    for peer in peers:
+        arrived(tile_land.at[peer], bias_receive.at[peer], {"seq": peer})
+    tile = tile_land[0]
+    for source in range(1, size):
+        tile += tile_land[source]
+    tile_line[place] = tile
+    for index, plane in enumerate(planes):
+        sent.append(
+            push(tile_line.at[place], tile_line.at[place], plane_send.at[index], plane_receive.at[place], {"batch": plane})
+        )
+    for plane in planes:
+        arrived(tile_line.at[plane], plane_receive.at[plane], {"batch": plane})
+    tile = tile_line[0]
+    for source in range(1, lax.axis_size("batch")):
+        tile += tile_line[source]
+    bias_out[...] = tile
+    squares = tile * tile
+    for index in range(count // 2, count):
+        line_sum.spread(index)
+    for row in range(0, 2 * width, 16):
+        value = total_ref[row : row + 16, :].astype(f32)
+        value = value * value
+        for begin in range(0, value.shape[1], LANES):
+            squares += value[:8, begin : begin + LANES] + value[8:, begin : begin + LANES]
+    head = jnp.sum(squares, axis=0, keepdims=True)
+    line8 = lax.broadcasted_iota(jnp.int32, (8, LANES), 0)
+    tile_out[...] = jnp.where(line8 == 0, head, note_ref[...])
+    note_out[spot] = tile_out[...]
+    for index, peer in enumerate(peers):
+        sent.append(
+            push(tile_out, note_out.at[spot], note_send.at[index], note_receive.at[spot], {"seq": peer})
+        )
+    for peer in peers:
+        arrived(note_out.at[peer], note_receive.at[peer], {"seq": peer})
+    for copy in sent:
+        copy.wait_send()
+    line_sum.finish()
+
+
+def reduce_gradients(grad, bias, note):
+    size = lax.axis_size("seq")
+    lines = lax.axis_size("batch")
+    _, _, width, depth = grad.shape
+    rows = size // 4
+    count = 4
+    bf16 = jnp.bfloat16
+    vmem = pl.BlockSpec(memory_space=pltpu.VMEM)
+    dma = pltpu.SemaphoreType.DMA
+    near = max(rows - 1, 1)
+    return pl.pallas_call(
+        functools.partial(reduce_kernel, count),
+        in_specs=[pl.BlockSpec(memory_space=pl.ANY), vmem, vmem],
+        out_specs=[vmem, vmem, vmem],
+        out_shape=[
+            jax.ShapeDtypeStruct((2 * width, depth), bf16),
+            jax.ShapeDtypeStruct(bias.shape[1:], jnp.float32),
+            jax.ShapeDtypeStruct((size,) + note.shape, jnp.float32),
+        ],
+        scratch_shapes=[
+            pltpu.VMEM((rows, 2, 2, width, depth), bf16),
+            pltpu.VMEM((rows, 2, 2, width, depth), bf16),
+            pltpu.VMEM((rows, width, depth), bf16),
+            pltpu.VMEM((near, 2, width, depth), bf16),
+            pltpu.VMEM((near, width, depth), bf16),
+            pltpu.VMEM((width, depth), bf16),
+            pltpu.VMEM((rows, width, depth), bf16),
+            pltpu.VMEM((2 * width, depth), jnp.float32),
+        ] + LineSum.scratch(count, 2 * width, depth) + [
+            pltpu.VMEM((size,) + bias.shape[1:], jnp.float32),
+            pltpu.VMEM((lines,) + bias.shape[1:], jnp.float32),
+            pltpu.VMEM(note.shape, jnp.float32),
+            dma((rows, 2)),
+            dma((rows, 2)),
+            dma((rows, 2)),
+            dma((rows,)),
+            dma((rows,)),
+            dma((near, 2)),
+            dma((near, 2)),
+            dma((rows,)),
+            dma((rows,)),
+            dma((size - 1,)),
+            dma((size,)),
+            dma((lines - 1,)),
+            dma((lines,)),
+            dma((size - 1,)),
+            dma((size,)),
+        ],
+        compiler_params=pltpu.CompilerParams(
+            collective_id=6, has_side_effects=True, vmem_limit_bytes=VMEM_BYTES
+        ),
+        name="reduce_gradients",
+    )(grad, bias, note)
 
 
 def body(
@@ -371,100 +1085,83 @@
     mom1_bias,
     mom2_bias,
 ):
+    bf16 = jnp.bfloat16
+    f32 = jnp.float32
     tok_rows = token_ids.shape[1]
     width = embed_in.shape[1]
     vocab_rows = unembed.shape[0]
     n_seq = lax.axis_size("seq")
+    n_batch = lax.axis_size("batch")
     batch_index = lax.axis_index("batch")
     seq_index = lax.axis_index("seq")
-    all_ids, all_weights, all_padding = (
-        lax.all_gather(token_ids, "batch", axis=0, tiled=True),
-        lax.all_gather(pos_weights, "batch", axis=0, tiled=True),
-        lax.all_gather(pad_lengths, "batch", axis=0, tiled=True),
+    rows = n_batch * tok_rows
+    head_count = width // HEAD_DIM
+    plane_heads = head_count // n_batch
+    plane_width = plane_heads * HEAD_DIM
+    own_heads = head_count // n_seq
+    hidden_rows = w_proj.shape[0]
+
+    padding = jnp.broadcast_to(pad_lengths[:, None], (1, tok_rows))
+    tile = jnp.concatenate([token_ids, pos_weights, padding, jnp.zeros((5, tok_rows), jnp.int32)], axis=0)
+    tiles = share(tile, "batch", 0, "share_tokens")
+    flat_ids = tiles[:, 0].reshape(-1)
+    local_places = seq_index * tok_rows + jnp.arange(tok_rows, dtype=jnp.int32)
+    living = local_places[None, :] < tok_rows * n_seq - tiles[:, 2]
+    weights = jnp.where(living, tiles[:, 1], 0).astype(f32).reshape(-1)
+
+    out_w = lax.all_gather(w_out, ("seq", "batch"), axis=0, tiled=True)
+    out_w = lax.dynamic_slice_in_dim(out_w, batch_index * plane_width, plane_width, 0)
+    trans_low = lax.all_gather(trans_weight.astype(bf16), "seq", axis=1, tiled=True)
+
+    picked = lookup(flat_ids - batch_index * vocab_rows, embed_in)
+    own_rows = w_qkv.shape[0]
+    joined_cut = jnp.transpose(w_qkv.reshape(own_rows, 3, n_batch, plane_width), (2, 0, 1, 3))
+    joined_cut = joined_cut.reshape(n_batch, own_rows, 3 * plane_width)
+    fc_cut = jnp.transpose(w_fc.reshape(own_rows, n_seq, n_batch, hidden_rows), (2, 0, 1, 3))
+    fc_cut = fc_cut.reshape(n_batch, own_rows, n_seq * hidden_rows)
+    bias_tile = jnp.zeros((8, LANES), f32).at[:2, : trans_bias.shape[1]].set(trans_bias)
+    stream_low, joined_w, fc_w, proj_w, bias_all = front(picked, joined_cut, fc_cut, w_proj, bias_tile)
+    joined_w = joined_w.reshape(width, 3 * plane_width)
+    fc_w = fc_w.reshape(width, n_seq * hidden_rows)
+    proj_w = proj_w.reshape(n_seq * hidden_rows, width)
+    bias_full = jnp.transpose(bias_all[:, :2, : trans_bias.shape[1]], (1, 0, 2)).reshape(2, width)
+    stream0 = stream_low.astype(f32)
+
+    def plane_part(vector, parts, size):
+        return lax.dynamic_slice_in_dim(vector.reshape(parts, n_batch, size), batch_index, 1, 1).reshape(-1)
+
+    x_attn = normalize(stream0, norm_gains[0], layer_biases[0]).astype(bf16)
+    x_mlp = normalize(stream0, norm_gains[1], layer_biases[1]).astype(bf16)
+    joined = jnp.dot(x_attn, joined_w, preferred_element_type=f32) + plane_part(
+        wide_bias[: 3 * width], 3, plane_width
     )
-    local_places = seq_index * tok_rows + jnp.arange(tok_rows, dtype=jnp.int32)
-    living = local_places[None, :] < (tok_rows * n_seq - all_padding)[:, None]
-    weight_all = jnp.where(living, all_weights, 0).astype(jnp.float32)
-    weight_own = lax.dynamic_slice_in_dim(weight_all, batch_index, 1, 0)[0]
-    token_count = lax.psum(jnp.sum(weight_own), ("seq", "batch"))
-    flat_ids = all_ids.reshape(-1)
-    vocab_start = batch_index * vocab_rows
-    wanted = flat_ids - vocab_start
-    inside = (wanted >= 0) & (wanted < vocab_rows)
-    picked = jnp.take(embed_in, jnp.clip(wanted, 0, vocab_rows - 1), axis=0)
-    stream0 = lax.psum_scatter(
-        jnp.where(inside[:, None], picked.astype(jnp.float32), 0.0).astype(jnp.bfloat16),
-        "batch",
-        scatter_dimension=0,
-        tiled=True,
-    ).astype(jnp.float32)
-    joined_w, out_w, fc_w, proj_w = (
-        lax.all_gather(w_qkv, ("seq", "batch"), axis=0, tiled=True),
-        lax.all_gather(w_out, ("seq", "batch"), axis=0, tiled=True),
-        lax.all_gather(w_fc, ("seq", "batch"), axis=0, tiled=True),
-        lax.all_gather(w_proj, ("seq", "batch"), axis=0, tiled=True),
+    joined = joined.reshape(rows, 3, plane_heads, HEAD_DIM)
+    all_places = jnp.tile(local_places, n_batch)
+    heads = jnp.stack(
+        [rotate(joined[:, 0], all_places), rotate(joined[:, 1], all_places), joined[:, 2]]
+    ).astype(bf16)
+    spread = heads.reshape(3, n_batch, tok_rows, plane_heads // own_heads, own_heads * HEAD_DIM)
+    spread = jnp.transpose(spread, (1, 3, 0, 2, 4)).reshape(n_seq, 3, tok_rows, own_heads * HEAD_DIM)
+    mixed = attention(swap(spread, 2, "swap_heads"), own_heads)
+    attended = swap(mixed, 3, "swap_rows")
+    attended = attended.reshape(n_batch, plane_heads // own_heads, tok_rows, own_heads * HEAD_DIM)
+    attended = jnp.transpose(attended, (0, 2, 1, 3)).reshape(rows, plane_width)
+    hidden = jax.nn.gelu(
+        jnp.dot(x_mlp, fc_w, preferred_element_type=f32)
+        + plane_part(wide_bias[3 * width :], n_seq, hidden_rows),
+        approximate=False,
+    ).astype(bf16)
+    part = jnp.dot(attended, out_w, preferred_element_type=f32) + jnp.dot(
+        hidden, proj_w, preferred_element_type=f32
     )
-    trans_full, bias_full = (
-        lax.all_gather(trans_weight.astype(jnp.bfloat16), "seq", axis=1, tiled=True).astype(
-            trans_weight.dtype
-        ),
-        lax.all_gather(trans_bias.astype(jnp.bfloat16), "seq", axis=1, tiled=True).astype(
-            trans_bias.dtype
-        ),
-    )
-    head_count = width // HEAD_DIM
-    x_attn = normalize(stream0, norm_gains[0], layer_biases[0]).astype(jnp.bfloat16)
-    x_mlp = normalize(stream0, norm_gains[1], layer_biases[1]).astype(jnp.bfloat16)
-    joined = (
-        jnp.dot(x_attn, joined_w, preferred_element_type=jnp.float32) + wide_bias[: 3 * width]
-    ).reshape(tok_rows, 3, head_count, HEAD_DIM)
-    queries = rotate(joined[:, 0], local_places).astype(jnp.bfloat16)
-    key_rows = rotate(joined[:, 1], local_places).astype(jnp.bfloat16).reshape(tok_rows, width)
-    value_rows = joined[:, 2].astype(jnp.bfloat16).reshape(tok_rows, width)
-    peaks = jnp.full((head_count, tok_rows), -1e30, jnp.float32)
-    key_part = lax.all_gather(key_rows, "seq", axis=0, tiled=True).reshape(-1, head_count, HEAD_DIM)
-    value_part = lax.all_gather(value_rows, "seq", axis=0, tiled=True).reshape(
-        -1, head_count, HEAD_DIM
-    )
-    scores = jnp.einsum(
-        "qhd,khd->hqk", queries, key_part, preferred_element_type=jnp.float32
-    ) * HEAD_DIM ** (-0.5)
-    key_places = jnp.arange(key_part.shape[0], dtype=jnp.int32)
-    allowed = (key_places[None, :] <= local_places[:, None])[None]
-    scores = jnp.where(allowed, scores, -1e30)
-    new_peaks = jnp.maximum(peaks, jnp.max(scores, axis=-1))
-    exponent = jnp.where(allowed, jnp.exp(scores - new_peaks[..., None]), 0.0)
-    weighted = jnp.einsum(
-        "hqk,khd->hqd",
-        exponent.astype(jnp.bfloat16),
-        value_part,
-        preferred_element_type=jnp.float32,
-    )
-    weighted, peaks, summed = (weighted, new_peaks, jnp.sum(exponent, axis=-1))
-    attended = (
-        jnp.transpose(weighted / summed[..., None], (1, 0, 2))
-        .reshape(tok_rows, width)
-        .astype(jnp.bfloat16)
-    )
-    attn = jnp.dot(attended, out_w, preferred_element_type=jnp.float32) + layer_biases[2]
-    hidden = jax.nn.gelu(
-        jnp.dot(x_mlp, fc_w, preferred_element_type=jnp.float32) + wide_bias[3 * width :],
-        approximate=False,
-    ).astype(jnp.bfloat16)
-    stream1 = (
-        stream0
-        + attn
-        + jnp.dot(hidden, proj_w, preferred_element_type=jnp.float32)
-        + layer_biases[3]
-    )
+    stream1 = stream0 + layer_sum(part).astype(f32) + layer_biases[2] + layer_biases[3]
     gain_final = norm_gains[2]
     offset_final = layer_biases[4]
     probe_in = (stream0, stream1)
-    probe_low = (stream0.astype(jnp.bfloat16), stream1.astype(jnp.bfloat16))
-    trans_low = trans_full.astype(jnp.bfloat16)
+    probe_low = (stream_low, stream1.astype(bf16))
     translated = [
         probe_in[index]
-        + jnp.dot(probe_low[index], trans_low[index], preferred_element_type=jnp.float32)
+        + jnp.dot(probe_low[index], trans_low[index], preferred_element_type=f32)
         + bias_full[index]
         for index in range(2)
     ]
@@ -474,79 +1171,49 @@
             normalize(translated[0], gain_final, offset_final),
             normalize(translated[1], gain_final, offset_final),
         ]
-    ).astype(jnp.bfloat16)
-    gathered = lax.all_gather(states, "batch", axis=1, tiled=True)
-    all_rows = gathered.shape[1]
-
-    first, second, peaks, sums_part, cross_part = vocab_forward(gathered, unembed)
-    peak_all = peaks[-1]
-    sums_all = jnp.sum(sums_part, axis=1)
-    cross_all = jnp.sum(cross_part, axis=1)
-
-    def combine(earlier, later):
-        peak_a, sums_a, cross_a = earlier
-        peak_b, sums_b, cross_b = later
-        peak_new = jnp.maximum(peak_a, peak_b)
-        factor_a = jnp.exp(peak_a - peak_new)
-        factor_b = jnp.exp(peak_b - peak_new)
-        return (
-            peak_new,
-            sums_a * factor_a + sums_b * factor_b,
-            cross_a * factor_a[0] + cross_b * factor_b[0],
-        )
-
-    peak_all, sums_all, cross_all = merged((peak_all, sums_all, cross_all), "batch", combine)
+    ).astype(bf16)
+    first, second, peaks, sums_part, cross_part = vocab_forward(states, unembed)
+    stats = jnp.concatenate([peaks[-1], jnp.sum(sums_part, axis=1), jnp.sum(cross_part, axis=1)], axis=0)
+    gathered = share(stats, "batch", 5, "share_stats")
+    peak_all = jnp.max(gathered[:, :3], axis=0)
+    fades = jnp.exp(gathered[:, :3] - peak_all)
+    sums_all = jnp.sum(gathered[:, 3:6] * fades, axis=0)
+    cross_all = jnp.sum(gathered[:, 6:] * fades[:, :1], axis=0)
     log_totals = peak_all + jnp.log(sums_all)
     diverge = cross_all / sums_all[0] - log_totals[0] + log_totals[1:]
-    diverge_own = lax.dynamic_slice_in_dim(diverge, batch_index * tok_rows, tok_rows, 1)
-    loss_local = jnp.sum(weight_own * (diverge_own[0] + diverge_own[1]))
-    token_coef = weight_all.reshape(-1) / token_count
-    scales = token_coef[None, None, :] * jnp.exp(peaks - log_totals[None])
-    partial = vocab_backward(first, second, scales, unembed)
-    dstates = (
-        lax.psum_scatter(
-            jnp.transpose(partial, (1, 0, 2)).reshape(all_rows, 2 * width).astype(jnp.bfloat16),
-            "batch",
-            scatter_dimension=0,
-            tiled=True,
+    loss_part = jnp.sum(weights * (diverge[0] + diverge[1]))
+    scales = weights * jnp.exp(peaks - log_totals[None])
+    dstates = vocab_backward(first, second, scales, unembed)
+    grad_list = []
+    bias_list = []
+    for index in range(2):
+        delta = norm_back(translated[index], dstates[index], gain_final)
+        grad_list.append(
+            jnp.einsum("td,te->de", probe_low[index], delta.astype(bf16), preferred_element_type=f32)
         )
-        .astype(jnp.float32)
-        .reshape(tok_rows, 2, width)
+        bias_list.append(jnp.sum(delta, axis=0))
+    grad = jnp.stack(grad_list).astype(bf16).reshape(2, n_seq, width // n_seq, width)
+    bias_grad = jnp.transpose(jnp.stack(bias_list).reshape(2, n_seq, width // n_seq), (1, 0, 2))
+    bias_grad = jnp.pad(bias_grad, ((0, 0), (0, 6), (0, LANES - width // n_seq)))
+    ones = jnp.ones((LANES,), f32) / LANES
+    note = jnp.concatenate(
+        [
+            jnp.zeros((1, LANES), f32),
+            (loss_part * ones)[None],
+            (jnp.sum(weights) * ones)[None],
+            jnp.zeros((5, LANES), f32),
+        ]
     )
-    grad_w_list = []
-    grad_b_list = []
-    for index in range(2):
-        delta = norm_back(translated[index], dstates[:, index], gain_final)
-        grad_w_list.append(
-            jnp.einsum(
-                "td,te->de",
-                probe_low[index],
-                delta.astype(jnp.bfloat16),
-                preferred_element_type=jnp.float32,
-            )
-        )
-        grad_b_list.append(jnp.sum(delta, axis=0))
-    grad_w = jnp.stack(grad_w_list)
-    grad_b = jnp.stack(grad_b_list)
-    grad_w, grad_b = (
-        lax.psum(grad_w.astype(jnp.bfloat16), "batch").astype(jnp.float32),
-        lax.psum(grad_b.astype(jnp.bfloat16), "batch").astype(jnp.float32),
-    )
-    grad_w, grad_b = (
-        lax.psum_scatter(
-            grad_w.astype(jnp.bfloat16), "seq", scatter_dimension=1, tiled=True
-        ).astype(jnp.float32),
-        lax.psum_scatter(
-            grad_b.astype(jnp.bfloat16), "seq", scatter_dimension=1, tiled=True
-        ).astype(jnp.float32),
-    )
-    squares = jnp.sum(grad_w * grad_w) + jnp.sum(grad_b * grad_b)
-    first_copy = (batch_index == 0).astype(jnp.float32)
-    loss_sum, norm_square = lax.psum((loss_local, squares * first_copy), ("seq", "batch"))
-    grad_norm = jnp.sqrt(norm_square)
-    factor = jnp.minimum(1.0, clip_max / (grad_norm + 1e-06))
-    first_w, second_w, new_w = adam_update(trans_weight, grad_w * factor, mom1_weight, mom2_weight)
-    first_b, second_b, new_b = adam_update(trans_bias, grad_b * factor, mom1_bias, mom2_bias)
+    grad_sum, bias_sum, notes = reduce_gradients(grad, bias_grad, note)
+    sums = jnp.sum(notes, axis=(0, 2))
+    loss_sum = sums[1]
+    token_count = jnp.round(sums[2])
+    grad_norm = jnp.sqrt(sums[0]) / token_count
+    factor = jnp.minimum(1.0, clip_max / (grad_norm + 1e-06)) / token_count
+    grad_w = grad_sum.astype(f32).reshape(trans_weight.shape) * factor
+    grad_b = bias_sum[:2, : trans_bias.shape[1]] * factor
+    first_w, second_w, new_w = adam_update(trans_weight, grad_w, mom1_weight, mom2_weight)
+    first_b, second_b, new_b = adam_update(trans_bias, grad_b, mom1_bias, mom2_bias)
     return (loss_sum, token_count, grad_norm, first_w, second_w, new_w, first_b, second_b, new_b)
 
 

time: 909 us -> 443 us (0.49)
  waiting for transfers between devices: 523 us -> 0.74 us
  Pallas kernels: 101 us -> 342 us
  blocking collectives: 165 us -> 0 us
  local copies, waits for them, and re-layouts: 31.6 us -> 13.3 us
  matrix products: 32.4 us -> 23 us
  other arithmetic: 26.7 us -> 36 us
    all_gather x8 -> x2, waiting for transfers between devices: 363 us -> 0.04 us  [the longest x1 0.02 us: body(): out_w = lax.all_gather(w_out, ('seq', 'batch'), axis=0, tiled=True)]
    pallas_call x0 -> x9, Pallas kernels: none -> 241 us  [the longest x1 76.8 us: front(): pl.pallas_call(functools.partial(front_kernel, count), in_specs=[vmem, an...]
    psum x3 -> x0, blocking collectives: 87.7 us -> none  [the longest x1 38.9 us: body(): token_count = lax.psum(jnp.sum(weight_own), ('seq', 'batch'))]
    unnamed x15 -> x2, waiting for transfers between devices: 84 us -> 0.7 us
    reduce_scatter x2 -> x0, waiting for transfers between devices: 76.1 us -> none  [the longest x1 49.6 us: body(): lax.psum_scatter(grad_w.astype(jnp.bfloat16), 'seq', scatter_dimension=1,...]
    all_gather x6 -> x0, blocking collectives: 71 us -> none  [the longest x3 39.3 us: merged(): gathered = jax.tree.map(lambda a: lax.all_gather(a, axis), part)]
    gather x1 -> x0, local copies, waits for them, and re-layouts: 14.4 us -> none  [body(): picked = jnp.take(embed_in, jnp.clip(wanted, 0, vocab_rows - 1), axis=0)]
    unnamed x39 -> x41, local copies, waits for them, and re-layouts: 12.3 us -> 2.02 us
  transfers between devices with their start and end apart: 13 -> 2, of which waited for: 12 -> 0; matrix products, arithmetic and copies ran while one was open for 4% -> 8% of each run, Pallas kernels for 0% -> 40%
where the time goes in v3:
time: 443 us; the launch traced here: 436 us
  Pallas kernels  342 us (77%)
  other arithmetic  36 us (8%)
  matrix products  23 us (5%)
  between operations  20.8 us (5%)
  local copies, waits for them, and re-layouts  13.3 us (3%)
    pallas_call x1, Pallas kernels, front(): pl.pallas_call(functools.partial(front_kernel, count), in_specs=[vmem, an...  76.8 us
    pallas_call x1, Pallas kernels, vocab_forward(): pl.pallas_call(functools.partial(forward_kernel, vocab), grid=(tiles + 1,...  65.3 us
    pallas_call x1, Pallas kernels, reduce_gradients(): pl.pallas_call(functools.partial(reduce_kernel, count), in_specs=[pl.Bloc...  58.1 us
    pallas_call x1, Pallas kernels, layer_sum(): pl.pallas_call(functools.partial(layer_sum_kernel, count), in_specs=[vmem...  37.9 us
    pallas_call x1, Pallas kernels, vocab_backward(): pl.pallas_call(functools.partial(backward_kernel, vocab), grid=(tiles + 1...  36 us
    pallas_call x1, Pallas kernels, lookup(): pl.pallas_call(lookup_kernel, in_specs=[pl.BlockSpec(memory_space=pltpu.S...  25.8 us
    pallas_call x2, Pallas kernels, swap(): pl.pallas_call(swap_kernel, in_specs=[space], out_specs=space, out_shape=...  21.7 us
    pallas_call x2, Pallas kernels, share(): pl.pallas_call(functools.partial(share_kernel, axis), in_specs=[space], o...  15.5 us
  transfers between devices with their start and end apart: 2, of which 0 were waited for; matrix products, arithmetic and copies ran while one was open for 8% of the time, Pallas kernels for 40%

profile of v3, /device:TPU:0, one launch (start us, length us, event | category | flops | bytes accessed | tf_op | source)
XLA Modules:
  0.0 436.1 jit_solution(13081716562664588639)
XLA Ops:
  8.0 2.1 convert_element_type.63
  11.6 8.6 %share_tokens.1 = s32[4,8,128]{2,1,0:T(8,128)} custom-call(s32[8,128]{1,0:T(8,128)} %add_add_fusion.1.tile_ref), custom_call_target="tpu_custom_call" | custom-call | tf_op jit(solution)/shard_map/share_tokens/pallas_call | solution.py:508
  22.5 1.4 fusion.88
  23.9 25.8 %lookup.1.picked_ref = bf16[512,1024]{1,0:T(8,128)(2,1)} custom-call(s32[512]{0:T(512)} %bitcast.164, bf16[12576,1024]{1,0:T(8,128)(2,1)} %table_ref.3), custom_call_target="tpu_custom_call" | custom-call | tf_op jit(solution)/shard_map/lookup/pallas_call | solution.py:602
  50.3 76.8 %front.1 = (bf16[512,1024]{1,0:T(8,128)(2,1)}, bf16[8,4,32,768]{3,2,1,0:T(8,128)(2,1)}, bf16[8,4,32,1024]{3,2,1,0:T(8,128)(2,1)}, bf16[8,128,1024]{2,1,0:T(8,128)(2,1)}, f32[8,8,128]{2,1,0:T(8,128)}) custom-call(bf16[512,1024]{1,0:T(8,128)(2,1)} %lookup.1.picked_ref, bf16[4,32,768]{2,1,0:T(8,128)(2,1)} %reshape.319.joined_ref, ...), custom_call_target="tpu_custom_call" | custom-call | tf_op jit(solution)/shard_map/front/pallas_call | solution.py:768
  127.1 1.5 convert_reduce_fusion
  128.6 1.6 fusion.8
  130.3 3.8 convolution_add_fusion.1
  134.1 1.9 copy.32
  137.3 1.4 copy.33
  138.8 12.6 %swap_heads.1.in_ref = bf16[8,3,128,128]{3,2,1,0:T(8,128)(2,1)} custom-call(bf16[8,3,128,128]{3,2,1,0:T(8,128)(2,1)} %bitcast.135), custom_call_target="tpu_custom_call" | custom-call | tf_op jit(solution)/shard_map/swap_heads/pallas_call | solution.py:543
  151.4 5.1 %attention.1.send_ref = bf16[8,128,128]{2,1,0:T(8,128)(2,1)} custom-call(bf16[8,3,128,128]{3,2,1,0:T(8,128)(2,1)} %swap_heads.1.in_ref), custom_call_target="tpu_custom_call" | custom-call | tf_op jit(solution)/shard_map/attention/pallas_call | solution.py:861
  156.5 9.1 %swap_rows.1 = bf16[8,128,128]{2,1,0:T(8,128)(2,1)} custom-call(bf16[8,128,128]{2,1,0:T(8,128)(2,1)} %attention.1.send_ref), custom_call_target="tpu_custom_call" | custom-call | tf_op jit(solution)/shard_map/swap_rows/pallas_call | solution.py:543
  167.6 8.6 %fusion.28 = f32[512,1024]{1,0:T(8,128)S(1)} fusion(bf16[1024,1024]{1,0:T(8,128)(2,1)} %bitcast.173, bf16[1024,1024]{1,0:T(8,128)(2,1)} %bitcast.172, bf16[512,1024]{1,0:T(8,128)(2,1)S(1)} %copy-done.2, f32[1024]{0:T(1024)S(1)} %bitcast.167, f32[1024]{0:T(1024)S(1)} %bitcast.165, f32[1024]{0:T(1024)S(1)} %bitcast.168, f32[512]{0:T(512)S(1)} %add_rsqrt_fusion.3, ...), kind=kOutput, calls=%fused_computation.65 | convolution fusion | flops 2185232384 | bytes 7356416 | tf_op jit(solution)/shard_map/dot_general | solution.py:1154
  176.3 2.8 convolution_add_fusion.part_ref
  179.1 37.9 %layer_sum.1 = bf16[512,1024]{1,0:T(8,128)(2,1)} custom-call(f32[512,1024]{1,0:T(8,128)} %convolution_add_fusion.part_ref), custom_call_target="tpu_custom_call" | custom-call | tf_op jit(solution)/shard_map/layer_sum/pallas_call | solution.py:814
  217.0 1.8 fusion.82
  219.5 3.8 fusion.133
  223.7 1.4 fusion.132
  225.4 1.6 copy-done.4
  227.1 1.8 fusion.30
  228.8 2.0 pad_maximum_fusion.1.states_ref
  230.9 65.3 %vocab_forward.1 = (bf16[10,3,1280,256]{3,2,1,0:T(8,128)(2,1)}, bf16[10,3,1280,256]{3,2,1,0:T(8,128)(2,1)}, f32[10,3,512]{2,1,0:T(4,128)}, f32[3,8,512]{2,1,0:T(8,128)}, f32[2,8,512]{2,1,0:T(8,128)}) custom-call(bf16[3,512,1024]{2,1,0:T(8,128)(2,1)} %pad_maximum_fusion.1.states_ref, bf16[12576,1024]{1,0:T(8,128)(2,1)} %table_ref.5), custom_call_target="tpu_custom_call" | custom-call | flops 39560675328 | bytes 64389120 | tf_op jit(solution)/shard_map/vocab_forward/pallas_call | solution.py:204
  299.1 6.9 %share_stats.1 = f32[4,8,512]{2,1,0:T(8,128)} custom-call(f32[8,512]{1,0:T(8,128)} %pad_maximum_fusion.4.tile_ref), custom_call_target="tpu_custom_call" | custom-call | tf_op jit(solution)/shard_map/share_stats/pallas_call | solution.py:508
  310.7 1.6 exponential_multiply_fusion.scales_ref
  312.3 36.0 %vocab_backward.1 = f32[2,512,1024]{2,1,0:T(8,128)} custom-call(bf16[10,3,1280,256]{3,2,1,0:T(8,128)(2,1)} %get-tuple-element.39.first_ref, bf16[10,3,1280,256]{3,2,1,0:T(8,128)(2,1)} %get-tuple-element.40.second_ref, f32[10,3,512]{2,1,0:T(4,128)} %exponential_multiply_fusion.scales_ref, bf16[12576,1024]{1,0:T(8,128)(2,1)} %table_ref.5), custom_call_target="tpu_custom_call" | custom-call | flops 26373783552 | bytes 64389120 | tf_op jit(solution)/shard_map/vocab_backward/pallas_call | solution.py:317
  348.3 4.3 fusion.26
  352.9 1.5 fusion.126
  356.4 1.3 convolution_convert_fusion
  357.8 2.3 pad_maximum_fusion.grad_ref
  360.8 58.1 %reduce_gradients.1 = (bf16[256,1024]{1,0:T(8,128)(2,1)}, f32[8,128]{1,0:T(8,128)}, f32[8,8,128]{2,1,0:T(8,128)}) custom-call(bf16[2,8,128,1024]{3,2,1,0:T(8,128)(2,1)} %pad_maximum_fusion.grad_ref, f32[8,8,128]{2,1,0:T(8,128)} %pad.7.bias_ref, f32[8,128]{1,0:T(8,128)} %broadcast.230.note_ref), custom_call_target="tpu_custom_call" | custom-call | tf_op jit(solution)/shard_map/reduce_gradients/pallas_call | solution.py:1023
  424.4 2.2 multiply_subtract_fusion
  (123 shorter events, 22.4 us)
Async XLA Ops:
  7.2 3.8 copy-start.18
  7.2 3.7 copy-start.17
  7.2 13.0 %copy-start.10 = (bf16[32,4096]{1,0:T(8,128)(2,1)S(1)}, bf16[32,4096]{1,0:T(8,128)(2,1)}, u32[]{:S(2)}) copy-start(bf16[32,4096]{1,0:T(8,128)(2,1)} %param.26) | copy-start | bytes 786436
  7.2 14.0 %copy-start.11 = (bf16[32,3072]{1,0:T(8,128)(2,1)S(1)}, bf16[32,3072]{1,0:T(8,128)(2,1)}, u32[]{:S(2)}) copy-start(bf16[32,3072]{1,0:T(8,128)(2,1)} %param.24) | copy-start | bytes 589828
  7.2 169.0 %all-gather.3.cloned.1.call-start = ((), (), s32[]{:S(2)}) async-start(), calls=%async_computation | async-start | bytes 2162688 | tf_op jit(solution)/shard_map/all_gather | solution.py:1112
  8.0 211.5 %all-gather.5.cloned.1.call-start = ((), (), s32[]{:S(2)}) async-start(), calls=%async_computation.1 | async-start | bytes 4718592 | tf_op jit(solution)/shard_map/all_gather | solution.py:1114
  10.1 12.3 %slice-start = ((f32[7168]{0:T(1024)}), f32[3072]{0:T(1024)S(1)}, s32[]{:S(2)}) async-start(f32[7168]{0:T(1024)} %param.30), calls=%async_computation.2 | async-start | bytes 24576 | tf_op jit(solution)/shard_map/slice | solution.py:1136
  23.9 25.8 %copy-start.14 = (f32[2,128]{1,0:T(2,128)S(1)}, f32[2,128]{1,0:T(2,128)}, u32[]{:S(2)}) copy-start(f32[2,128]{1,0:T(2,128)} %param.33) | copy-start | bytes 3076
  49.7 80.6 %copy-start.13 = (f32[3,1024]{1,0:T(4,128)S(1)}, f32[3,1024]{1,0:T(4,128)}, u32[]{:S(2)}) copy-start(f32[3,1024]{1,0:T(4,128)} %param.28) | copy-start | bytes 36868
  49.7 80.6 %copy-start.12 = (f32[5,1024]{1,0:T(8,128)S(1)}, f32[5,1024]{1,0:T(8,128)}, u32[]{:S(2)}) copy-start(f32[5,1024]{1,0:T(8,128)} %param.29) | copy-start | bytes 61444
  127.1 3.3 copy-start.2
  138.8 28.0 %slice-start.1 = ((f32[7168]{0:T(1024)}), f32[4096]{0:T(1024)S(1)}, s32[]{:S(2)}) async-start(f32[7168]{0:T(1024)} %param.30), calls=%async_computation.3 | async-start | bytes 32768 | tf_op jit(solution)/shard_map/slice | solution.py:1151
  217.0 1.8 copy-start.3
  219.5 4.2 copy-start.19
  225.1 3.8 copy-start
  225.1 2.0 copy-start.4
  348.2 4.4 copy-start.1
  348.3 4.7 %copy-start.6 = (f32[2,512,1024]{2,1,0:T(8,128)S(1)}, f32[2,512,1024]{2,1,0:T(8,128)}, u32[]{:S(2)}) copy-start(f32[2,512,1024]{2,1,0:T(8,128)} %vocab_backward.1) | copy-start | bytes 12582916
  355.1 1.3 copy-start.5
  360.8 62.3 %copy-start.15 = (f32[2,128]{1,0:T(2,128)S(1)}, f32[2,128]{1,0:T(2,128)}, u32[]{:S(2)}) copy-start(f32[2,128]{1,0:T(2,128)} %param.37) | copy-start | bytes 3076
  360.8 62.3 %copy-start.16 = (f32[2,128]{1,0:T(2,128)S(1)}, f32[2,128]{1,0:T(2,128)}, u32[]{:S(2)}) copy-start(f32[2,128]{1,0:T(2,128)} %param.36) | copy-start | bytes 3076
  360.8 63.5 %copy-start.7 = (f32[2,128,1024]{2,1,0:T(8,128)S(1)}, f32[2,128,1024]{2,1,0:T(8,128)}, u32[]{:S(2)}) copy-start(f32[2,128,1024]{2,1,0:T(8,128)} %param.32) | copy-start | bytes 3145732
  360.8 63.6 %copy-start.8 = (f32[2,128,1024]{2,1,0:T(8,128)S(1)}, f32[2,128,1024]{2,1,0:T(8,128)}, u32[]{:S(2)}) copy-start(f32[2,128,1024]{2,1,0:T(8,128)} %param.35) | copy-start | bytes 3145732
  360.8 63.5 %copy-start.9 = (f32[2,128,1024]{2,1,0:T(8,128)S(1)}, f32[2,128,1024]{2,1,0:T(8,128)}, u32[]{:S(2)}) copy-start(f32[2,128,1024]{2,1,0:T(8,128)} %param.34) | copy-start | bytes 3145732
Sparse Core Ops, SparseCore 0:
  11.0 60.2 all-gather.2
  73.7 45.1 all-gather.4

commit v4 on v3

--- a/solution.py
+++ b/solution.py
@@ -23,13 +23,6 @@
 learn_rate = 0.03
 decay_rate = 0.01
 adam_eps = 1e-08
-
-
-def normalize(values, gain_row, offset_row):
-    average = jnp.mean(values, axis=-1, keepdims=True)
-    centered = values - average
-    variance = jnp.mean(centered * centered, axis=-1, keepdims=True)
-    return centered * lax.rsqrt(variance + norm_eps) * gain_row + offset_row
 
 
 def norm_back(values, upstream, gain_row):
@@ -44,24 +37,6 @@
         - jnp.mean(scaled, axis=-1, keepdims=True)
         - unit * jnp.mean(scaled * unit, axis=-1, keepdims=True)
     ) * inverse
-
-
-def rotate(vectors, places):
-    half_rot = ROT // 2
-    frequency = 10000.0 ** (-2.0 * jnp.arange(half_rot, dtype=jnp.float32) / ROT)
-    angles = places.astype(jnp.float32)[:, None] * frequency[None, :]
-    cosine = jnp.cos(angles)[:, None, :]
-    sine = jnp.sin(angles)[:, None, :]
-    lower_part = vectors[..., :half_rot]
-    upper_part = vectors[..., half_rot:ROT]
-    return jnp.concatenate(
-        [
-            lower_part * cosine - upper_part * sine,
-            upper_part * cosine + lower_part * sine,
-            vectors[..., ROT:],
-        ],
-        axis=-1,
-    )
 
 
 def adam_update(weight, gradient, earlier, later):
@@ -520,106 +495,13 @@
     )(tile)
 
 
-def swap_kernel(send_ref, out_ref, local_sem, send_sem, receive_sem):
-    place = lax.axis_index("seq")
-    peers = others("seq")
-    local = pltpu.make_async_copy(send_ref.at[place], out_ref.at[place], local_sem)
-    local.start()
-    greet([{"seq": peer} for peer in peers])
-    copies = [
-        push(send_ref.at[peer], out_ref.at[place], send_sem.at[index], receive_sem.at[place], {"seq": peer})
-        for index, peer in enumerate(peers)
-    ]
-    for peer in peers:
-        arrived(out_ref.at[peer], receive_sem.at[peer], {"seq": peer})
-    for copy in copies:
-        copy.wait_send()
-    local.wait()
-
-
-def swap(blocks, identity, name):
-    size = lax.axis_size("seq")
-    space = pl.BlockSpec(memory_space=pltpu.VMEM)
-    return pl.pallas_call(
-        swap_kernel,
-        in_specs=[space],
-        out_specs=space,
-        out_shape=jax.ShapeDtypeStruct(blocks.shape, blocks.dtype),
-        scratch_shapes=[
-            pltpu.SemaphoreType.DMA,
-            pltpu.SemaphoreType.DMA((size - 1,)),
-            pltpu.SemaphoreType.DMA((size,)),
-        ],
-        compiler_params=pltpu.CompilerParams(
-            collective_id=identity, has_side_effects=True, vmem_limit_bytes=VMEM_BYTES
-        ),
-        name=name,
-    )(blocks)
-
-
-def lookup_kernel(ids_ref, table_ref, out_ref, window, rows_f32, sems):
-    rows, depth = out_ref.shape
-    vocab = table_ref.shape[0]
-    ring = window.shape[0]
-    group = window.shape[1]
-    rows_f32[...] = jnp.zeros_like(rows_f32)
-    line = lax.broadcasted_iota(jnp.int32, (group, depth), 0)
-
-    def fetch(index, slot):
-        base = pl.multiple_of(ids_ref[index] // group * group, group)
-        return pltpu.make_async_copy(table_ref.at[pl.ds(base, group)], window.at[slot], sems.at[slot])
-
-    def inside(index):
-        value = ids_ref[index]
-        return (value >= 0) & (value < vocab)
-
-    def loop(index, carry):
-        slot = lax.rem(index, ring)
-        late = jnp.maximum(index - ring, 0)
-
-        @pl.when((index >= ring) & inside(late))
-        def _():
-            fetch(late, slot).wait()
-            place = lax.rem(ids_ref[late], group)
-            block = window[slot].astype(jnp.float32)
-            rows_f32[pl.ds(late, 1), :] = jnp.sum(jnp.where(line == place, block, 0.0), axis=0, keepdims=True)
-
-        now = jnp.minimum(index, rows - 1)
-
-        @pl.when((index < rows) & inside(now))
-        def _():
-            fetch(now, slot).start()
-
-        return carry
-
-    lax.fori_loop(0, rows + ring, loop, 0)
-    out_ref[...] = rows_f32[...].astype(jnp.bfloat16)
-
-
-def lookup(ids, table):
-    rows = ids.shape[0]
-    depth = table.shape[1]
-    return pl.pallas_call(
-        lookup_kernel,
-        in_specs=[pl.BlockSpec(memory_space=pltpu.SMEM), pl.BlockSpec(memory_space=pl.ANY)],
-        out_specs=pl.BlockSpec(memory_space=pltpu.VMEM),
-        out_shape=jax.ShapeDtypeStruct((rows, depth), jnp.bfloat16),
-        scratch_shapes=[
-            pltpu.VMEM((64, 16, depth), jnp.bfloat16),
-            pltpu.VMEM((rows, depth), jnp.float32),
-            pltpu.SemaphoreType.DMA((64,)),
-        ],
-        compiler_params=pltpu.CompilerParams(vmem_limit_bytes=VMEM_BYTES),
-        name="lookup",
-    )(ids, table)
-
-
 def front_kernel(
     count,
-    picked_ref, joined_ref, fc_ref, proj_ref, bias_ref,
-    stream_ref, joined_out, fc_out, proj_out, bias_out,
+    tile_ref, table_ref, joined_ref, fc_ref, proj_ref, out_ref, trans_ref, bias_ref,
+    tiles_out, stream_ref, joined_out, fc_out, proj_out, out_out, trans_out, bias_out,
+    table, column_ids, chosen, picked, trans_low,
     land, held, inner_sem, outer_sem, receive_sem,
-    local_sem, cross_send, cross_receive, plane_send, plane_receive, bias_send, bias_receive,
+    local_sem, table_sem, tile_send, tile_receive, cross_send, cross_receive, plane_send, plane_receive, bias_send, bias_receive,
 ):
     lines = lax.axis_size("batch")
     place = lax.axis_index("batch")
@@ -633,13 +515,22 @@
     corners = [plane_index(core, 1 - column, lax.rem(line + step, rows)) for step in range(1, rows)]
     planes = others("batch")
     peers = others("seq")
-    outs = (joined_out, fc_out, proj_out)
-    proj_rows = proj_ref.shape[0]
+    outs = (joined_out, fc_out, proj_out, out_out, trans_out)
+    total_rows, depth = stream_ref.shape
+    chunk = total_rows // count
+    tokens = tile_ref.shape[1]
+    vocab = table_ref.shape[0]
+    number = spot * lines + place
+    goal = {"seq": lax.rem(number, size), "batch": number // size}
+    wanted = place * size + spot
+    origin = {"seq": wanted // lines, "batch": lax.rem(wanted, lines)}
+    stays = number == wanted
 
     def piece(array, half, slot):
+        out = outs[array]
         if array < 2:
-            return outs[array].at[slot, pl.ds(half * (lines // 2), lines // 2)]
-        return outs[array].at[slot, pl.ds(half * (proj_rows // 2), proj_rows // 2)]
+            return out.at[slot, pl.ds(half * (lines // 2), lines // 2)]
+        return out.at[slot, :, pl.ds(half * (depth // 2), depth // 2)]
 
     started = []
 
@@ -687,101 +578,216 @@
                 for half in range(2):
                     await_piece(array, half, source)
 
-    proj_copy = pltpu.make_async_copy(proj_ref, proj_out.at[spot], local_sem.at[0])
-    proj_copy.start()
+    width = chosen.shape[1]
+    cuts = table.shape[0] // width
+    table_copies = [
+        pltpu.make_async_copy(
+            table_ref.at[pl.ds(cut * width, min(width, vocab - cut * width))],
+            table.at[pl.ds(cut * width, min(width, vocab - cut * width))],
+            table_sem.at[cut],
+        )
+        for cut in range(cuts)
+    ]
+    for copy in table_copies:
+        copy.start()
+    if table.shape[0] > vocab:
+        table[vocab:, :] = jnp.zeros((table.shape[0] - vocab, depth), table.dtype)
+    trans_low[...] = trans_ref[...].astype(jnp.bfloat16)
     locals_ = [
-        pltpu.make_async_copy(source.at[place], out.at[spot, place], local_sem.at[1 + index])
-        for index, (source, out) in enumerate(((joined_ref, joined_out), (fc_ref, fc_out)))
+        pltpu.make_async_copy(source, target, local_sem.at[index])
+        for index, (source, target) in enumerate(
+            (
+                (proj_ref, proj_out.at[spot]),
+                (trans_low, trans_out.at[spot]),
+                (joined_ref.at[place], joined_out.at[spot, place]),
+                (fc_ref.at[place], fc_out.at[spot, place]),
+                (tile_ref, tiles_out.at[place]),
+                (bias_ref, bias_out.at[spot]),
+            )
+        )
     ]
     for copy in locals_:
         copy.start()
-    bias_copy = pltpu.make_async_copy(bias_ref, bias_out.at[spot], local_sem.at[3])
-    bias_copy.start()
-    greet([{"batch": plane} for plane in planes] + [{"seq": peer} for peer in peers])
-    line_sum = LineSum(
-        count, stream_ref.shape[0] // count, lambda at: picked_ref[at, :],
-        land, held, stream_ref, inner_sem, outer_sem, receive_sem,
-    )
-    line_sum.begin(range(count))
+    out_copy = pltpu.make_async_copy(out_ref, out_out.at[spot], local_sem.at[6])
+
+    @pl.when(stays)
+    def _():
+        out_copy.start()
+
+    barrier = pltpu.get_barrier_semaphore()
+    for partner in [{"batch": plane} for plane in planes] + [{"seq": peer} for peer in peers]:
+        pl.semaphore_signal(barrier, inc=1, device_id=partner, device_id_type=pl.DeviceIdType.MESH)
+
+    @pl.when(jnp.logical_not(stays))
+    def _():
+        pl.semaphore_signal(barrier, inc=1, device_id=origin, device_id_type=pl.DeviceIdType.MESH)
+
+    pl.semaphore_wait(barrier, jnp.where(stays, 0, 1) + len(planes) + len(peers))
+
+    tile_copies = [
+        push(tile_ref, tiles_out.at[place], tile_send.at[index], tile_receive.at[place], {"batch": plane})
+        for index, plane in enumerate(planes)
+    ]
+    for copy in locals_[:2]:
+        copy.wait()
+    own(2)
     crossing = []
     for array, source, out in ((0, joined_ref, joined_out), (1, fc_ref, fc_out)):
         for index, plane in enumerate(planes):
             crossing.append(
                 push(source.at[plane], out.at[spot, place], cross_send.at[array, index], cross_receive.at[array, place], {"batch": plane})
             )
+    out_push = pltpu.make_async_remote_copy(
+        src_ref=out_ref, dst_ref=out_out.at[goal["seq"]], send_sem=cross_send.at[2, 0],
+        recv_sem=cross_receive.at[2, 0], device_id=goal, device_id_type=pl.DeviceIdType.MESH,
+    )
+
+    @pl.when(jnp.logical_not(stays))
+    def _():
+        out_push.start()
+
+    own(4)
     bias_copies = [
         push(bias_ref, bias_out.at[spot], bias_send.at[index], bias_receive.at[spot], {"seq": peer})
         for index, peer in enumerate(peers)
     ]
-    proj_copy.wait()
-    own(2)
-    for copy in locals_:
+    for copy in locals_[2:]:
         copy.wait()
-
-    def receive_cross(array):
+    for plane in planes:
+        arrived(tiles_out.at[plane], tile_receive.at[plane], {"batch": plane})
+    for sequence in range(lines):
+        turned = jnp.transpose(tiles_out[sequence].astype(jnp.float32))
+        column_ids[sequence * tokens : (sequence + 1) * tokens, :] = jnp.broadcast_to(
+            turned[:, 0:1] - (place * vocab).astype(jnp.float32), (tokens, LANES)
+        )
+    half = total_rows // 2
+    lane = lax.broadcasted_iota(jnp.int32, (half, LANES), 1)
+
+    def look(part):
+        at = slice(part * half, (part + 1) * half)
+        for cut in range(cuts):
+            if part == 0:
+                table_copies[cut].wait()
+            for block in range(width // LANES):
+                number_ = (lane + (cut * width + block * LANES)).astype(jnp.float32)
+                chosen[:, block * LANES : (block + 1) * LANES] = jnp.where(
+                    column_ids[at, :] == number_, 1.0, 0.0
+                ).astype(jnp.bfloat16)
+            found = jnp.dot(
+                chosen[...], table[cut * width : (cut + 1) * width, :], preferred_element_type=jnp.float32
+            )
+            if cut == 0:
+                picked[at, :] = found
+            else:
+                picked[at, :] += found
+
+    line_sum = LineSum(
+        count, chunk, lambda at: picked[at, :],
+        land, held, stream_ref, inner_sem, outer_sem, receive_sem,
+    )
+
+    def turn(array):
         for plane in planes:
             arrived(outs[array].at[spot, plane], cross_receive.at[array, plane], {"batch": plane})
-
-    def turn(array):
-        receive_cross(array)
         own(array)
 
+    def turn_out():
+        @pl.when(stays)
+        def _():
+            out_copy.wait()
+
+        @pl.when(jnp.logical_not(stays))
+        def _():
+            arrived(out_out.at[spot], cross_receive.at[2, 0], origin)
+
+        own(3)
+
     todo = [
+        lambda: relay_side(2),
         lambda: turn(0),
-        lambda: relay_side(2),
+        turn_out,
+        lambda: relay_side(4),
         lambda: turn(1),
         lambda: relay_core(2),
         lambda: relay_side(0),
+        lambda: relay_side(3),
+        lambda: relay_core(4),
         lambda: relay_core(0),
         lambda: relay_side(1),
+        lambda: relay_core(3),
         lambda: relay_core(1),
         lambda: receive_core(2),
+        lambda: receive_core(4),
         lambda: receive_core(0),
+        lambda: receive_core(3),
         lambda: receive_core(1),
     ]
+    for part in range(2):
+        look(part)
+        line_sum.begin(range(part * count // 2, (part + 1) * count // 2))
+        todo.pop(0)()
     for index in range(count + 1):
         if index < count:
             line_sum.gather(index)
         if index >= 1:
             line_sum.spread(index - 1)
-        if todo:
+        if todo and index % 2:
             todo.pop(0)()
     for work in todo:
         work()
     for peer in peers:
         arrived(bias_out.at[peer], bias_receive.at[peer], {"seq": peer})
-    bias_copy.wait()
-    for copy in started + crossing + bias_copies:
+    for copy in started + crossing + bias_copies + tile_copies:
         copy.wait_send()
+
+    @pl.when(jnp.logical_not(stays))
+    def _():
+        out_push.wait_send()
+
     line_sum.finish()
 
 
-def front(picked, joined, fc, proj, bias):
+def front(tile, table, joined, fc, proj, out, trans, bias):
     size = lax.axis_size("seq")
     lines = lax.axis_size("batch")
-    rows, depth = picked.shape
-    count = 8
+    vocab, depth = table.shape
+    rows = lines * tile.shape[1]
+    count = 16
     vmem = pl.BlockSpec(memory_space=pltpu.VMEM)
     anywhere = pl.BlockSpec(memory_space=pl.ANY)
     dma = pltpu.SemaphoreType.DMA
     chips = size // 2
+    bf16 = jnp.bfloat16
+    spread = lambda part, kind: jax.ShapeDtypeStruct((size,) + part.shape, kind)
     return pl.pallas_call(
         functools.partial(front_kernel, count),
-        in_specs=[vmem, anywhere, anywhere, anywhere, vmem],
-        out_specs=[vmem, anywhere, anywhere, anywhere, vmem],
+        in_specs=[vmem, anywhere, anywhere, anywhere, anywhere, anywhere, vmem, vmem],
+        out_specs=[vmem, vmem, anywhere, anywhere, anywhere, anywhere, anywhere, vmem],
         out_shape=[
-            jax.ShapeDtypeStruct((rows, depth), jnp.bfloat16),
-            jax.ShapeDtypeStruct((size,) + joined.shape, jnp.bfloat16),
-            jax.ShapeDtypeStruct((size,) + fc.shape, jnp.bfloat16),
-            jax.ShapeDtypeStruct((size,) + proj.shape, jnp.bfloat16),
-            jax.ShapeDtypeStruct((size,) + bias.shape, jnp.float32),
+            jax.ShapeDtypeStruct((lines,) + tile.shape, tile.dtype),
+            jax.ShapeDtypeStruct((rows, depth), bf16),
+            spread(joined, bf16),
+            spread(fc, bf16),
+            spread(proj, bf16),
+            spread(out, bf16),
+            spread(trans, bf16),
+            spread(bias, jnp.float32),
         ],
-        scratch_shapes=LineSum.scratch(count, rows, depth) + [
-            dma((4,)),
-            dma((2, lines - 1)),
-            dma((2, lines)),
-            dma((3, 2, size // 4 + 1, chips + 1)),
-            dma((3, 2, size)),
+        scratch_shapes=[
+            pltpu.VMEM((pl.cdiv(vocab, VOCAB_TILE) * VOCAB_TILE, depth), bf16),
+            pltpu.VMEM((rows, LANES), jnp.float32),
+            pltpu.VMEM((rows // 2, VOCAB_TILE), bf16),
+            pltpu.VMEM((rows, depth), jnp.float32),
+            pltpu.VMEM(trans.shape, bf16),
+        ] + LineSum.scratch(count, rows, depth) + [
+            dma((7,)),
+            dma((pl.cdiv(vocab, VOCAB_TILE),)),
+            dma((lines - 1,)),
+            dma((lines,)),
+            dma((3, lines - 1)),
+            dma((3, lines)),
+            dma((5, 2, size // 4 + 1, chips + 1)),
+            dma((5, 2, size)),
             dma((size - 1,)),
             dma((size,)),
         ],
@@ -789,83 +795,227 @@
             collective_id=1, has_side_effects=True, vmem_limit_bytes=VMEM_BYTES
         ),
         name="front",
-    )(picked, joined, fc, proj, bias)
-
-
-def layer_sum_kernel(count, part_ref, total_ref, land, held, inner_sem, outer_sem, receive_sem):
+    )(tile, table, joined, fc, proj, out, trans, bias)
+
+
+def row_norm(values):
+    average = jnp.mean(values, axis=-1, keepdims=True)
+    centered = values - average
+    variance = jnp.mean(centered * centered, axis=-1, keepdims=True)
+    return centered * lax.rsqrt(variance + norm_eps)
+
+
+def layer_kernel(
+    count, heads,
+    stream_ref, joined_ref, fc_ref, proj_ref, out_ref, trans_ref, next_ref,
+    gains_ref, offsets_ref, joined_bias, fc_bias, trans_bias, turns_ref,
+    states_ref, moved_ref, low_ref,
+    own_next, next_all, x_attn, x_mlp, spread, gathered, mixed, returned, part,
+    land, held, total, inner_sem, outer_sem, receive_sem,
+    local_sem, heads_send, heads_receive, rows_send, rows_receive, next_send, next_receive,
+):
+    f32 = jnp.float32
+    bf16 = jnp.bfloat16
+    lines = lax.axis_size("batch")
+    place = lax.axis_index("batch")
+    size = lax.axis_size("seq")
+    spot = lax.axis_index("seq")
+    planes = others("batch")
+    peers = others("seq")
+    rows, depth = stream_ref.shape
+    tokens = rows // lines
+    plane_width = joined_ref.shape[1] // 3
+    columns = spread.shape[3]
+    groups = plane_width // columns
+    head_dim = columns // heads
+    step_rows = 32
+
+    own_next[...] = next_ref[...].astype(bf16)
+    greet([{"batch": plane} for plane in planes] + [{"seq": peer} for peer in peers])
+    sent = [
+        push(own_next, next_all.at[spot], next_send.at[index], next_receive.at[spot], {"seq": peer})
+        for index, peer in enumerate(peers)
+    ]
+    next_copy = pltpu.make_async_copy(own_next, next_all.at[spot], local_sem.at[0])
+    next_copy.start()
+
+    def norms(index, carry):
+        at = pl.ds(pl.multiple_of(index * step_rows, step_rows), step_rows)
+        unit = row_norm(stream_ref[at, :].astype(f32))
+        x_attn[at, :] = (unit * gains_ref[0:1, :] + offsets_ref[0:1, :]).astype(bf16)
+        x_mlp[at, :] = (unit * gains_ref[1:2, :] + offsets_ref[1:2, :]).astype(bf16)
+        return carry
+
+    lax.fori_loop(0, rows // step_rows, norms, 0)
+    half_rot = ROT // 2
+    for sequence in range(lines):
+        at = slice(sequence * tokens, (sequence + 1) * tokens)
+        for kind in range(3):
+            place_ = slice(kind * plane_width, (kind + 1) * plane_width)
+            value = jnp.dot(x_attn[at, :], joined_ref[:, place_], preferred_element_type=f32)
+            value = value + joined_bias[0:1, place_]
+            if kind < 2:
+                value = (
+                    value * turns_ref[0]
+                    + pltpu.roll(value, plane_width - half_rot, 1) * turns_ref[1]
+                    + pltpu.roll(value, half_rot, 1) * turns_ref[2]
+                )
+            value = value.astype(bf16)
+            for group in range(groups):
+                spread[sequence * groups + group, kind] = value[:, group * columns : (group + 1) * columns]
+    for index, peer in enumerate(peers):
+        sent.append(
+            push(spread.at[peer], gathered.at[spot], heads_send.at[index], heads_receive.at[spot], {"seq": peer})
+        )
+    heads_copy = pltpu.make_async_copy(spread.at[spot], gathered.at[spot], local_sem.at[1])
+    heads_copy.start()
+
+    def hidden_part(index, carry):
+        at = pl.ds(pl.multiple_of(index * tokens, tokens), tokens)
+        value = jnp.dot(x_mlp[at, :], fc_ref[...], preferred_element_type=f32) + fc_bias[...]
+        value = 0.5 * value * (1.0 + lax.erf(value * (0.5 ** 0.5)))
+        part[at, :] = jnp.dot(value.astype(bf16), proj_ref[...], preferred_element_type=f32)
+        return carry
+
+    lax.fori_loop(0, lines, hidden_part, 0)
+
+    def translate(probe, stream, low, weights, at):
+        moved = stream + jnp.dot(low, weights, preferred_element_type=f32) + trans_bias[probe : probe + 1, :]
+        moved_ref[probe, at, :] = moved
+        states_ref[1 + probe, at, :] = (
+            row_norm(moved) * gains_ref[2:3, :] + offsets_ref[4:5, :]
+        ).astype(bf16)
+
+    def first_probe(index, carry):
+        at = pl.ds(pl.multiple_of(index * tokens, tokens), tokens)
+        low = stream_ref[at, :]
+        translate(0, low.astype(f32), low, trans_ref[...], at)
+        return carry
+
+    lax.fori_loop(0, lines, first_probe, 0)
+    heads_copy.wait()
+    for peer in peers:
+        arrived(gathered.at[peer], heads_receive.at[peer], {"seq": peer})
+    length = size * tokens
+    block = 2 * tokens
+    lane = lax.broadcasted_iota(jnp.int32, (block, columns), 1) // head_dim
+    keys = jnp.concatenate([gathered[source, 1] for source in range(size)], axis=0)
+    values = jnp.concatenate([gathered[source, 2] for source in range(size)], axis=0)
+    for first in range(0, length, block):
+        end = first + block
+        queries = jnp.concatenate([gathered[first // tokens, 0], gathered[first // tokens + 1, 0]], axis=0)
+        allowed = lax.broadcasted_iota(jnp.int32, (block, end), 1) <= (
+            lax.broadcasted_iota(jnp.int32, (block, end), 0) + first
+        )
+        result = None
+        for head in range(heads):
+            chosen = jnp.where(lane == head, queries, jnp.zeros((), bf16))
+            scores = lax.dot_general(
+                chosen, keys[:end], (((1,), (1,)), ((), ())), preferred_element_type=f32
+            ) * head_dim ** (-0.5)
+            scores = jnp.where(allowed, scores, NEGATIVE)
+            exponent = jnp.exp(scores - jnp.max(scores, axis=-1, keepdims=True))
+            value = jnp.dot(
+                exponent.astype(bf16), values[:end], preferred_element_type=f32
+            ) / jnp.sum(exponent, axis=-1, keepdims=True)
+            result = value if result is None else jnp.where(lane == head, value, result)
+        result = result.astype(bf16)
+        for index in range(2):
+            mixed[first // tokens + index] = result[index * tokens : (index + 1) * tokens]
+    for index, peer in enumerate(peers):
+        sent.append(
+            push(mixed.at[peer], returned.at[spot], rows_send.at[index], rows_receive.at[spot], {"seq": peer})
+        )
+    rows_copy = pltpu.make_async_copy(mixed.at[spot], returned.at[spot], local_sem.at[2])
+    rows_copy.start()
+    rows_copy.wait()
+    for peer in peers:
+        arrived(returned.at[peer], rows_receive.at[peer], {"seq": peer})
+    for sequence in range(lines):
+        at = slice(sequence * tokens, (sequence + 1) * tokens)
+        attended = jnp.concatenate(
+            [returned[sequence * groups + group] for group in range(groups)], axis=1
+        )
+        part[at, :] += jnp.dot(attended, out_ref[...], preferred_element_type=f32)
     line_sum = LineSum(
-        count, part_ref.shape[0] // count, lambda at: part_ref[at, :],
-        land, held, total_ref, inner_sem, outer_sem, receive_sem,
+        count, rows // count, lambda at: part[at, :],
+        land, held, total, inner_sem, outer_sem, receive_sem,
     )
-    greet([{"batch": plane} for plane in others("batch")])
     line_sum.begin(range(count))
     for index in range(count + 1):
         if index < count:
             line_sum.gather(index)
         if index >= 1:
             line_sum.spread(index - 1)
+    next_copy.wait()
+    for peer in peers:
+        arrived(next_all.at[peer], next_receive.at[peer], {"seq": peer})
+    weights = next_all[...].reshape(depth, depth)
+
+    def second_probe(index, carry):
+        at = pl.ds(pl.multiple_of(index * tokens, tokens), tokens)
+        stream = (
+            stream_ref[at, :].astype(f32) + total[at, :].astype(f32) + offsets_ref[2:3, :] + offsets_ref[3:4, :]
+        )
+        states_ref[0, at, :] = (row_norm(stream) * gains_ref[2:3, :] + offsets_ref[4:5, :]).astype(bf16)
+        low = stream.astype(bf16)
+        low_ref[at, :] = low
+        translate(1, stream, low, next_all[...].reshape(depth, depth), at)
+        return carry
+
+    lax.fori_loop(0, lines, second_probe, 0)
+    for copy in sent:
+        copy.wait_send()
     line_sum.finish()
 
 
-def layer_sum(part):
-    rows, depth = part.shape
-    count = 8
+def layer(stream, joined, fc, proj, out, trans, next_trans, gains, offsets, joined_bias, fc_bias, trans_bias, turns):
+    size = lax.axis_size("seq")
+    lines = lax.axis_size("batch")
+    rows, depth = stream.shape
+    tokens = rows // lines
+    own_heads = depth // HEAD_DIM // size
+    columns = own_heads * HEAD_DIM
+    count = 32
+    bf16 = jnp.bfloat16
+    f32 = jnp.float32
     vmem = pl.BlockSpec(memory_space=pltpu.VMEM)
+    dma = pltpu.SemaphoreType.DMA
     return pl.pallas_call(
-        functools.partial(layer_sum_kernel, count),
-        in_specs=[vmem],
-        out_specs=vmem,
-        out_shape=jax.ShapeDtypeStruct((rows, depth), jnp.bfloat16),
-        scratch_shapes=LineSum.scratch(count, rows, depth),
+        functools.partial(layer_kernel, count, own_heads),
+        in_specs=[vmem] * 13,
+        out_specs=[vmem] * 3,
+        out_shape=[
+            jax.ShapeDtypeStruct((3, rows, depth), bf16),
+            jax.ShapeDtypeStruct((2, rows, depth), f32),
+            jax.ShapeDtypeStruct((rows, depth), bf16),
+        ],
+        scratch_shapes=[
+            pltpu.VMEM(next_trans.shape, bf16),
+            pltpu.VMEM((size,) + next_trans.shape, bf16),
+            pltpu.VMEM((rows, depth), bf16),
+            pltpu.VMEM((rows, depth), bf16),
+            pltpu.VMEM((size, 3, tokens, columns), bf16),
+            pltpu.VMEM((size, 3, tokens, columns), bf16),
+            pltpu.VMEM((size, tokens, columns), bf16),
+            pltpu.VMEM((size, tokens, columns), bf16),
+            pltpu.VMEM((rows, depth), f32),
+        ] + LineSum.scratch(count, rows, depth)[:2] + [
+            pltpu.VMEM((rows, depth), bf16),
+        ] + LineSum.scratch(count, rows, depth)[2:] + [
+            dma((3,)),
+            dma((size - 1,)),
+            dma((size,)),
+            dma((size - 1,)),
+            dma((size,)),
+            dma((size - 1,)),
+            dma((size,)),
+        ],
         compiler_params=pltpu.CompilerParams(
-            collective_id=4, has_side_effects=True, vmem_limit_bytes=VMEM_BYTES
+            collective_id=2, has_side_effects=True, vmem_limit_bytes=VMEM_BYTES
         ),
-        name="layer_sum",
-    )(part)
-
-
-def attention_kernel(heads, in_ref, out_ref):
-    sources, _, tokens, columns = in_ref.shape
-    length = sources * tokens
-    head_dim = columns // heads
-    block = 2 * tokens
-    lane = lax.broadcasted_iota(jnp.int32, (block, columns), 1) // head_dim
-    keys = jnp.concatenate([in_ref[source, 1] for source in range(sources)], axis=0)
-    values = jnp.concatenate([in_ref[source, 2] for source in range(sources)], axis=0)
-    for first in range(0, length, block):
-        end = first + block
-        queries = jnp.concatenate([in_ref[source, 0] for source in range(first // tokens, end // tokens)], axis=0)
-        allowed = lax.broadcasted_iota(jnp.int32, (block, end), 1) <= (
-            lax.broadcasted_iota(jnp.int32, (block, end), 0) + first
-        )
-        mixed = None
-        for head in range(heads):
-            chosen = jnp.where(lane == head, queries, jnp.zeros((), queries.dtype))
-            scores = lax.dot_general(
-                chosen, keys[:end], (((1,), (1,)), ((), ())), preferred_element_type=jnp.float32
-            ) * head_dim ** (-0.5)
-            scores = jnp.where(allowed, scores, NEGATIVE)
-            exponent = jnp.exp(scores - jnp.max(scores, axis=-1, keepdims=True))
-            result = jnp.dot(
-                exponent.astype(jnp.bfloat16), values[:end], preferred_element_type=jnp.float32
-            ) / jnp.sum(exponent, axis=-1, keepdims=True)
-            mixed = result if mixed is None else jnp.where(lane == head, result, mixed)
-        mixed = mixed.astype(jnp.bfloat16)
-        for index in range(block // tokens):
-            out_ref[first // tokens + index] = mixed[index * tokens : (index + 1) * tokens]
-
-
-def attention(blocks, heads):
-    sources, _, tokens, columns = blocks.shape
-    vmem = pl.BlockSpec(memory_space=pltpu.VMEM)
-    return pl.pallas_call(
-        functools.partial(attention_kernel, heads),
-        in_specs=[vmem],
-        out_specs=vmem,
-        out_shape=jax.ShapeDtypeStruct((sources, tokens, columns), jnp.bfloat16),
-        compiler_params=pltpu.CompilerParams(vmem_limit_bytes=VMEM_BYTES),
-        name="attention",
-    )(blocks)
+        name="layer",
+    )(stream, joined, fc, proj, out, trans, next_trans, gains, offsets, joined_bias, fc_bias, trans_bias, turns)
 
 
 def reduce_kernel(
@@ -1094,84 +1244,65 @@
     n_batch = lax.axis_size("batch")
     batch_index = lax.axis_index("batch")
     seq_index = lax.axis_index("seq")
-    rows = n_batch * tok_rows
     head_count = width // HEAD_DIM
     plane_heads = head_count // n_batch
     plane_width = plane_heads * HEAD_DIM
-    own_heads = head_count // n_seq
     hidden_rows = w_proj.shape[0]
 
+    half_rot = ROT // 2
+    local_places = seq_index * tok_rows + jnp.arange(tok_rows, dtype=jnp.int32)
+    frequency = 10000.0 ** (-2.0 * jnp.arange(half_rot, dtype=f32) / ROT)
+    angles = local_places.astype(f32)[:, None] * frequency[None, :]
+    cosine = jnp.cos(angles)
+    sine = jnp.sin(angles)
+    still = jnp.zeros((tok_rows, HEAD_DIM - ROT), f32)
+    blank = jnp.zeros((tok_rows, half_rot), f32)
+    turns = jnp.stack(
+        [
+            jnp.concatenate([cosine, cosine, still + 1.0], axis=1),
+            jnp.concatenate([-sine, blank, still], axis=1),
+            jnp.concatenate([blank, sine, still], axis=1),
+        ]
+    )
+    turns = jnp.tile(turns, (1, 1, plane_heads))
+
+    def plane_part(vector, parts, size):
+        return lax.dynamic_slice_in_dim(vector.reshape(parts, n_batch, size), batch_index, 1, 1).reshape(1, -1)
+
+    joined_bias = plane_part(wide_bias[: 3 * width], 3, plane_width)
+    fc_bias = plane_part(wide_bias[3 * width :], n_seq, hidden_rows)
     padding = jnp.broadcast_to(pad_lengths[:, None], (1, tok_rows))
     tile = jnp.concatenate([token_ids, pos_weights, padding, jnp.zeros((5, tok_rows), jnp.int32)], axis=0)
-    tiles = share(tile, "batch", 0, "share_tokens")
-    flat_ids = tiles[:, 0].reshape(-1)
-    local_places = seq_index * tok_rows + jnp.arange(tok_rows, dtype=jnp.int32)
-    living = local_places[None, :] < tok_rows * n_seq - tiles[:, 2]
-    weights = jnp.where(living, tiles[:, 1], 0).astype(f32).reshape(-1)
-
-    out_w = lax.all_gather(w_out, ("seq", "batch"), axis=0, tiled=True)
-    out_w = lax.dynamic_slice_in_dim(out_w, batch_index * plane_width, plane_width, 0)
-    trans_low = lax.all_gather(trans_weight.astype(bf16), "seq", axis=1, tiled=True)
-
-    picked = lookup(flat_ids - batch_index * vocab_rows, embed_in)
     own_rows = w_qkv.shape[0]
     joined_cut = jnp.transpose(w_qkv.reshape(own_rows, 3, n_batch, plane_width), (2, 0, 1, 3))
     joined_cut = joined_cut.reshape(n_batch, own_rows, 3 * plane_width)
     fc_cut = jnp.transpose(w_fc.reshape(own_rows, n_seq, n_batch, hidden_rows), (2, 0, 1, 3))
     fc_cut = fc_cut.reshape(n_batch, own_rows, n_seq * hidden_rows)
-    bias_tile = jnp.zeros((8, LANES), f32).at[:2, : trans_bias.shape[1]].set(trans_bias)
-    stream_low, joined_w, fc_w, proj_w, bias_all = front(picked, joined_cut, fc_cut, w_proj, bias_tile)
-    joined_w = joined_w.reshape(width, 3 * plane_width)
-    fc_w = fc_w.reshape(width, n_seq * hidden_rows)
-    proj_w = proj_w.reshape(n_seq * hidden_rows, width)
-    bias_full = jnp.transpose(bias_all[:, :2, : trans_bias.shape[1]], (1, 0, 2)).reshape(2, width)
-    stream0 = stream_low.astype(f32)
-
-    def plane_part(vector, parts, size):
-        return lax.dynamic_slice_in_dim(vector.reshape(parts, n_batch, size), batch_index, 1, 1).reshape(-1)
-
-    x_attn = normalize(stream0, norm_gains[0], layer_biases[0]).astype(bf16)
-    x_mlp = normalize(stream0, norm_gains[1], layer_biases[1]).astype(bf16)
-    joined = jnp.dot(x_attn, joined_w, preferred_element_type=f32) + plane_part(
-        wide_bias[: 3 * width], 3, plane_width
+    own_width = trans_bias.shape[1]
+    bias_tile = jnp.zeros((8, LANES), f32).at[:2, :own_width].set(trans_bias)
+    tiles, stream_low, joined_w, fc_w, proj_w, out_w, trans_low, bias_all = front(
+        tile, embed_in, joined_cut, fc_cut, w_proj, w_out, trans_weight[0], bias_tile
     )
-    joined = joined.reshape(rows, 3, plane_heads, HEAD_DIM)
-    all_places = jnp.tile(local_places, n_batch)
-    heads = jnp.stack(
-        [rotate(joined[:, 0], all_places), rotate(joined[:, 1], all_places), joined[:, 2]]
-    ).astype(bf16)
-    spread = heads.reshape(3, n_batch, tok_rows, plane_heads // own_heads, own_heads * HEAD_DIM)
-    spread = jnp.transpose(spread, (1, 3, 0, 2, 4)).reshape(n_seq, 3, tok_rows, own_heads * HEAD_DIM)
-    mixed = attention(swap(spread, 2, "swap_heads"), own_heads)
-    attended = swap(mixed, 3, "swap_rows")
-    attended = attended.reshape(n_batch, plane_heads // own_heads, tok_rows, own_heads * HEAD_DIM)
-    attended = jnp.transpose(attended, (0, 2, 1, 3)).reshape(rows, plane_width)
-    hidden = jax.nn.gelu(
-        jnp.dot(x_mlp, fc_w, preferred_element_type=f32)
-        + plane_part(wide_bias[3 * width :], n_seq, hidden_rows),
-        approximate=False,
-    ).astype(bf16)
-    part = jnp.dot(attended, out_w, preferred_element_type=f32) + jnp.dot(
-        hidden, proj_w, preferred_element_type=f32
+    living = local_places[None, :] < tok_rows * n_seq - tiles[:, 2]
+    weights = jnp.where(living, tiles[:, 1], 0).astype(f32).reshape(-1)
+    bias_full = jnp.transpose(bias_all[:, :2, :own_width], (1, 0, 2)).reshape(2, width)
+    states, translated, low1 = layer(
+        stream_low,
+        joined_w.reshape(width, 3 * plane_width),
+        fc_w.reshape(width, n_seq * hidden_rows),
+        proj_w.reshape(n_seq * hidden_rows, width),
+        out_w.reshape(plane_width, width),
+        trans_low.reshape(width, width),
+        trans_weight[1],
+        norm_gains,
+        layer_biases,
+        joined_bias,
+        fc_bias,
+        bias_full,
+        turns,
     )
-    stream1 = stream0 + layer_sum(part).astype(f32) + layer_biases[2] + layer_biases[3]
+    probe_low = (stream_low, low1)
     gain_final = norm_gains[2]
-    offset_final = layer_biases[4]
-    probe_in = (stream0, stream1)
-    probe_low = (stream_low, stream1.astype(bf16))
-    translated = [
-        probe_in[index]
-        + jnp.dot(probe_low[index], trans_low[index], preferred_element_type=f32)
-        + bias_full[index]
-        for index in range(2)
-    ]
-    states = jnp.stack(
-        [
-            normalize(stream1, gain_final, offset_final),
-            normalize(translated[0], gain_final, offset_final),
-            normalize(translated[1], gain_final, offset_final),
-        ]
-    ).astype(bf16)
     first, second, peaks, sums_part, cross_part = vocab_forward(states, unembed)
     stats = jnp.concatenate([peaks[-1], jnp.sum(sums_part, axis=1), jnp.sum(cross_part, axis=1)], axis=0)
     gathered = share(stats, "batch", 5, "share_stats")

time: 443 us -> 414 us (0.935)
  matrix products: 23 us -> 7.99 us
  between operations: 20.8 us -> 7.12 us
  other arithmetic: 36 us -> 24.2 us
  Pallas kernels: 342 us -> 351 us
    dot_general x5 -> x0, matrix products: 20.4 us -> none  [the longest x1 8.58 us: body(): jnp.dot(hidden, proj_w, preferred_element_type=f32)]
    pallas_call x5 -> x1, Pallas kernels: 90.4 us -> 111 us  [layer(): pl.pallas_call(functools.partial(layer_kernel, count, own_heads), in_spec...]
    pallas_call x2 -> x1, Pallas kernels: 15.5 us -> 6.95 us  [share(): pl.pallas_call(functools.partial(share_kernel, axis), in_specs=[space], o...]
    dot_general x2, matrix products: 2.64 us -> 7.99 us  [body(): jnp.einsum('td,te->de', probe_low[index], delta.astype(bf16), preferred_e...]
  transfers between devices with their start and end apart: 2 -> 0, of which waited for: 0 -> 0; matrix products, arithmetic and copies ran while one was open for 8% -> 0% of each run, Pallas kernels for 40% -> 0%
where the time goes in v4:
time: 414 us; the launch traced here: 407 us
  Pallas kernels  351 us (85%)
  other arithmetic  24.2 us (6%)
  local copies, waits for them, and re-layouts  17.1 us (4%)
  matrix products  7.99 us (2%)
  between operations  7.12 us (2%)
    pallas_call x1, Pallas kernels, layer(): pl.pallas_call(functools.partial(layer_kernel, count, own_heads), in_spec...  111 us
    pallas_call x1, Pallas kernels, front(): pl.pallas_call(functools.partial(front_kernel, count), in_specs=[vmem, an...  75.4 us
    pallas_call x1, Pallas kernels, vocab_forward(): pl.pallas_call(functools.partial(forward_kernel, vocab), grid=(tiles + 1,...  65.4 us
    pallas_call x1, Pallas kernels, reduce_gradients(): pl.pallas_call(functools.partial(reduce_kernel, count), in_specs=[pl.Bloc...  56.3 us
    pallas_call x1, Pallas kernels, vocab_backward(): pl.pallas_call(functools.partial(backward_kernel, vocab), grid=(tiles + 1...  36.3 us

profile of v4, /device:TPU:0, one launch (start us, length us, event | category | flops | bytes accessed | tf_op | source)
XLA Modules:
  0.0 407.4 jit_solution(15623663831860484947)
XLA Ops:
  1.2 0.9 copy.33.turns_ref
  4.8 1.1 slice_bitcast_fusion
  6.1 0.8 reshape.304.fc_ref
  7.1 0.9 reshape.302.joined_ref
  10.1 75.4 %front.1 = (s32[4,8,128]{2,1,0:T(8,128)}, bf16[512,1024]{1,0:T(8,128)(2,1)}, bf16[8,4,32,768]{3,2,1,0:T(8,128)(2,1)}, bf16[8,4,32,1024]{3,2,1,0:T(8,128)(2,1)}, ...) custom-call(s32[8,128]{1,0:T(8,128)} %add_add_fusion.tile_ref, ...), custom_call_target="tpu_custom_call" | custom-call | tf_op jit(solution)/shard_map/front/pallas_call | solution.py:762
  85.5 1.4 slice_bitcast_fusion.3.trans_bias
  86.8 110.7 %layer.1 = (bf16[3,512,1024]{2,1,0:T(8,128)(2,1)}, f32[2,512,1024]{2,1,0:T(8,128)}, bf16[512,1024]{1,0:T(8,128)(2,1)}) custom-call(bf16[512,1024]{1,0:T(8,128)(2,1)} %get-tuple-element.40.stream_ref, bf16[1024,768]{1,0:T(8,128)(2,1)} %bitcast.123, bf16[1024,1024]{1,0:T(8,128)(2,1)} %bitcast.120, bf16[1024,1024]{1,0:T(8,128)(2,1)} %bitcast.121, ...), custom_call_target="tpu_custom_call" | custom-call | tf_op jit(solution)/shard_map/layer/pallas_call | solution.py:984
  197.6 65.4 %vocab_forward.1 = (bf16[10,3,1280,256]{3,2,1,0:T(8,128)(2,1)}, bf16[10,3,1280,256]{3,2,1,0:T(8,128)(2,1)}, f32[10,3,512]{2,1,0:T(4,128)}, f32[3,8,512]{2,1,0:T(8,128)}, f32[2,8,512]{2,1,0:T(8,128)}) custom-call(bf16[3,512,1024]{2,1,0:T(8,128)(2,1)} %get-tuple-element.47.states_ref, bf16[12576,1024]{1,0:T(8,128)(2,1)} %table_ref.5), custom_call_target="tpu_custom_call" | custom-call | flops 39560675328 | bytes 64389120 | tf_op jit(solution)/shard_map/vocab_forward/pallas_call | solution.py:179
  263.7 0.8 reduce_sum.153
  264.5 0.8 reduce_sum.154
  265.9 6.9 %share_stats.1 = f32[4,8,512]{2,1,0:T(8,128)} custom-call(f32[8,512]{1,0:T(8,128)} %pad_maximum_fusion.2.tile_ref), custom_call_target="tpu_custom_call" | custom-call | tf_op jit(solution)/shard_map/share_stats/pallas_call | solution.py:483
  272.8 0.9 slice_reduce_fusion.2
  273.7 0.9 multiply_reduce_fusion.6
  274.7 0.9 multiply_reduce_fusion.7
  275.6 0.8 fusion.15
  279.1 1.6 exponential_multiply_fusion.scales_ref
  280.6 36.3 %vocab_backward.1 = f32[2,512,1024]{2,1,0:T(8,128)} custom-call(bf16[10,3,1280,256]{3,2,1,0:T(8,128)(2,1)} %get-tuple-element.48.first_ref, bf16[10,3,1280,256]{3,2,1,0:T(8,128)(2,1)} %get-tuple-element.49.second_ref, f32[10,3,512]{2,1,0:T(4,128)} %exponential_multiply_fusion.scales_ref, bf16[12576,1024]{1,0:T(8,128)(2,1)} %table_ref.5), custom_call_target="tpu_custom_call" | custom-call | flops 26373783552 | bytes 64389120 | tf_op jit(solution)/shard_map/vocab_backward/pallas_call | solution.py:292
  316.9 2.6 slice_reduce_fusion.1
  319.6 0.8 copy-done
  320.7 0.7 slice.128
  321.4 2.6 fusion.2
  324.3 1.3 multiply_reduce_fusion.1
  326.9 1.3 copy.36
  328.2 4.0 convert_bitcast_fusion.1
  332.2 2.3 copy.37
  334.5 4.0 convert_bitcast_fusion
  338.5 2.3 pad_maximum_fusion.grad_ref
  340.8 56.3 %reduce_gradients.1 = (bf16[256,1024]{1,0:T(8,128)(2,1)}, f32[8,128]{1,0:T(8,128)}, f32[8,8,128]{2,1,0:T(8,128)}) custom-call(bf16[2,8,128,1024]{3,2,1,0:T(8,128)(2,1)} %pad_maximum_fusion.grad_ref, f32[8,8,128]{2,1,0:T(8,128)} %pad.7.bias_ref, f32[8,128]{1,0:T(8,128)} %broadcast.206.note_ref), custom_call_target="tpu_custom_call" | custom-call | tf_op jit(solution)/shard_map/reduce_gradients/pallas_call | solution.py:1173
  397.1 0.9 reduce_sum.169
  400.1 1.3 multiply_subtract_fusion.1
  401.3 1.1 convert_multiply_fusion
  402.5 2.2 multiply_subtract_fusion
  (77 shorter events, 10.1 us)
Async XLA Ops:
  0.6 4.1 %copy-start.2 = (f32[2,128,1024]{2,1,0:T(8,128)S(1)}, f32[2,128,1024]{2,1,0:T(8,128)}, u32[]{:S(2)}) copy-start(f32[2,128,1024]{2,1,0:T(8,128)} %param.32) | copy-start | bytes 3145732
  0.7 5.2 %copy-start.6 = (bf16[32,4096]{1,0:T(8,128)(2,1)S(1)}, bf16[32,4096]{1,0:T(8,128)(2,1)}, u32[]{:S(2)}) copy-start(bf16[32,4096]{1,0:T(8,128)(2,1)} %param.26) | copy-start | bytes 786436
  1.2 5.7 %copy-start.7 = (bf16[32,3072]{1,0:T(8,128)(2,1)S(1)}, bf16[32,3072]{1,0:T(8,128)(2,1)}, u32[]{:S(2)}) copy-start(bf16[32,3072]{1,0:T(8,128)(2,1)} %param.24) | copy-start | bytes 589828
  4.7 4.1 %copy-start.11 = (s32[1,128]{1,0:T(1,128)S(1)}, s32[1,128]{1,0:T(1,128)}, u32[]{:S(2)}) copy-start(s32[1,128]{1,0:T(1,128)} %param.21) | copy-start | bytes 1540
  4.7 4.1 %copy-start.12 = (s32[1,128]{1,0:T(1,128)S(1)}, s32[1,128]{1,0:T(1,128)}, u32[]{:S(2)}) copy-start(s32[1,128]{1,0:T(1,128)} %param.20) | copy-start | bytes 1540
  4.7 4.8 %copy-start.8 = (f32[2,128]{1,0:T(2,128)S(1)}, f32[2,128]{1,0:T(2,128)}, u32[]{:S(2)}) copy-start(f32[2,128]{1,0:T(2,128)} %param.33) | copy-start | bytes 3076
  316.9 3.5 copy-start
  321.4 2.8 copy-start.1
  325.6 1.3 copy-start.3
  340.8 59.3 %copy-start.9 = (f32[2,128]{1,0:T(2,128)S(1)}, f32[2,128]{1,0:T(2,128)}, u32[]{:S(2)}) copy-start(f32[2,128]{1,0:T(2,128)} %param.37) | copy-start | bytes 3076
  340.8 59.3 %copy-start.10 = (f32[2,128]{1,0:T(2,128)S(1)}, f32[2,128]{1,0:T(2,128)}, u32[]{:S(2)}) copy-start(f32[2,128]{1,0:T(2,128)} %param.36) | copy-start | bytes 3076
  340.8 61.7 %copy-start.4 = (f32[2,128,1024]{2,1,0:T(8,128)S(1)}, f32[2,128,1024]{2,1,0:T(8,128)}, u32[]{:S(2)}) copy-start(f32[2,128,1024]{2,1,0:T(8,128)} %param.35) | copy-start | bytes 3145732
  340.8 61.7 %copy-start.5 = (f32[2,128,1024]{2,1,0:T(8,128)S(1)}, f32[2,128,1024]{2,1,0:T(8,128)}, u32[]{:S(2)}) copy-start(f32[2,128,1024]{2,1,0:T(8,128)} %param.34) | copy-start | bytes 3145732

commit v5 on v4

--- a/solution.py
+++ b/solution.py
@@ -213,7 +213,10 @@
     )(states, table)
 
 
-def backward_kernel(vocab, first_ref, second_ref, scales_ref, table_ref, out_ref, left, right, tail):
+def backward_kernel(
+    vocab, first_ref, second_ref, scales_ref, table_ref, moved_ref, low0_ref, low1_ref, gain_ref,
+    grad_ref, bias_ref, out_ref, left, right, tail, delta, turned,
+):
     step = pl.program_id(0)
     tiles = pl.num_programs(0) - 1
     width, depth = table_ref.shape
@@ -282,37 +285,71 @@
         stage(0, left, units(1, second_ref, right, tile))
         stage(1, right, units(0, first_ref, left, ahead))
 
-
-def vocab_backward(first, second, scales, table):
+    @pl.when(step == tiles)
+    def _():
+        rows = out_ref.shape[1]
+        chunk = 32
+        block = 256
+        for probe in range(2):
+            low_ref = (low0_ref, low1_ref)[probe]
+
+            def back(index, total, probe=probe):
+                at = pl.ds(pl.multiple_of(index * chunk, chunk), chunk)
+                value = norm_back(moved_ref[probe, at, :], out_ref[probe, at, :], gain_ref[2:3, :])
+                delta[at, :] = value.astype(jnp.bfloat16)
+                return total + jnp.sum(value, axis=0, keepdims=True)
+
+            bias_ref[probe : probe + 1, :] = lax.fori_loop(
+                0, rows // chunk, back, jnp.zeros((1, depth), jnp.float32)
+            )
+            turned[...] = jnp.transpose(low_ref[...])
+            for begin in range(0, depth, block):
+                grad_ref[probe, begin : begin + block, :] = jnp.dot(
+                    turned[begin : begin + block, :], delta[...], preferred_element_type=jnp.float32
+                ).astype(jnp.bfloat16)
+
+
+def vocab_backward(first, second, scales, table, moved, low0, low1, gains):
     tiles, _, _, half = first.shape
     vocab, depth = table.shape
     rows = 2 * half
     last = vocab - (tiles - 1) * VOCAB_TILE
     block = (1, 3, VOCAB_TILE, half)
+    whole = lambda *shape: pl.BlockSpec(shape, lambda i: (0,) * len(shape))
     return pl.pallas_call(
         functools.partial(backward_kernel, vocab),
         grid=(tiles + 1,),
         in_specs=[
             pl.BlockSpec(block, lambda i: (jnp.minimum(i, tiles - 1), 0, 0, 0)),
             pl.BlockSpec(block, lambda i: (jnp.maximum(i - 1, 0), 0, 0, 0)),
-            pl.BlockSpec((tiles, 3, rows), lambda i: (0, 0, 0)),
+            whole(tiles, 3, rows),
             pl.BlockSpec((VOCAB_TILE, depth), lambda i: (jnp.maximum(i - 1, 0), 0)),
+            whole(2, rows, depth),
+            whole(rows, depth),
+            whole(rows, depth),
+            whole(*gains.shape),
         ],
-        out_specs=pl.BlockSpec((2, rows, depth), lambda i: (0, 0, 0)),
-        out_shape=jax.ShapeDtypeStruct((2, rows, depth), jnp.float32),
+        out_specs=[whole(2, depth, depth), whole(2, depth)],
+        out_shape=[
+            jax.ShapeDtypeStruct((2, depth, depth), jnp.bfloat16),
+            jax.ShapeDtypeStruct((2, depth), jnp.float32),
+        ],
         scratch_shapes=[
+            pltpu.VMEM((2, rows, depth), jnp.float32),
             pltpu.VMEM((2 * half, VOCAB_TILE), jnp.bfloat16),
             pltpu.VMEM((2 * half, VOCAB_TILE), jnp.bfloat16),
             pltpu.VMEM((VOCAB_TILE - last // 256 * 256, depth), jnp.bfloat16),
+            pltpu.VMEM((rows, depth), jnp.bfloat16),
+            pltpu.VMEM((depth, rows), jnp.bfloat16),
         ],
         compiler_params=pltpu.CompilerParams(vmem_limit_bytes=VMEM_BYTES),
         cost_estimate=pl.CostEstimate(
-            flops=4 * rows * depth * vocab,
+            flops=4 * rows * depth * (vocab + depth),
             bytes_accessed=2 * vocab * (depth + 3 * rows),
             transcendentals=0,
         ),
         name="vocab_backward",
-    )(first, second, scales, table)
+    )(first, second, scales, table, moved, low0, low1, gains)
 
 
 def plane_place(place):
@@ -434,6 +471,18 @@
                 self.outer,
             )
 
+    def run(self, lag, todo=()):
+        todo = list(todo)
+        for index in range(self.count + lag):
+            if index < self.count:
+                self.gather(index)
+            if index >= lag:
+                self.spread(index - lag)
+            if todo:
+                todo.pop(0)()
+        for work in todo:
+            work()
+
     def finish(self):
         for index in range(self.count):
             rows = self.rows(index)
@@ -454,52 +503,90 @@
         ]
 
 
+class PlaneGather:
+    def __init__(self, views, send_sem, receive_sem):
+        self.views, self.send_sem, self.receive_sem = views, send_sem, receive_sem
+        self.size = lax.axis_size("seq")
+        self.spot = lax.axis_index("seq")
+        core, column, line = self.where = plane_place(self.spot)
+        self.rows = self.size // 4
+        self.beside = plane_index(core, 1 - column, line)
+        self.sibling = plane_index(1 - core, column, line)
+        lines = [lax.rem(line + step, self.rows) for step in range(1, self.rows)]
+        self.across = [plane_index(core, column, at) for at in lines]
+        self.corners = [plane_index(core, 1 - column, at) for at in lines]
+        self.started = []
+
+    def send(self, array, half, slot, way, index, target):
+        view = self.views[array](half, slot)
+        self.started.append(
+            push(
+                view, view, self.send_sem.at[array, half, way, index], self.receive_sem.at[array, half, slot],
+                {"seq": target},
+            )
+        )
+
+    def wait(self, array, half, slot):
+        arrived(self.views[array](half, slot), self.receive_sem.at[array, half, slot], {"seq": slot})
+
+    def own(self, array):
+        for half in range(2):
+            self.send(array, half, self.spot, 0, 0, self.beside)
+            for index, target in enumerate(self.across):
+                self.send(array, half, self.spot, 1 + index, 0, target)
+            self.send(array, half, self.spot, self.rows, 0, self.sibling)
+
+    def relay_side(self, array):
+        self.wait(array, 0, self.beside)
+        for index, target in enumerate(self.across):
+            self.send(array, 0, self.beside, 1 + index, 1, target)
+        for index, source in enumerate(self.across):
+            self.wait(array, 1, source)
+            self.send(array, 1, source, 0, 1 + index, self.beside)
+
+    def relay_core(self, array):
+        self.send(array, 0, self.beside, self.rows, 1, self.sibling)
+        self.wait(array, 1, self.beside)
+        self.send(array, 1, self.beside, self.rows, 1, self.sibling)
+        for index, source in enumerate(self.across):
+            self.send(array, 1, source, self.rows, 2 + index, self.sibling)
+            self.wait(array, 0, source)
+            self.send(array, 0, source, self.rows, 2 + index, self.sibling)
+        for index, source in enumerate(self.corners):
+            for half in range(2):
+                self.wait(array, half, source)
+                self.send(array, half, source, self.rows, 1 + self.rows + index, self.sibling)
+
+    def receive_core(self, array):
+        core, _, line = self.where
+        for step in range(self.rows):
+            for side in range(2):
+                source = plane_index(1 - core, side, lax.rem(line + step, self.rows))
+                for half in range(2):
+                    self.wait(array, half, source)
+
+    def finish(self):
+        for copy in self.started:
+            copy.wait_send()
+
+    @staticmethod
+    def scratch(arrays):
+        size = lax.axis_size("seq")
+        dma = pltpu.SemaphoreType.DMA
+        return [dma((arrays, 2, size // 4 + 1, size // 2 + 1)), dma((arrays, 2, size))]
+
+
 def others(axis):
     size = lax.axis_size(axis)
     place = lax.axis_index(axis)
     return [lax.rem(place + step, size) for step in range(1, size)]
 
 
-def share_kernel(axis, tile_ref, out_ref, local_sem, send_sem, receive_sem):
-    place = lax.axis_index(axis)
-    peers = others(axis)
-    local = pltpu.make_async_copy(tile_ref, out_ref.at[place], local_sem)
-    local.start()
-    greet([{axis: peer} for peer in peers])
-    copies = [
-        push(tile_ref, out_ref.at[place], send_sem.at[index], receive_sem.at[place], {axis: peer})
-        for index, peer in enumerate(peers)
-    ]
-    for peer in peers:
-        arrived(out_ref.at[peer], receive_sem.at[peer], {axis: peer})
-    for copy in copies:
-        copy.wait_send()
-    local.wait()
-
-
-def share(tile, axis, identity, name):
-    size = lax.axis_size(axis)
-    space = pl.BlockSpec(memory_space=pltpu.VMEM)
-    return pl.pallas_call(
-        functools.partial(share_kernel, axis),
-        in_specs=[space],
-        out_specs=space,
-        out_shape=jax.ShapeDtypeStruct((size,) + tile.shape, tile.dtype),
-        scratch_shapes=[
-            pltpu.SemaphoreType.DMA,
-            pltpu.SemaphoreType.DMA((size - 1,)),
-            pltpu.SemaphoreType.DMA((size,)),
-        ],
-        compiler_params=pltpu.CompilerParams(collective_id=identity, has_side_effects=True),
-        name=name,
-    )(tile)
-
-
 def front_kernel(
     count,
-    tile_ref, table_ref, joined_ref, fc_ref, proj_ref, out_ref, trans_ref, bias_ref,
-    tiles_out, stream_ref, joined_out, fc_out, proj_out, out_out, trans_out, bias_out,
-    table, column_ids, chosen, picked, trans_low,
+    tile_ref, table_ref, joined_ref, fc_ref, proj_ref, out_ref, bias_ref,
+    tiles_out, stream_ref, joined_out, fc_out, proj_out, out_out, bias_out,
+    table, column_ids, chosen, picked,
     land, held, inner_sem, outer_sem, receive_sem,
     local_sem, table_sem, tile_send, tile_receive, cross_send, cross_receive, plane_send, plane_receive, bias_send, bias_receive,
 ):
@@ -507,15 +594,9 @@
     place = lax.axis_index("batch")
     size = lax.axis_size("seq")
     spot = lax.axis_index("seq")
-    core, column, line = plane_place(spot)
-    rows = size // 4
-    beside = plane_index(core, 1 - column, line)
-    sibling = plane_index(1 - core, column, line)
-    across = [plane_index(core, column, lax.rem(line + step, rows)) for step in range(1, rows)]
-    corners = [plane_index(core, 1 - column, lax.rem(line + step, rows)) for step in range(1, rows)]
     planes = others("batch")
     peers = others("seq")
-    outs = (joined_out, fc_out, proj_out, out_out, trans_out)
+    outs = (joined_out, fc_out, proj_out, out_out)
     total_rows, depth = stream_ref.shape
     chunk = total_rows // count
     tokens = tile_ref.shape[1]
@@ -526,58 +607,13 @@
     origin = {"seq": wanted // lines, "batch": lax.rem(wanted, lines)}
     stays = number == wanted
 
-    def piece(array, half, slot):
+    def view(array):
         out = outs[array]
         if array < 2:
-            return out.at[slot, pl.ds(half * (lines // 2), lines // 2)]
-        return out.at[slot, :, pl.ds(half * (depth // 2), depth // 2)]
-
-    started = []
-
-    def send(array, half, slot, way, index, target):
-        view = piece(array, half, slot)
-        started.append(
-            push(view, view, plane_send.at[array, half, way, index], plane_receive.at[array, half, slot], {"seq": target})
-        )
-
-    def await_piece(array, half, slot):
-        arrived(piece(array, half, slot), plane_receive.at[array, half, slot], {"seq": slot})
-
-    def own(array):
-        for half in range(2):
-            send(array, half, spot, 0, 0, beside)
-            for index, target in enumerate(across):
-                send(array, half, spot, 1 + index, 0, target)
-            send(array, half, spot, rows, 0, sibling)
-
-    def relay_side(array):
-        await_piece(array, 0, beside)
-        for index, target in enumerate(across):
-            send(array, 0, beside, 1 + index, 1, target)
-        for index, source in enumerate(across):
-            await_piece(array, 1, source)
-            send(array, 1, source, 0, 1 + index, beside)
-
-    def relay_core(array):
-        send(array, 0, beside, rows, 1, sibling)
-        await_piece(array, 1, beside)
-        send(array, 1, beside, rows, 1, sibling)
-        for index, source in enumerate(across):
-            send(array, 1, source, rows, 2 + index, sibling)
-            await_piece(array, 0, source)
-            send(array, 0, source, rows, 2 + index, sibling)
-        for index, source in enumerate(corners):
-            for half in range(2):
-                await_piece(array, half, source)
-                send(array, half, source, rows, 1 + rows + index, sibling)
-
-    def receive_core(array):
-        for step in range(rows):
-            for side in range(2):
-                source = plane_index(1 - core, side, lax.rem(line + step, rows))
-                for half in range(2):
-                    await_piece(array, half, source)
-
+            return lambda half, slot: out.at[slot, pl.ds(half * (lines // 2), lines // 2)]
+        return lambda half, slot: out.at[slot, :, pl.ds(half * (depth // 2), depth // 2)]
+
+    plane = PlaneGather([view(array) for array in range(4)], plane_send, plane_receive)
     width = chosen.shape[1]
     cuts = table.shape[0] // width
     table_copies = [
@@ -592,13 +628,11 @@
         copy.start()
     if table.shape[0] > vocab:
         table[vocab:, :] = jnp.zeros((table.shape[0] - vocab, depth), table.dtype)
-    trans_low[...] = trans_ref[...].astype(jnp.bfloat16)
     locals_ = [
         pltpu.make_async_copy(source, target, local_sem.at[index])
         for index, (source, target) in enumerate(
             (
                 (proj_ref, proj_out.at[spot]),
-                (trans_low, trans_out.at[spot]),
                 (joined_ref.at[place], joined_out.at[spot, place]),
                 (fc_ref.at[place], fc_out.at[spot, place]),
                 (tile_ref, tiles_out.at[place]),
@@ -608,14 +642,14 @@
     ]
     for copy in locals_:
         copy.start()
-    out_copy = pltpu.make_async_copy(out_ref, out_out.at[spot], local_sem.at[6])
+    out_copy = pltpu.make_async_copy(out_ref, out_out.at[spot], local_sem.at[5])
 
     @pl.when(stays)
     def _():
         out_copy.start()
 
     barrier = pltpu.get_barrier_semaphore()
-    for partner in [{"batch": plane} for plane in planes] + [{"seq": peer} for peer in peers]:
+    for partner in [{"batch": other} for other in planes] + [{"seq": peer} for peer in peers]:
         pl.semaphore_signal(barrier, inc=1, device_id=partner, device_id_type=pl.DeviceIdType.MESH)
 
     @pl.when(jnp.logical_not(stays))
@@ -625,17 +659,16 @@
     pl.semaphore_wait(barrier, jnp.where(stays, 0, 1) + len(planes) + len(peers))
 
     tile_copies = [
-        push(tile_ref, tiles_out.at[place], tile_send.at[index], tile_receive.at[place], {"batch": plane})
-        for index, plane in enumerate(planes)
+        push(tile_ref, tiles_out.at[place], tile_send.at[index], tile_receive.at[place], {"batch": other})
+        for index, other in enumerate(planes)
     ]
-    for copy in locals_[:2]:
-        copy.wait()
-    own(2)
+    locals_[0].wait()
+    plane.own(2)
     crossing = []
     for array, source, out in ((0, joined_ref, joined_out), (1, fc_ref, fc_out)):
-        for index, plane in enumerate(planes):
+        for index, other in enumerate(planes):
             crossing.append(
-                push(source.at[plane], out.at[spot, place], cross_send.at[array, index], cross_receive.at[array, place], {"batch": plane})
+                push(source.at[other], out.at[spot, place], cross_send.at[array, index], cross_receive.at[array, place], {"batch": other})
             )
     out_push = pltpu.make_async_remote_copy(
         src_ref=out_ref, dst_ref=out_out.at[goal["seq"]], send_sem=cross_send.at[2, 0],
@@ -646,15 +679,14 @@
     def _():
         out_push.start()
 
-    own(4)
     bias_copies = [
         push(bias_ref, bias_out.at[spot], bias_send.at[index], bias_receive.at[spot], {"seq": peer})
         for index, peer in enumerate(peers)
     ]
-    for copy in locals_[2:]:
+    for copy in locals_[1:]:
         copy.wait()
-    for plane in planes:
-        arrived(tiles_out.at[plane], tile_receive.at[plane], {"batch": plane})
+    for other in planes:
+        arrived(tiles_out.at[other], tile_receive.at[other], {"batch": other})
     for sequence in range(lines):
         turned = jnp.transpose(tiles_out[sequence].astype(jnp.float32))
         column_ids[sequence * tokens : (sequence + 1) * tokens, :] = jnp.broadcast_to(
@@ -687,9 +719,9 @@
     )
 
     def turn(array):
-        for plane in planes:
-            arrived(outs[array].at[spot, plane], cross_receive.at[array, plane], {"batch": plane})
-        own(array)
+        for other in planes:
+            arrived(outs[array].at[spot, other], cross_receive.at[array, other], {"batch": other})
+        plane.own(array)
 
     def turn_out():
         @pl.when(stays)
@@ -700,54 +732,46 @@
         def _():
             arrived(out_out.at[spot], cross_receive.at[2, 0], origin)
 
-        own(3)
+        plane.own(3)
 
     todo = [
-        lambda: relay_side(2),
         lambda: turn(0),
-        turn_out,
-        lambda: relay_side(4),
-        lambda: turn(1),
-        lambda: relay_core(2),
-        lambda: relay_side(0),
-        lambda: relay_side(3),
-        lambda: relay_core(4),
-        lambda: relay_core(0),
-        lambda: relay_side(1),
-        lambda: relay_core(3),
-        lambda: relay_core(1),
-        lambda: receive_core(2),
-        lambda: receive_core(4),
-        lambda: receive_core(0),
-        lambda: receive_core(3),
-        lambda: receive_core(1),
+        lambda: (plane.relay_side(2), turn(1)),
+        lambda: (turn_out(), plane.relay_core(2)),
+        lambda: plane.relay_side(0),
+        lambda: None,
+        lambda: plane.relay_core(0),
+        lambda: None,
+        lambda: plane.relay_side(1),
+        lambda: plane.relay_side(3),
+        lambda: None,
+        lambda: plane.relay_core(1),
+        lambda: None,
+        lambda: plane.relay_core(3),
+        lambda: plane.receive_core(2),
+        lambda: plane.receive_core(0),
+        lambda: plane.receive_core(1),
+        lambda: plane.receive_core(3),
     ]
     for part in range(2):
         look(part)
         line_sum.begin(range(part * count // 2, (part + 1) * count // 2))
         todo.pop(0)()
-    for index in range(count + 1):
-        if index < count:
-            line_sum.gather(index)
-        if index >= 1:
-            line_sum.spread(index - 1)
-        if todo and index % 2:
-            todo.pop(0)()
-    for work in todo:
-        work()
+    line_sum.run(3, todo)
     for peer in peers:
         arrived(bias_out.at[peer], bias_receive.at[peer], {"seq": peer})
-    for copy in started + crossing + bias_copies + tile_copies:
+    for copy in crossing + bias_copies + tile_copies:
         copy.wait_send()
 
     @pl.when(jnp.logical_not(stays))
     def _():
         out_push.wait_send()
 
+    plane.finish()
     line_sum.finish()
 
 
-def front(tile, table, joined, fc, proj, out, trans, bias):
+def front(tile, table, joined, fc, proj, out, bias):
     size = lax.axis_size("seq")
     lines = lax.axis_size("batch")
     vocab, depth = table.shape
@@ -756,13 +780,12 @@
     vmem = pl.BlockSpec(memory_space=pltpu.VMEM)
     anywhere = pl.BlockSpec(memory_space=pl.ANY)
     dma = pltpu.SemaphoreType.DMA
-    chips = size // 2
     bf16 = jnp.bfloat16
     spread = lambda part, kind: jax.ShapeDtypeStruct((size,) + part.shape, kind)
     return pl.pallas_call(
         functools.partial(front_kernel, count),
-        in_specs=[vmem, anywhere, anywhere, anywhere, anywhere, anywhere, vmem, vmem],
-        out_specs=[vmem, vmem, anywhere, anywhere, anywhere, anywhere, anywhere, vmem],
+        in_specs=[vmem, anywhere, anywhere, anywhere, anywhere, anywhere, vmem],
+        out_specs=[vmem, vmem, anywhere, anywhere, anywhere, anywhere, vmem],
         out_shape=[
             jax.ShapeDtypeStruct((lines,) + tile.shape, tile.dtype),
             jax.ShapeDtypeStruct((rows, depth), bf16),
@@ -770,7 +793,6 @@
             spread(fc, bf16),
             spread(proj, bf16),
             spread(out, bf16),
-            spread(trans, bf16),
             spread(bias, jnp.float32),
         ],
         scratch_shapes=[
@@ -778,16 +800,14 @@
             pltpu.VMEM((rows, LANES), jnp.float32),
             pltpu.VMEM((rows // 2, VOCAB_TILE), bf16),
             pltpu.VMEM((rows, depth), jnp.float32),
-            pltpu.VMEM(trans.shape, bf16),
         ] + LineSum.scratch(count, rows, depth) + [
-            dma((7,)),
+            dma((6,)),
             dma((pl.cdiv(vocab, VOCAB_TILE),)),
             dma((lines - 1,)),
             dma((lines,)),
             dma((3, lines - 1)),
             dma((3, lines)),
-            dma((5, 2, size // 4 + 1, chips + 1)),
-            dma((5, 2, size)),
+        ] + PlaneGather.scratch(4) + [
             dma((size - 1,)),
             dma((size,)),
         ],
@@ -795,7 +815,7 @@
             collective_id=1, has_side_effects=True, vmem_limit_bytes=VMEM_BYTES
         ),
         name="front",
-    )(tile, table, joined, fc, proj, out, trans, bias)
+    )(tile, table, joined, fc, proj, out, bias)
 
 
 def row_norm(values):
@@ -807,12 +827,12 @@
 
 def layer_kernel(
     count, heads,
-    stream_ref, joined_ref, fc_ref, proj_ref, out_ref, trans_ref, next_ref,
+    stream_ref, joined_ref, fc_ref, proj_ref, out_ref, trans_ref,
     gains_ref, offsets_ref, joined_bias, fc_bias, trans_bias, turns_ref,
     states_ref, moved_ref, low_ref,
-    own_next, next_all, x_attn, x_mlp, spread, gathered, mixed, returned, part,
+    first_trans, second_trans, x_attn, x_mlp, spread, gathered, mixed, returned, part,
     land, held, total, inner_sem, outer_sem, receive_sem,
-    local_sem, heads_send, heads_receive, rows_send, rows_receive, next_send, next_receive,
+    local_sem, heads_send, heads_receive, rows_send, rows_receive, plane_send, plane_receive,
 ):
     f32 = jnp.float32
     bf16 = jnp.bfloat16
@@ -830,14 +850,16 @@
     head_dim = columns // heads
     step_rows = 32
 
-    own_next[...] = next_ref[...].astype(bf16)
+    spans = (first_trans, second_trans)
+    for probe in range(2):
+        spans[probe][spot] = trans_ref[probe].astype(bf16)
     greet([{"batch": plane} for plane in planes] + [{"seq": peer} for peer in peers])
-    sent = [
-        push(own_next, next_all.at[spot], next_send.at[index], next_receive.at[spot], {"seq": peer})
-        for index, peer in enumerate(peers)
-    ]
-    next_copy = pltpu.make_async_copy(own_next, next_all.at[spot], local_sem.at[0])
-    next_copy.start()
+    sent = []
+
+    def view(array):
+        return lambda half, slot: spans[array].at[slot, :, pl.ds(half * (depth // 2), depth // 2)]
+
+    plane = PlaneGather([view(0), view(1)], plane_send, plane_receive)
 
     def norms(index, carry):
         at = pl.ds(pl.multiple_of(index * step_rows, step_rows), step_rows)
@@ -867,8 +889,10 @@
         sent.append(
             push(spread.at[peer], gathered.at[spot], heads_send.at[index], heads_receive.at[spot], {"seq": peer})
         )
-    heads_copy = pltpu.make_async_copy(spread.at[spot], gathered.at[spot], local_sem.at[1])
+    heads_copy = pltpu.make_async_copy(spread.at[spot], gathered.at[spot], local_sem.at[0])
     heads_copy.start()
+    plane.own(0)
+    plane.own(1)
 
     def hidden_part(index, carry):
         at = pl.ds(pl.multiple_of(index * tokens, tokens), tokens)
@@ -886,13 +910,12 @@
             row_norm(moved) * gains_ref[2:3, :] + offsets_ref[4:5, :]
         ).astype(bf16)
 
-    def first_probe(index, carry):
-        at = pl.ds(pl.multiple_of(index * tokens, tokens), tokens)
+    def first_probe(sequence):
+        at = slice(sequence * tokens, (sequence + 1) * tokens)
         low = stream_ref[at, :]
-        translate(0, low.astype(f32), low, trans_ref[...], at)
-        return carry
-
-    lax.fori_loop(0, lines, first_probe, 0)
+        translate(0, low.astype(f32), low, first_trans[...].reshape(depth, depth), at)
+
+    plane.relay_side(0)
     heads_copy.wait()
     for peer in peers:
         arrived(gathered.at[peer], heads_receive.at[peer], {"seq": peer})
@@ -926,8 +949,10 @@
         sent.append(
             push(mixed.at[peer], returned.at[spot], rows_send.at[index], rows_receive.at[spot], {"seq": peer})
         )
-    rows_copy = pltpu.make_async_copy(mixed.at[spot], returned.at[spot], local_sem.at[2])
+    rows_copy = pltpu.make_async_copy(mixed.at[spot], returned.at[spot], local_sem.at[1])
     rows_copy.start()
+    plane.relay_core(0)
+    plane.relay_side(1)
     rows_copy.wait()
     for peer in peers:
         arrived(returned.at[peer], rows_receive.at[peer], {"seq": peer})
@@ -942,15 +967,10 @@
         land, held, total, inner_sem, outer_sem, receive_sem,
     )
     line_sum.begin(range(count))
-    for index in range(count + 1):
-        if index < count:
-            line_sum.gather(index)
-        if index >= 1:
-            line_sum.spread(index - 1)
-    next_copy.wait()
-    for peer in peers:
-        arrived(next_all.at[peer], next_receive.at[peer], {"seq": peer})
-    weights = next_all[...].reshape(depth, depth)
+    todo = [lambda: None, lambda: plane.relay_core(1), lambda: plane.receive_core(0)]
+    todo += [functools.partial(first_probe, sequence) for sequence in range(lines)]
+    todo += [lambda: plane.receive_core(1)]
+    line_sum.run(3, todo)
 
     def second_probe(index, carry):
         at = pl.ds(pl.multiple_of(index * tokens, tokens), tokens)
@@ -960,30 +980,31 @@
         states_ref[0, at, :] = (row_norm(stream) * gains_ref[2:3, :] + offsets_ref[4:5, :]).astype(bf16)
         low = stream.astype(bf16)
         low_ref[at, :] = low
-        translate(1, stream, low, next_all[...].reshape(depth, depth), at)
+        translate(1, stream, low, second_trans[...].reshape(depth, depth), at)
         return carry
 
     lax.fori_loop(0, lines, second_probe, 0)
     for copy in sent:
         copy.wait_send()
+    plane.finish()
     line_sum.finish()
 
 
-def layer(stream, joined, fc, proj, out, trans, next_trans, gains, offsets, joined_bias, fc_bias, trans_bias, turns):
+def layer(stream, joined, fc, proj, out, trans, gains, offsets, joined_bias, fc_bias, trans_bias, turns):
     size = lax.axis_size("seq")
     lines = lax.axis_size("batch")
     rows, depth = stream.shape
     tokens = rows // lines
     own_heads = depth // HEAD_DIM // size
     columns = own_heads * HEAD_DIM
-    count = 32
+    count = 16
     bf16 = jnp.bfloat16
     f32 = jnp.float32
     vmem = pl.BlockSpec(memory_space=pltpu.VMEM)
     dma = pltpu.SemaphoreType.DMA
     return pl.pallas_call(
         functools.partial(layer_kernel, count, own_heads),
-        in_specs=[vmem] * 13,
+        in_specs=[vmem] * 12,
         out_specs=[vmem] * 3,
         out_shape=[
             jax.ShapeDtypeStruct((3, rows, depth), bf16),
@@ -991,8 +1012,8 @@
             jax.ShapeDtypeStruct((rows, depth), bf16),
         ],
         scratch_shapes=[
-            pltpu.VMEM(next_trans.shape, bf16),
-            pltpu.VMEM((size,) + next_trans.shape, bf16),
+            pltpu.VMEM((size,) + trans.shape[1:], bf16),
+            pltpu.VMEM((size,) + trans.shape[1:], bf16),
             pltpu.VMEM((rows, depth), bf16),
             pltpu.VMEM((rows, depth), bf16),
             pltpu.VMEM((size, 3, tokens, columns), bf16),
@@ -1003,26 +1024,101 @@
         ] + LineSum.scratch(count, rows, depth)[:2] + [
             pltpu.VMEM((rows, depth), bf16),
         ] + LineSum.scratch(count, rows, depth)[2:] + [
-            dma((3,)),
+            dma((2,)),
             dma((size - 1,)),
             dma((size,)),
             dma((size - 1,)),
             dma((size,)),
-            dma((size - 1,)),
-            dma((size,)),
-        ],
+        ] + PlaneGather.scratch(2),
         compiler_params=pltpu.CompilerParams(
             collective_id=2, has_side_effects=True, vmem_limit_bytes=VMEM_BYTES
         ),
         name="layer",
-    )(stream, joined, fc, proj, out, trans, next_trans, gains, offsets, joined_bias, fc_bias, trans_bias, turns)
+    )(stream, joined, fc, proj, out, trans, gains, offsets, joined_bias, fc_bias, trans_bias, turns)
+
+
+def stats_kernel(
+    tiles_ref, peaks_ref, sums_ref, cross_ref, scales_ref, note_ref,
+    gathered, send_sem, receive_sem,
+):
+    place = lax.axis_index("batch")
+    spot = lax.axis_index("seq")
+    size = lax.axis_size("seq")
+    planes = others("batch")
+    tiles = peaks_ref.shape[0]
+    rows = peaks_ref.shape[2]
+    lines = gathered.shape[0]
+    tokens = rows // lines
+    gathered[place, 0:3, :] = peaks_ref[tiles - 1]
+    for state in range(3):
+        gathered[place, 3 + state : 4 + state, :] = jnp.sum(sums_ref[state], axis=0, keepdims=True)
+    for other in range(2):
+        gathered[place, 6 + other : 7 + other, :] = jnp.sum(cross_ref[other], axis=0, keepdims=True)
+    greet([{"batch": plane} for plane in planes])
+    copies = [
+        push(gathered.at[place], gathered.at[place], send_sem.at[index], receive_sem.at[place], {"batch": plane})
+        for index, plane in enumerate(planes)
+    ]
+    position = spot * tokens + lax.broadcasted_iota(jnp.int32, (1, tokens), 1)
+    weights = jnp.concatenate(
+        [
+            jnp.where(position < size * tokens - tiles_ref[line, 2:3, :], tiles_ref[line, 1:2, :], 0).astype(jnp.float32)
+            for line in range(lines)
+        ],
+        axis=1,
+    )
+    for plane in planes:
+        arrived(gathered.at[plane], receive_sem.at[plane], {"batch": plane})
+    tops = gathered[0, 0:3, :]
+    for line in range(1, lines):
+        tops = jnp.maximum(tops, gathered[line, 0:3, :])
+    sums = jnp.zeros((3, rows), jnp.float32)
+    cross = jnp.zeros((2, rows), jnp.float32)
+    for line in range(lines):
+        fade = jnp.exp(gathered[line, 0:3, :] - tops)
+        sums += gathered[line, 3:6, :] * fade
+        cross += gathered[line, 6:8, :] * fade[0:1]
+    totals = tops + jnp.log(sums)
+    diverge = cross / sums[0:1] - totals[0:1] + totals[1:3]
+    loss = weights * (diverge[0:1] + diverge[1:2])
+    for tile in range(tiles):
+        scales_ref[tile] = weights * jnp.exp(peaks_ref[tile] - totals)
+    note_ref[...] = jnp.zeros_like(note_ref)
+    for line in range(rows // LANES):
+        at = slice(line * LANES, (line + 1) * LANES)
+        note_ref[1:2, :] += loss[:, at]
+        note_ref[2:3, :] += weights[:, at]
+    for copy in copies:
+        copy.wait_send()
+
+
+def statistics(tiles, peaks, sums, cross):
+    lines = lax.axis_size("batch")
+    rows = peaks.shape[2]
+    vmem = pl.BlockSpec(memory_space=pltpu.VMEM)
+    return pl.pallas_call(
+        stats_kernel,
+        in_specs=[vmem] * 4,
+        out_specs=[vmem] * 2,
+        out_shape=[
+            jax.ShapeDtypeStruct(peaks.shape, jnp.float32),
+            jax.ShapeDtypeStruct((8, LANES), jnp.float32),
+        ],
+        scratch_shapes=[
+            pltpu.VMEM((lines, 8, rows), jnp.float32),
+            pltpu.SemaphoreType.DMA((lines - 1,)),
+            pltpu.SemaphoreType.DMA((lines,)),
+        ],
+        compiler_params=pltpu.CompilerParams(collective_id=5, has_side_effects=True),
+        name="statistics",
+    )(tiles, peaks, sums, cross)
 
 
 def reduce_kernel(
     count,
     grad_ref, bias_ref, note_ref,
     total_ref, bias_out, note_out,
-    mine, sibling_land, side_land, line_land, side_sum, line_sum_ref, last_land, own_sum,
+    mine, sibling_land, side_land, line_land, side_sum, line_part, last_land, own_sum,
     land, held, inner_sem, outer_sem, receive_sem,
     tile_land, tile_line, tile_out,
     local_sem, core_send, core_receive, side_send, side_receive, line_send, line_receive,
@@ -1033,121 +1129,164 @@
     place = lax.axis_index("batch")
     core, column, line = plane_place(spot)
     rows = size // 4
-    width = total_ref.shape[0] // 2
+    step_rows = total_ref.shape[0] // count // 2
     beside = {"seq": plane_index(core, 1 - column, line)}
     sibling = {"seq": plane_index(1 - core, column, line)}
     across = [{"seq": plane_index(core, column, lax.rem(line + step, rows))} for step in range(1, rows)]
     peers = others("seq")
     planes = others("batch")
     f32 = jnp.float32
-    order = [(lax.rem(line + step, rows), side) for step in range(rows) for side in (1 - column, column)]
-    places = [(step, side) for step in range(rows) for side in range(2)]
-
-    loads = [
-        pltpu.make_async_copy(
-            grad_ref.at[:, plane_index(core, side, at)], mine.at[step, index], local_sem.at[step, index]
-        )
-        for (step, index), (at, side) in zip(places, order)
+    bf16 = jnp.bfloat16
+    chips = [
+        (step, index, lax.rem(line + step, rows), side)
+        for step in range(rows)
+        for index, side in enumerate((1 - column, column))
     ]
-    for copy in loads:
-        copy.start()
+    sent = []
+
+    def cut(chunk):
+        return pl.ds(chunk * step_rows, step_rows)
+
+    loads = {}
+    for chunk in range(count):
+        for step, index, at, side in chips:
+            copy = pltpu.make_async_copy(
+                grad_ref.at[:, plane_index(core, side, at), cut(chunk)], mine.at[chunk, step, index],
+                local_sem.at[chunk, step, index],
+            )
+            copy.start()
+            loads[chunk, step, index] = copy
     tile_land[spot] = bias_ref[spot]
     greet([{"batch": plane} for plane in planes] + [{"seq": peer} for peer in peers])
-    sent = []
-    for (step, index), (at, side) in zip(places, order):
-        sent.append(
-            push(
-                grad_ref.at[:, plane_index(1 - core, side, at)], sibling_land.at[step, index],
-                core_send.at[step, index], core_receive.at[step, index], sibling,
+    for chunk in range(count):
+        for step, index, at, side in chips:
+            sent.append(
+                push(
+                    grad_ref.at[:, plane_index(1 - core, side, at), cut(chunk)], sibling_land.at[chunk, step, index],
+                    core_send.at[chunk, step, index], core_receive.at[chunk, step, index], sibling,
+                )
             )
-        )
     for index, peer in enumerate(peers):
         sent.append(
             push(bias_ref.at[peer], tile_land.at[spot], bias_send.at[index], bias_receive.at[spot], {"seq": peer})
         )
-    for (step, index), copy in zip(places, loads):
-        copy.wait()
-        arrived(sibling_land.at[step, index], core_receive.at[step, index], sibling)
-        mine[step, index] = (
-            mine[step, index].astype(f32) + sibling_land[step, index].astype(f32)
-        ).astype(jnp.bfloat16)
-        if index == 0:
-            sent.append(
-                push(mine.at[step, 0, 0], side_land.at[step], side_send.at[step], side_receive.at[step], beside)
-            )
-        if step > 0:
+    line_sum = LineSum(
+        count, 2 * step_rows, lambda at: own_sum[at, :],
+        land, held, total_ref, inner_sem, outer_sem, receive_sem,
+    )
+
+    def pair(chunk):
+        for step, index, _, _ in chips:
+            loads[chunk, step, index].wait()
+            arrived(sibling_land.at[chunk, step, index], core_receive.at[chunk, step, index], sibling)
+            mine[chunk, step, index] = (
+                mine[chunk, step, index].astype(f32) + sibling_land[chunk, step, index].astype(f32)
+            ).astype(bf16)
+            if index == 0:
+                sent.append(
+                    push(
+                        mine.at[chunk, step, 0, 0], side_land.at[chunk, step],
+                        side_send.at[chunk, step], side_receive.at[chunk, step], beside,
+                    )
+                )
+            if step > 0:
+                sent.append(
+                    push(
+                        mine.at[chunk, step, index, 1], line_land.at[chunk, step - 1, index],
+                        line_send.at[chunk, step - 1, index], line_receive.at[chunk, step - 1, index],
+                        across[step - 1],
+                    )
+                )
+
+    def second(chunk):
+        begin = chunk * 2 * step_rows
+        for step in list(range(1, rows)) + [0]:
+            arrived(side_land.at[chunk, step], side_receive.at[chunk, step], beside)
+            both = mine[chunk, step, 1, 0].astype(f32) + side_land[chunk, step].astype(f32)
+            if step > 0:
+                side_sum[chunk, step - 1] = both.astype(bf16)
+                sent.append(
+                    push(
+                        side_sum.at[chunk, step - 1], last_land.at[chunk, step],
+                        last_send.at[chunk, step], last_receive.at[chunk, step], across[step - 1],
+                    )
+                )
+            else:
+                own_sum[begin : begin + step_rows, :] = both
+        for index in range(2):
+            both = mine[chunk, 0, index, 1].astype(f32)
+            for step in range(1, rows):
+                arrived(
+                    line_land.at[chunk, step - 1, index], line_receive.at[chunk, step - 1, index], across[-step]
+                )
+                both += line_land[chunk, step - 1, index].astype(f32)
+            if index == 0:
+                line_part[chunk] = both.astype(bf16)
+                sent.append(
+                    push(
+                        line_part.at[chunk], last_land.at[chunk, 0],
+                        last_send.at[chunk, 0], last_receive.at[chunk, 0], beside,
+                    )
+                )
+            else:
+                own_sum[begin + step_rows : begin + 2 * step_rows, :] = both
+
+    def third(chunk):
+        begin = chunk * 2 * step_rows
+        for step in range(1, rows):
+            arrived(last_land.at[chunk, step], last_receive.at[chunk, step], across[-step])
+            own_sum[begin : begin + step_rows, :] += last_land[chunk, step].astype(f32)
+        arrived(last_land.at[chunk, 0], last_receive.at[chunk, 0], beside)
+        own_sum[begin + step_rows : begin + 2 * step_rows, :] += last_land[chunk, 0].astype(f32)
+        line_sum.begin([chunk])
+        line_sum.gather(chunk)
+
+    def tiles_in_plane():
+        for peer in peers:
+            arrived(tile_land.at[peer], bias_receive.at[peer], {"seq": peer})
+        tile = tile_land[0]
+        for source in range(1, size):
+            tile += tile_land[source]
+        tile_line[place] = tile
+        for index, plane in enumerate(planes):
             sent.append(
                 push(
-                    mine.at[step, index, 1], line_land.at[step - 1, index],
-                    line_send.at[step - 1, index], line_receive.at[step - 1, index], across[step - 1],
+                    tile_line.at[place], tile_line.at[place], plane_send.at[index], plane_receive.at[place],
+                    {"batch": plane},
                 )
             )
-    for step in list(range(1, rows)) + [0]:
-        arrived(side_land.at[step], side_receive.at[step], beside)
-        both = mine[step, 1, 0].astype(f32) + side_land[step].astype(f32)
-        if step > 0:
-            side_sum[step - 1] = both.astype(jnp.bfloat16)
-            sent.append(
-                push(
-                    side_sum.at[step - 1], last_land.at[step], last_send.at[step], last_receive.at[step],
-                    across[step - 1],
-                )
-            )
-        else:
-            own_sum[0:width, :] = both
-    for index in range(2):
-        both = mine[0, index, 1].astype(f32)
-        for step in range(1, rows):
-            arrived(line_land.at[step - 1, index], line_receive.at[step - 1, index], across[-step])
-            both += line_land[step - 1, index].astype(f32)
-        if index == 0:
-            line_sum_ref[...] = both.astype(jnp.bfloat16)
-            sent.append(push(line_sum_ref, last_land.at[0], last_send.at[0], last_receive.at[0], beside))
-        else:
-            own_sum[width:, :] = both
-    for step in range(1, rows):
-        arrived(last_land.at[step], last_receive.at[step], across[-step])
-        own_sum[0:width, :] += last_land[step].astype(f32)
-    line_sum = LineSum(
-        count, 2 * width // count, lambda at: own_sum[at, :],
-        land, held, total_ref, inner_sem, outer_sem, receive_sem,
-    )
-    line_sum.begin(range(count // 2))
-    for index in range(count // 2):
-        line_sum.gather(index)
-    arrived(last_land.at[0], last_receive.at[0], beside)
-    own_sum[width:, :] += last_land[0].astype(f32)
-    line_sum.begin(range(count // 2, count))
-    for index in range(count // 2, count):
-        line_sum.gather(index)
-        line_sum.spread(index - count // 2)
-    for peer in peers:
-        arrived(tile_land.at[peer], bias_receive.at[peer], {"seq": peer})
-    tile = tile_land[0]
-    for source in range(1, size):
-        tile += tile_land[source]
-    tile_line[place] = tile
-    for index, plane in enumerate(planes):
-        sent.append(
-            push(tile_line.at[place], tile_line.at[place], plane_send.at[index], plane_receive.at[place], {"batch": plane})
-        )
+
+    squares = []
+
+    def square(chunk):
+        line_sum.spread(chunk)
+        for row in range(chunk * 2 * step_rows, (chunk + 1) * 2 * step_rows, 16):
+            value = total_ref[row : row + 16, :].astype(f32)
+            value = value * value
+            for begin in range(0, value.shape[1], LANES):
+                block = value[:8, begin : begin + LANES] + value[8:, begin : begin + LANES]
+                squares[:] = [block + squares[0]] if squares else [block]
+
+    for time in range(count + 5):
+        if time < count:
+            pair(time)
+        if 0 <= time - 2 < count:
+            second(time - 2)
+        if 0 <= time - 3 < count:
+            third(time - 3)
+        if time == count:
+            tiles_in_plane()
+        if 0 <= time - 5 < count:
+            square(time - 5)
     for plane in planes:
         arrived(tile_line.at[plane], plane_receive.at[plane], {"batch": plane})
     tile = tile_line[0]
     for source in range(1, lax.axis_size("batch")):
         tile += tile_line[source]
     bias_out[...] = tile
-    squares = tile * tile
-    for index in range(count // 2, count):
-        line_sum.spread(index)
-    for row in range(0, 2 * width, 16):
-        value = total_ref[row : row + 16, :].astype(f32)
-        value = value * value
-        for begin in range(0, value.shape[1], LANES):
-            squares += value[:8, begin : begin + LANES] + value[8:, begin : begin + LANES]
-    head = jnp.sum(squares, axis=0, keepdims=True)
-    line8 = lax.broadcasted_iota(jnp.int32, (8, LANES), 0)
-    tile_out[...] = jnp.where(line8 == 0, head, note_ref[...])
+    head = jnp.sum(squares[0] + tile * tile, axis=0, keepdims=True)
+    row8 = lax.broadcasted_iota(jnp.int32, (8, LANES), 0)
+    tile_out[...] = jnp.where(row8 == 0, head, note_ref[...])
     note_out[spot] = tile_out[...]
     for index, peer in enumerate(peers):
         sent.append(
@@ -1166,11 +1305,12 @@
     _, _, width, depth = grad.shape
     rows = size // 4
     count = 4
+    cut = width // count
     bf16 = jnp.bfloat16
     vmem = pl.BlockSpec(memory_space=pltpu.VMEM)
     dma = pltpu.SemaphoreType.DMA
     near = max(rows - 1, 1)
-    return pl.pallas_call(
+    total, bias_sum, notes = pl.pallas_call(
         functools.partial(reduce_kernel, count),
         in_specs=[pl.BlockSpec(memory_space=pl.ANY), vmem, vmem],
         out_specs=[vmem, vmem, vmem],
@@ -1180,27 +1320,27 @@
             jax.ShapeDtypeStruct((size,) + note.shape, jnp.float32),
         ],
         scratch_shapes=[
-            pltpu.VMEM((rows, 2, 2, width, depth), bf16),
-            pltpu.VMEM((rows, 2, 2, width, depth), bf16),
-            pltpu.VMEM((rows, width, depth), bf16),
-            pltpu.VMEM((near, 2, width, depth), bf16),
-            pltpu.VMEM((near, width, depth), bf16),
-            pltpu.VMEM((width, depth), bf16),
-            pltpu.VMEM((rows, width, depth), bf16),
+            pltpu.VMEM((count, rows, 2, 2, cut, depth), bf16),
+            pltpu.VMEM((count, rows, 2, 2, cut, depth), bf16),
+            pltpu.VMEM((count, rows, cut, depth), bf16),
+            pltpu.VMEM((count, near, 2, cut, depth), bf16),
+            pltpu.VMEM((count, near, cut, depth), bf16),
+            pltpu.VMEM((count, cut, depth), bf16),
+            pltpu.VMEM((count, rows, cut, depth), bf16),
             pltpu.VMEM((2 * width, depth), jnp.float32),
         ] + LineSum.scratch(count, 2 * width, depth) + [
             pltpu.VMEM((size,) + bias.shape[1:], jnp.float32),
             pltpu.VMEM((lines,) + bias.shape[1:], jnp.float32),
             pltpu.VMEM(note.shape, jnp.float32),
-            dma((rows, 2)),
-            dma((rows, 2)),
-            dma((rows, 2)),
-            dma((rows,)),
-            dma((rows,)),
-            dma((near, 2)),
-            dma((near, 2)),
-            dma((rows,)),
-            dma((rows,)),
+            dma((count, rows, 2)),
+            dma((count, rows, 2)),
+            dma((count, rows, 2)),
+            dma((count, rows)),
+            dma((count, rows)),
+            dma((count, near, 2)),
+            dma((count, near, 2)),
+            dma((count, rows)),
+            dma((count, rows)),
             dma((size - 1,)),
             dma((size,)),
             dma((lines - 1,)),
@@ -1213,6 +1353,8 @@
         ),
         name="reduce_gradients",
     )(grad, bias, note)
+    total = jnp.transpose(total.reshape(count, 2, cut, depth), (1, 0, 2, 3)).reshape(2, width, depth)
+    return total, bias_sum, notes
 
 
 def body(
@@ -1280,11 +1422,9 @@
     fc_cut = fc_cut.reshape(n_batch, own_rows, n_seq * hidden_rows)
     own_width = trans_bias.shape[1]
     bias_tile = jnp.zeros((8, LANES), f32).at[:2, :own_width].set(trans_bias)
-    tiles, stream_low, joined_w, fc_w, proj_w, out_w, trans_low, bias_all = front(
-        tile, embed_in, joined_cut, fc_cut, w_proj, w_out, trans_weight[0], bias_tile
+    tiles, stream_low, joined_w, fc_w, proj_w, out_w, bias_all = front(
+        tile, embed_in, joined_cut, fc_cut, w_proj, w_out, bias_tile
     )
-    living = local_places[None, :] < tok_rows * n_seq - tiles[:, 2]
-    weights = jnp.where(living, tiles[:, 1], 0).astype(f32).reshape(-1)
     bias_full = jnp.transpose(bias_all[:, :2, :own_width], (1, 0, 2)).reshape(2, width)
     states, translated, low1 = layer(
         stream_low,
@@ -1292,8 +1432,7 @@
         fc_w.reshape(width, n_seq * hidden_rows),
         proj_w.reshape(n_seq * hidden_rows, width),
         out_w.reshape(plane_width, width),
-        trans_low.reshape(width, width),
-        trans_weight[1],
+        trans_weight,
         norm_gains,
         layer_biases,
         joined_bias,
@@ -1301,47 +1440,21 @@
         bias_full,
         turns,
     )
-    probe_low = (stream_low, low1)
-    gain_final = norm_gains[2]
     first, second, peaks, sums_part, cross_part = vocab_forward(states, unembed)
-    stats = jnp.concatenate([peaks[-1], jnp.sum(sums_part, axis=1), jnp.sum(cross_part, axis=1)], axis=0)
-    gathered = share(stats, "batch", 5, "share_stats")
-    peak_all = jnp.max(gathered[:, :3], axis=0)
-    fades = jnp.exp(gathered[:, :3] - peak_all)
-    sums_all = jnp.sum(gathered[:, 3:6] * fades, axis=0)
-    cross_all = jnp.sum(gathered[:, 6:] * fades[:, :1], axis=0)
-    log_totals = peak_all + jnp.log(sums_all)
-    diverge = cross_all / sums_all[0] - log_totals[0] + log_totals[1:]
-    loss_part = jnp.sum(weights * (diverge[0] + diverge[1]))
-    scales = weights * jnp.exp(peaks - log_totals[None])
-    dstates = vocab_backward(first, second, scales, unembed)
-    grad_list = []
-    bias_list = []
-    for index in range(2):
-        delta = norm_back(translated[index], dstates[index], gain_final)
-        grad_list.append(
-            jnp.einsum("td,te->de", probe_low[index], delta.astype(bf16), preferred_element_type=f32)
-        )
-        bias_list.append(jnp.sum(delta, axis=0))
-    grad = jnp.stack(grad_list).astype(bf16).reshape(2, n_seq, width // n_seq, width)
-    bias_grad = jnp.transpose(jnp.stack(bias_list).reshape(2, n_seq, width // n_seq), (1, 0, 2))
-    bias_grad = jnp.pad(bias_grad, ((0, 0), (0, 6), (0, LANES - width // n_seq)))
-    ones = jnp.ones((LANES,), f32) / LANES
-    note = jnp.concatenate(
-        [
-            jnp.zeros((1, LANES), f32),
-            (loss_part * ones)[None],
-            (jnp.sum(weights) * ones)[None],
-            jnp.zeros((5, LANES), f32),
-        ]
+    scales, note = statistics(tiles, peaks, sums_part, cross_part)
+    grad, bias_grad = vocab_backward(
+        first, second, scales, unembed, translated, stream_low, low1, norm_gains
     )
+    bias_grad = jnp.transpose(bias_grad.reshape(2, n_seq, own_width), (1, 0, 2))
+    bias_grad = jnp.pad(bias_grad, ((0, 0), (0, 6), (0, LANES - own_width)))
+    grad = grad.reshape(2, n_seq, own_width, width)
     grad_sum, bias_sum, notes = reduce_gradients(grad, bias_grad, note)
     sums = jnp.sum(notes, axis=(0, 2))
     loss_sum = sums[1]
     token_count = jnp.round(sums[2])
     grad_norm = jnp.sqrt(sums[0]) / token_count
     factor = jnp.minimum(1.0, clip_max / (grad_norm + 1e-06)) / token_count
-    grad_w = grad_sum.astype(f32).reshape(trans_weight.shape) * factor
+    grad_w = grad_sum.astype(f32) * factor
     grad_b = bias_sum[:2, : trans_bias.shape[1]] * factor
     first_w, second_w, new_w = adam_update(trans_weight, grad_w, mom1_weight, mom2_weight)
     first_b, second_b, new_b = adam_update(trans_bias, grad_b, mom1_bias, mom2_bias)

time: 414 us -> 357 us (0.86)
  Pallas kernels: 351 us -> 325 us
  other arithmetic: 24.2 us -> 7.04 us
  matrix products: 7.99 us -> 0 us
  local copies, waits for them, and re-layouts: 17.1 us -> 12.7 us
    pallas_call x1, Pallas kernels: 111 us -> 79.4 us  [layer(): pl.pallas_call(functools.partial(layer_kernel, count, own_heads), in_spec...]
    pallas_call x1, Pallas kernels: 36.3 us -> 50.3 us  [vocab_backward(): pl.pallas_call(functools.partial(backward_kernel, vocab), grid=(tiles + 1...]
    reduce_sum x10 -> x0, other arithmetic: 11.5 us -> none  [the longest x1 2.64 us: norm_back(): average = jnp.mean(values, axis=-1, keepdims=True)]
    dot_general x2 -> x0, matrix products: 7.99 us -> none  [body(): jnp.einsum('td,te->de', probe_low[index], delta.astype(bf16), preferred_e...]
    pallas_call x1, Pallas kernels: 56.3 us -> 51.8 us  [reduce_gradients(): pl.pallas_call(functools.partial(reduce_kernel, count), in_specs=[pl.Bloc...]
    pallas_call x1, Pallas kernels: 75.4 us -> 71.2 us  [front(): pl.pallas_call(functools.partial(front_kernel, count), in_specs=[vmem, an...]
where the time goes in v5:
time: 357 us; the launch traced here: 351 us
  Pallas kernels  325 us (91%)
  local copies, waits for them, and re-layouts  12.7 us (4%)
  other arithmetic  7.04 us (2%)
  between operations  5.48 us (2%)
    pallas_call x1, Pallas kernels, layer(): pl.pallas_call(functools.partial(layer_kernel, count, own_heads), in_spec...  79.4 us
    pallas_call x1, Pallas kernels, front(): pl.pallas_call(functools.partial(front_kernel, count), in_specs=[vmem, an...  71.2 us
    pallas_call x1, Pallas kernels, vocab_forward(): pl.pallas_call(functools.partial(forward_kernel, vocab), grid=(tiles + 1,...  65.4 us
    pallas_call x1, Pallas kernels, reduce_gradients(): pl.pallas_call(functools.partial(reduce_kernel, count), in_specs=[pl.Bloc...  51.8 us
    pallas_call x1, Pallas kernels, vocab_backward(): pl.pallas_call(functools.partial(backward_kernel, vocab), grid=(tiles + 1...  50.3 us
    pallas_call x1, Pallas kernels, statistics(): pl.pallas_call(stats_kernel, in_specs=[vmem] * 4, out_specs=[vmem] * 2, o...  7.26 us

profile of v5, /device:TPU:0, one launch (start us, length us, event | category | flops | bytes accessed | tf_op | source)
XLA Modules:
  0.0 350.6 jit_solution(12327803671250509321)
XLA Ops:
  1.3 0.1 pad.22.clone
  1.4 0.1 pad.23.clone
  1.5 0.1 pad.16.clone
  1.5 0.1 pad.19.clone
  1.6 1.3 add_add_fusion.tile_ref
  3.0 1.3 scatter.4.bias_ref
  4.2 0.1 multiply_cosine_fusion
  4.3 0.7 slice.57
  5.1 0.6 constant_dynamic-slice_fusion
  5.7 0.7 slice.59
  6.4 0.6 dynamic-slice_bitcast_fusion.fc_bias
  7.0 0.1 maximum_bitcast_fusion.1
  7.1 1.1 reshape.128
  8.2 0.1 copy.37
  8.3 0.9 reshape.129.joined_ref
  9.2 1.1 reshape.130
  10.3 0.8 reshape.131.fc_ref
  11.2 0.9 copy.32.turns_ref
  12.1 71.2 %front.1 = (s32[4,8,128]{2,1,0:T(8,128)}, bf16[512,1024]{1,0:T(8,128)(2,1)}, bf16[8,4,32,768]{3,2,1,0:T(8,128)(2,1)}, bf16[8,4,32,1024]{3,2,1,0:T(8,128)(2,1)}, ...) custom-call(s32[8,128]{1,0:T(8,128)} %add_add_fusion.tile_ref, ...), custom_call_target="tpu_custom_call" | custom-call | tf_op jit(solution)/shard_map/front/pallas_call | solution.py:785
  83.3 1.4 slice_bitcast_fusion.trans_bias
  84.7 79.4 %layer.1 = (bf16[3,512,1024]{2,1,0:T(8,128)(2,1)}, f32[2,512,1024]{2,1,0:T(8,128)}, bf16[512,1024]{1,0:T(8,128)(2,1)}) custom-call(bf16[512,1024]{1,0:T(8,128)(2,1)} %get-tuple-element.43.stream_ref.low0_ref, bf16[1024,768]{1,0:T(8,128)(2,1)} %bitcast.50, bf16[1024,1024]{1,0:T(8,128)(2,1)} %bitcast.47, bf16[1024,1024]{1,0:T(8,128)(2,1)} %bitcast.48, ...), custom_call_target="tpu_custom_call" | custom-call | tf_op jit(solution)/shard_map/layer/pallas_call | solution.py:1005
  164.1 65.4 %vocab_forward.1 = (bf16[10,3,1280,256]{3,2,1,0:T(8,128)(2,1)}, bf16[10,3,1280,256]{3,2,1,0:T(8,128)(2,1)}, f32[10,3,512]{2,1,0:T(4,128)}, f32[3,8,512]{2,1,0:T(8,128)}, f32[2,8,512]{2,1,0:T(8,128)}) custom-call(bf16[3,512,1024]{2,1,0:T(8,128)(2,1)} %get-tuple-element.49.states_ref, bf16[12576,1024]{1,0:T(8,128)(2,1)} %table_ref.5), custom_call_target="tpu_custom_call" | custom-call | flops 39560675328 | bytes 64389120 | tf_op jit(solution)/shard_map/vocab_forward/pallas_call | solution.py:179
  229.4 7.3 %statistics.1 = (f32[10,3,512]{2,1,0:T(4,128)}, f32[8,128]{1,0:T(8,128)}) custom-call(s32[4,8,128]{2,1,0:T(8,128)} %get-tuple-element.52.tiles_ref, f32[10,3,512]{2,1,0:T(4,128)} %get-tuple-element.53.peaks_ref, f32[3,8,512]{2,1,0:T(8,128)} %get-tuple-element.54.sums_ref, f32[2,8,512]{2,1,0:T(8,128)} %get-tuple-element.55.cross_ref), custom_call_target="tpu_custom_call" | custom-call | tf_op jit(solution)/shard_map/statistics/pallas_call | solution.py:1099
  236.7 50.3 %vocab_backward.1 = (bf16[2,1024,1024]{2,1,0:T(8,128)(2,1)}, f32[2,1024]{1,0:T(2,128)}) custom-call(bf16[10,3,1280,256]{3,2,1,0:T(8,128)(2,1)} %get-tuple-element.50.first_ref, bf16[10,3,1280,256]{3,2,1,0:T(8,128)(2,1)} %get-tuple-element.51.second_ref, f32[10,3,512]{2,1,0:T(4,128)} %get-tuple-element.56.scales_ref, bf16[12576,1024]{1,0:T(8,128)(2,1)} %table_ref.5, ...), custom_call_target="tpu_custom_call" | custom-call | flops 28521267200 | bytes 64389120 | tf_op jit(solution)/shard_map/vocab_backward/pallas_call | solution.py:319
  287.0 1.5 pad.7.bias_ref
  288.5 51.8 %reduce_gradients.1 = (bf16[256,1024]{1,0:T(8,128)(2,1)}, f32[8,128]{1,0:T(8,128)}, f32[8,8,128]{2,1,0:T(8,128)}) custom-call(bf16[2,8,128,1024]{3,2,1,0:T(8,128)(2,1)} %bitcast.45, f32[8,8,128]{2,1,0:T(8,128)} %pad.7.bias_ref, f32[8,128]{1,0:T(8,128)} %get-tuple-element.61.note_ref), custom_call_target="tpu_custom_call" | custom-call | tf_op jit(solution)/shard_map/reduce_gradients/pallas_call | solution.py:1313
  340.3 0.9 reduce_sum.9
  341.2 0.6 fusion.7
  343.3 1.3 multiply_subtract_fusion.1
  344.6 1.2 convert_multiply_fusion
  345.7 0.1 copy.33
  345.9 2.2 multiply_subtract_fusion
  (22 shorter events, 0.1 us)
Async XLA Ops:
  287.0 56.3 %copy-start.3 = (f32[2,128]{1,0:T(2,128)S(1)}, f32[2,128]{1,0:T(2,128)}, u32[]{:S(2)}) copy-start(f32[2,128]{1,0:T(2,128)} %param.33) | copy-start | bytes 3076
  287.0 56.3 %copy-start.4 = (f32[2,128]{1,0:T(2,128)S(1)}, f32[2,128]{1,0:T(2,128)}, u32[]{:S(2)}) copy-start(f32[2,128]{1,0:T(2,128)} %param.37) | copy-start | bytes 3076
  287.0 56.3 %copy-start.5 = (f32[2,128]{1,0:T(2,128)S(1)}, f32[2,128]{1,0:T(2,128)}, u32[]{:S(2)}) copy-start(f32[2,128]{1,0:T(2,128)} %param.36) | copy-start | bytes 3076
  287.0 58.9 %copy-start = (f32[2,128,1024]{2,1,0:T(8,128)S(1)}, f32[2,128,1024]{2,1,0:T(8,128)}, u32[]{:S(2)}) copy-start(f32[2,128,1024]{2,1,0:T(8,128)} %trans_ref.1) | copy-start | bytes 3145732
  287.0 58.9 %copy-start.1 = (f32[2,128,1024]{2,1,0:T(8,128)S(1)}, f32[2,128,1024]{2,1,0:T(8,128)}, u32[]{:S(2)}) copy-start(f32[2,128,1024]{2,1,0:T(8,128)} %param.35) | copy-start | bytes 3145732
  287.0 58.9 %copy-start.2 = (f32[2,128,1024]{2,1,0:T(8,128)S(1)}, f32[2,128,1024]{2,1,0:T(8,128)}, u32[]{:S(2)}) copy-start(f32[2,128,1024]{2,1,0:T(8,128)} %param.34) | copy-start | bytes 3145732

commit v6 on v5

--- a/solution.py
+++ b/solution.py
@@ -48,12 +48,13 @@
     return (earlier, later, weight * (1.0 - learn_rate * decay_rate) - learn_rate * update)
 
 
-def forward_kernel(vocab, states_ref, table_ref, first_ref, second_ref, peaks_ref, sums_ref, cross_ref, turned, left, right, peak):
+def forward_kernel(vocab, states_ref, table_ref, probe0_ref, probe1_ref, first_ref, second_ref, peaks_ref, sums_ref, cross_ref, turned, left, right, peak):
     step = pl.program_id(0)
     steps = pl.num_programs(0) - 1
     width = table_ref.shape[0]
-    half = left.shape[1] // 3
+    half = left.shape[1] // 2
     group = 16
+    given = (probe0_ref, probe1_ref)
     last = vocab - (pl.cdiv(vocab, width) - 1) * width
     row = lax.broadcasted_iota(jnp.int32, (group, LANES), 0)
 
@@ -66,20 +67,21 @@
     @pl.when(step == 0)
     def _():
         reset(0)
-        for state in range(3):
+        for state in range(2):
             for part in range(2):
                 turned[part, :, state * half : (state + 1) * half] = jnp.transpose(
-                    states_ref[state, part * half : (part + 1) * half, :]
+                    states_ref[2 * state, part * half : (part + 1) * half, :]
                 )
 
     @pl.when(step <= 1)
     def _():
         reset(1)
 
-    def multiply(part, target, state):
+    def multiply(part, target, state, cut):
         place = slice(state * half, (state + 1) * half)
-        target[:, place] = jnp.dot(
-            table_ref[...], turned[part, :, place], preferred_element_type=jnp.float32
+        at = slice(cut * width // 2, (cut + 1) * width // 2)
+        target[at, place] = jnp.dot(
+            table_ref[at, :], turned[part, :, place], preferred_element_type=jnp.float32
         )
 
     def units(part, source, target, tile):
@@ -92,8 +94,12 @@
             held = {}
 
             def logits(state, block, lanes=lanes):
-                begin = state * half + lanes * LANES
-                value = source[block * group : (block + 1) * group, begin : begin + LANES]
+                at = slice(block * group, (block + 1) * group)
+                if state == 1:
+                    value = given[part][0, at, lanes * LANES : (lanes + 1) * LANES]
+                else:
+                    begin = state // 2 * half + lanes * LANES
+                    value = source[at, begin : begin + LANES]
                 if (block + 1) * group > last:
                     value = jnp.where(row + block * group < limit, value, NEGATIVE)
                 return value
@@ -148,9 +154,9 @@
 
     def stage(part, target, work):
         done = 0
-        for state in range(3):
-            multiply(part, target, state)
-            upto = (state + 1) * len(work) // 3
+        for piece in range(4):
+            multiply(part, target, piece // 2, piece % 2)
+            upto = (piece + 1) * len(work) // 4
             for unit in work[done:upto]:
                 unit()
             done = upto
@@ -168,7 +174,7 @@
             unit()
 
 
-def vocab_forward(states, table):
+def vocab_forward(states, table, given):
     _, rows, depth = states.shape
     vocab = table.shape[0]
     tiles = pl.cdiv(vocab, VOCAB_TILE)
@@ -182,6 +188,8 @@
         in_specs=[
             whole(3, rows, depth),
             pl.BlockSpec((VOCAB_TILE, depth), lambda i: (jnp.minimum(i, tiles - 1), 0)),
+            pl.BlockSpec((1, VOCAB_TILE, half), lambda i: (jnp.minimum(i, tiles - 1), 0, 0)),
+            pl.BlockSpec((1, VOCAB_TILE, half), lambda i: (jnp.maximum(i - 1, 0), 0, 1)),
         ],
         out_specs=[
             pl.BlockSpec(block, lambda i: (jnp.minimum(i, tiles - 1), 0, 0, 0)),
@@ -198,19 +206,19 @@
             jax.ShapeDtypeStruct((2, 8, rows), jnp.float32),
         ],
         scratch_shapes=[
-            pltpu.VMEM((2, depth, 3 * half), jnp.bfloat16),
-            pltpu.VMEM((VOCAB_TILE, 3 * half), jnp.float32),
-            pltpu.VMEM((VOCAB_TILE, 3 * half), jnp.float32),
+            pltpu.VMEM((2, depth, 2 * half), jnp.bfloat16),
+            pltpu.VMEM((VOCAB_TILE, 2 * half), jnp.float32),
+            pltpu.VMEM((VOCAB_TILE, 2 * half), jnp.float32),
             pltpu.VMEM((8, rows), jnp.float32),
         ],
         compiler_params=pltpu.CompilerParams(vmem_limit_bytes=VMEM_BYTES),
         cost_estimate=pl.CostEstimate(
-            flops=6 * rows * depth * vocab,
-            bytes_accessed=2 * vocab * (depth + 3 * rows),
+            flops=4 * rows * depth * vocab,
+            bytes_accessed=2 * vocab * (depth + 5 * rows),
             transcendentals=3 * rows * vocab,
         ),
         name="vocab_forward",
-    )(states, table)
+    )(states, table, given, given)
 
 
 def backward_kernel(
@@ -300,7 +308,7 @@
                 return total + jnp.sum(value, axis=0, keepdims=True)
 
             bias_ref[probe : probe + 1, :] = lax.fori_loop(
-                0, rows // chunk, back, jnp.zeros((1, depth), jnp.float32)
+                0, rows // chunk, back, jnp.zeros((1, depth), jnp.float32), unroll=4
             )
             turned[...] = jnp.transpose(low_ref[...])
             for begin in range(0, depth, block):
@@ -695,23 +703,20 @@
     half = total_rows // 2
     lane = lax.broadcasted_iota(jnp.int32, (half, LANES), 1)
 
-    def look(part):
+    def look(part, cut):
         at = slice(part * half, (part + 1) * half)
-        for cut in range(cuts):
-            if part == 0:
-                table_copies[cut].wait()
-            for block in range(width // LANES):
-                number_ = (lane + (cut * width + block * LANES)).astype(jnp.float32)
-                chosen[:, block * LANES : (block + 1) * LANES] = jnp.where(
-                    column_ids[at, :] == number_, 1.0, 0.0
-                ).astype(jnp.bfloat16)
-            found = jnp.dot(
-                chosen[...], table[cut * width : (cut + 1) * width, :], preferred_element_type=jnp.float32
-            )
-            if cut == 0:
-                picked[at, :] = found
-            else:
-                picked[at, :] += found
+        if part == 0:
+            table_copies[cut].wait()
+        for block in range(width // LANES):
+            number_ = (lane + (cut * width + block * LANES)).astype(jnp.float32)
+            chosen[:, block * LANES : (block + 1) * LANES] = jnp.where(
+                column_ids[at, :] == number_, 1.0, 0.0
+            ).astype(jnp.bfloat16)
+        found = jnp.dot(chosen[...], table[cut * width : (cut + 1) * width, :], preferred_element_type=jnp.float32)
+        if cut == 0:
+            picked[at, :] = found
+        else:
+            picked[at, :] += found
 
     line_sum = LineSum(
         count, chunk, lambda at: picked[at, :],
@@ -734,29 +739,37 @@
 
         plane.own(3)
 
+    between = {
+        (0, 0): lambda: turn(0),
+        (0, 1): lambda: plane.relay_side(2),
+        (0, 3): lambda: turn(1),
+        (0, 4): lambda: turn_out(),
+        (0, 5): lambda: plane.relay_core(2),
+        (0, 7): lambda: plane.relay_side(0),
+    }
+    for part in range(2):
+        for cut in range(cuts):
+            if (part, cut) in between:
+                between.pop((part, cut))()
+            look(part, cut)
+        for work in [between.pop(key) for key in list(between) if key[0] == part]:
+            work()
+        line_sum.begin(range(part * count // 2, (part + 1) * count // 2))
     todo = [
-        lambda: turn(0),
-        lambda: (plane.relay_side(2), turn(1)),
-        lambda: (turn_out(), plane.relay_core(2)),
-        lambda: plane.relay_side(0),
-        lambda: None,
         lambda: plane.relay_core(0),
         lambda: None,
         lambda: plane.relay_side(1),
         lambda: plane.relay_side(3),
         lambda: None,
+        lambda: None,
         lambda: plane.relay_core(1),
+        lambda: plane.relay_core(3),
         lambda: None,
-        lambda: plane.relay_core(3),
         lambda: plane.receive_core(2),
         lambda: plane.receive_core(0),
         lambda: plane.receive_core(1),
         lambda: plane.receive_core(3),
     ]
-    for part in range(2):
-        look(part)
-        line_sum.begin(range(part * count // 2, (part + 1) * count // 2))
-        todo.pop(0)()
     line_sum.run(3, todo)
     for peer in peers:
         arrived(bias_out.at[peer], bias_receive.at[peer], {"seq": peer})
@@ -828,10 +841,11 @@
 def layer_kernel(
     count, heads,
     stream_ref, joined_ref, fc_ref, proj_ref, out_ref, trans_ref,
-    gains_ref, offsets_ref, joined_bias, fc_bias, trans_bias, turns_ref,
-    states_ref, moved_ref, low_ref,
+    gains_ref, offsets_ref, joined_bias, fc_bias, trans_bias, turns_ref, table_ref,
+    states_ref, moved_ref, low_ref, logits_ref,
     first_trans, second_trans, x_attn, x_mlp, spread, gathered, mixed, returned, part,
-    land, held, total, inner_sem, outer_sem, receive_sem,
+    land, inner_sem, outer_sem, receive_sem,
+    tables, turned, logits, table_sem, logits_sem,
     local_sem, heads_send, heads_receive, rows_send, rows_receive, plane_send, plane_receive,
 ):
     f32 = jnp.float32
@@ -850,6 +864,38 @@
     head_dim = columns // heads
     step_rows = 32
 
+    vocab = table_ref.shape[0]
+    cut_rows = tables.shape[1]
+    cuts = pl.cdiv(vocab, cut_rows)
+    sizes = [min(cut_rows, vocab - cut * cut_rows) for cut in range(cuts)]
+    loads = [
+        pltpu.make_async_copy(
+            table_ref.at[pl.ds(cut * cut_rows, sizes[cut])],
+            tables.at[cut % 2, pl.ds(0, sizes[cut])],
+            table_sem.at[cut % 2],
+        )
+        for cut in range(cuts)
+    ]
+    stores = [
+        pltpu.make_async_copy(
+            logits.at[cut % 2],
+            logits_ref.at[cut * cut_rows // VOCAB_TILE, pl.ds(cut * cut_rows % VOCAB_TILE, cut_rows)],
+            logits_sem.at[cut % 2],
+        )
+        for cut in range(cuts)
+    ]
+    loads[0].start()
+    loads[1].start()
+
+    def probe_logits(cut):
+        loads[cut].wait()
+        if cut >= 2:
+            stores[cut - 2].wait()
+        logits[cut % 2] = jnp.dot(tables[cut % 2], turned[...], preferred_element_type=f32)
+        stores[cut].start()
+        if cut + 2 < cuts:
+            loads[cut + 2].start()
+
     spans = (first_trans, second_trans)
     for probe in range(2):
         spans[probe][spot] = trans_ref[probe].astype(bf16)
@@ -868,7 +914,7 @@
         x_mlp[at, :] = (unit * gains_ref[1:2, :] + offsets_ref[1:2, :]).astype(bf16)
         return carry
 
-    lax.fori_loop(0, rows // step_rows, norms, 0)
+    lax.fori_loop(0, rows // step_rows, norms, 0, unroll=4)
     half_rot = ROT // 2
     for sequence in range(lines):
         at = slice(sequence * tokens, (sequence + 1) * tokens)
@@ -916,6 +962,7 @@
         translate(0, low.astype(f32), low, first_trans[...].reshape(depth, depth), at)
 
     plane.relay_side(0)
+    plane.relay_core(0)
     heads_copy.wait()
     for peer in peers:
         arrived(gathered.at[peer], heads_receive.at[peer], {"seq": peer})
@@ -951,8 +998,11 @@
         )
     rows_copy = pltpu.make_async_copy(mixed.at[spot], returned.at[spot], local_sem.at[1])
     rows_copy.start()
-    plane.relay_core(0)
     plane.relay_side(1)
+    plane.receive_core(0)
+    for sequence in range(lines):
+        first_probe(sequence)
+    turned[...] = jnp.transpose(states_ref[1])
     rows_copy.wait()
     for peer in peers:
         arrived(returned.at[peer], rows_receive.at[peer], {"seq": peer})
@@ -964,18 +1014,18 @@
         part[at, :] += jnp.dot(attended, out_ref[...], preferred_element_type=f32)
     line_sum = LineSum(
         count, rows // count, lambda at: part[at, :],
-        land, held, total, inner_sem, outer_sem, receive_sem,
+        land, x_attn, x_mlp, inner_sem, outer_sem, receive_sem,
     )
     line_sum.begin(range(count))
-    todo = [lambda: None, lambda: plane.relay_core(1), lambda: plane.receive_core(0)]
-    todo += [functools.partial(first_probe, sequence) for sequence in range(lines)]
-    todo += [lambda: plane.receive_core(1)]
+    todo = [functools.partial(probe_logits, cut) for cut in range(cuts)]
+    todo[3:3] = [lambda: plane.relay_core(1)]
+    todo[7:7] = [lambda: plane.receive_core(1)]
     line_sum.run(3, todo)
 
     def second_probe(index, carry):
         at = pl.ds(pl.multiple_of(index * tokens, tokens), tokens)
         stream = (
-            stream_ref[at, :].astype(f32) + total[at, :].astype(f32) + offsets_ref[2:3, :] + offsets_ref[3:4, :]
+            stream_ref[at, :].astype(f32) + x_mlp[at, :].astype(f32) + offsets_ref[2:3, :] + offsets_ref[3:4, :]
         )
         states_ref[0, at, :] = (row_norm(stream) * gains_ref[2:3, :] + offsets_ref[4:5, :]).astype(bf16)
         low = stream.astype(bf16)
@@ -986,11 +1036,13 @@
     lax.fori_loop(0, lines, second_probe, 0)
     for copy in sent:
         copy.wait_send()
+    for copy in stores[-2:]:
+        copy.wait()
     plane.finish()
     line_sum.finish()
 
 
-def layer(stream, joined, fc, proj, out, trans, gains, offsets, joined_bias, fc_bias, trans_bias, turns):
+def layer(stream, joined, fc, proj, out, trans, gains, offsets, joined_bias, fc_bias, trans_bias, turns, table):
     size = lax.axis_size("seq")
     lines = lax.axis_size("batch")
     rows, depth = stream.shape
@@ -998,18 +1050,21 @@
     own_heads = depth // HEAD_DIM // size
     columns = own_heads * HEAD_DIM
     count = 16
+    tiles = pl.cdiv(table.shape[0], VOCAB_TILE)
     bf16 = jnp.bfloat16
     f32 = jnp.float32
     vmem = pl.BlockSpec(memory_space=pltpu.VMEM)
+    anywhere = pl.BlockSpec(memory_space=pl.ANY)
     dma = pltpu.SemaphoreType.DMA
     return pl.pallas_call(
         functools.partial(layer_kernel, count, own_heads),
-        in_specs=[vmem] * 12,
-        out_specs=[vmem] * 3,
+        in_specs=[vmem] * 12 + [anywhere],
+        out_specs=[vmem] * 3 + [anywhere],
         out_shape=[
             jax.ShapeDtypeStruct((3, rows, depth), bf16),
             jax.ShapeDtypeStruct((2, rows, depth), f32),
             jax.ShapeDtypeStruct((rows, depth), bf16),
+            jax.ShapeDtypeStruct((tiles, VOCAB_TILE, rows), f32),
         ],
         scratch_shapes=[
             pltpu.VMEM((size,) + trans.shape[1:], bf16),
@@ -1021,9 +1076,12 @@
             pltpu.VMEM((size, tokens, columns), bf16),
             pltpu.VMEM((size, tokens, columns), bf16),
             pltpu.VMEM((rows, depth), f32),
-        ] + LineSum.scratch(count, rows, depth)[:2] + [
-            pltpu.VMEM((rows, depth), bf16),
-        ] + LineSum.scratch(count, rows, depth)[2:] + [
+        ] + LineSum.scratch(count, rows, depth)[:1] + LineSum.scratch(count, rows, depth)[2:] + [
+            pltpu.VMEM((2, VOCAB_TILE // 2, depth), bf16),
+            pltpu.VMEM((depth, rows), bf16),
+            pltpu.VMEM((2, VOCAB_TILE // 2, rows), f32),
+            dma((2,)),
+            dma((2,)),
             dma((2,)),
             dma((size - 1,)),
             dma((size,)),
@@ -1034,7 +1092,7 @@
             collective_id=2, has_side_effects=True, vmem_limit_bytes=VMEM_BYTES
         ),
         name="layer",
-    )(stream, joined, fc, proj, out, trans, gains, offsets, joined_bias, fc_bias, trans_bias, turns)
+    )(stream, joined, fc, proj, out, trans, gains, offsets, joined_bias, fc_bias, trans_bias, turns, table)
 
 
 def stats_kernel(
@@ -1426,7 +1484,7 @@
         tile, embed_in, joined_cut, fc_cut, w_proj, w_out, bias_tile
     )
     bias_full = jnp.transpose(bias_all[:, :2, :own_width], (1, 0, 2)).reshape(2, width)
-    states, translated, low1 = layer(
+    states, translated, low1, probe_logits = layer(
         stream_low,
         joined_w.reshape(width, 3 * plane_width),
         fc_w.reshape(width, n_seq * hidden_rows),
@@ -1439,8 +1497,9 @@
         fc_bias,
         bias_full,
         turns,
+        unembed,
     )
-    first, second, peaks, sums_part, cross_part = vocab_forward(states, unembed)
+    first, second, peaks, sums_part, cross_part = vocab_forward(states, unembed, probe_logits)
     scales, note = statistics(tiles, peaks, sums_part, cross_part)
     grad, bias_grad = vocab_backward(
         first, second, scales, unembed, translated, stream_low, low1, norm_gains

time: 357 us -> 349 us (0.978)
  Pallas kernels: 325 us -> 317 us
    pallas_call x1, Pallas kernels: 65.4 us -> 54.1 us  [vocab_forward(): pl.pallas_call(functools.partial(forward_kernel, vocab), grid=(tiles + 1,...]
    pallas_call x1, Pallas kernels: 79.4 us -> 87.3 us  [layer(): pl.pallas_call(functools.partial(layer_kernel, count, own_heads), in_spec...]
    pallas_call x1, Pallas kernels: 50.3 us -> 44 us  [vocab_backward(): pl.pallas_call(functools.partial(backward_kernel, vocab), grid=(tiles + 1...]
where the time goes in v6:
time: 349 us; the launch traced here: 343 us
  Pallas kernels  317 us (91%)
  local copies, waits for them, and re-layouts  12.8 us (4%)
  other arithmetic  7.05 us (2%)
  between operations  5.65 us (2%)
    pallas_call x1, Pallas kernels, layer(): pl.pallas_call(functools.partial(layer_kernel, count, own_heads), in_spec...  87.3 us
    pallas_call x1, Pallas kernels, front(): pl.pallas_call(functools.partial(front_kernel, count), in_specs=[vmem, an...  72 us
    pallas_call x1, Pallas kernels, vocab_forward(): pl.pallas_call(functools.partial(forward_kernel, vocab), grid=(tiles + 1,...  54.1 us
    pallas_call x1, Pallas kernels, reduce_gradients(): pl.pallas_call(functools.partial(reduce_kernel, count), in_specs=[pl.Bloc...  52.6 us
    pallas_call x1, Pallas kernels, vocab_backward(): pl.pallas_call(functools.partial(backward_kernel, vocab), grid=(tiles + 1...  44 us
    pallas_call x1, Pallas kernels, statistics(): pl.pallas_call(stats_kernel, in_specs=[vmem] * 4, out_specs=[vmem] * 2, o...  7.24 us

profile of v6, /device:TPU:0, one launch (start us, length us, event | category | flops | bytes accessed | tf_op | source)
XLA Modules:
  0.0 342.7 jit_solution(3012597216872392777)
XLA Ops:
  1.3 0.1 pad.22.clone
  1.4 0.1 pad.23.clone
  1.5 0.1 pad.16.clone
  1.5 0.1 pad.19.clone
  1.6 1.3 add_add_fusion.tile_ref
  3.0 1.3 scatter.4.bias_ref
  4.2 0.1 multiply_cosine_fusion
  4.3 0.7 slice.57
  5.1 0.6 constant_dynamic-slice_fusion
  5.7 0.7 slice.59
  6.4 0.6 dynamic-slice_bitcast_fusion.fc_bias
  7.0 0.1 maximum_bitcast_fusion.1
  7.1 1.1 reshape.128
  8.2 0.1 copy.37
  8.3 0.9 reshape.129.joined_ref
  9.2 1.1 reshape.130
  10.3 0.8 reshape.131.fc_ref
  11.2 0.9 copy.32.turns_ref
  12.1 72.0 %front.1 = (s32[4,8,128]{2,1,0:T(8,128)}, bf16[512,1024]{1,0:T(8,128)(2,1)}, bf16[8,4,32,768]{3,2,1,0:T(8,128)(2,1)}, bf16[8,4,32,1024]{3,2,1,0:T(8,128)(2,1)}, ...) custom-call(s32[8,128]{1,0:T(8,128)} %add_add_fusion.tile_ref, ...), custom_call_target="tpu_custom_call" | custom-call | tf_op jit(solution)/shard_map/front/pallas_call | solution.py:798
  84.1 1.4 slice_bitcast_fusion.trans_bias
  85.5 87.3 %layer.1 = (bf16[3,512,1024]{2,1,0:T(8,128)(2,1)}, f32[2,512,1024]{2,1,0:T(8,128)}, bf16[512,1024]{1,0:T(8,128)(2,1)}, f32[10,1280,512]{2,1,0:T(8,128)}) custom-call(bf16[512,1024]{1,0:T(8,128)(2,1)} %get-tuple-element.44.stream_ref.low0_ref, bf16[1024,768]{1,0:T(8,128)(2,1)} %bitcast.49, bf16[1024,1024]{1,0:T(8,128)(2,1)} %bitcast.47, ...), custom_call_target="tpu_custom_call" | custom-call | tf_op jit(solution)/shard_map/layer/pallas_call | solution.py:1059
  172.7 54.1 %vocab_forward.1 = (bf16[10,3,1280,256]{3,2,1,0:T(8,128)(2,1)}, bf16[10,3,1280,256]{3,2,1,0:T(8,128)(2,1)}, f32[10,3,512]{2,1,0:T(4,128)}, f32[3,8,512]{2,1,0:T(8,128)}, f32[2,8,512]{2,1,0:T(8,128)}) custom-call(bf16[3,512,1024]{2,1,0:T(8,128)(2,1)} %get-tuple-element.50.states_ref, bf16[12576,1024]{1,0:T(8,128)(2,1)} %table_ref.7, ...), custom_call_target="tpu_custom_call" | custom-call | flops 26373783552 | bytes 90144768 | tf_op jit(solution)/shard_map/vocab_forward/pallas_call | solution.py:185
  226.9 7.2 %statistics.1 = (f32[10,3,512]{2,1,0:T(4,128)}, f32[8,128]{1,0:T(8,128)}) custom-call(s32[4,8,128]{2,1,0:T(8,128)} %get-tuple-element.54.tiles_ref, f32[10,3,512]{2,1,0:T(4,128)} %get-tuple-element.55.peaks_ref, f32[3,8,512]{2,1,0:T(8,128)} %get-tuple-element.56.sums_ref, f32[2,8,512]{2,1,0:T(8,128)} %get-tuple-element.57.cross_ref), custom_call_target="tpu_custom_call" | custom-call | tf_op jit(solution)/shard_map/statistics/pallas_call | solution.py:1157
  234.1 44.0 %vocab_backward.1 = (bf16[2,1024,1024]{2,1,0:T(8,128)(2,1)}, f32[2,1024]{1,0:T(2,128)}) custom-call(bf16[10,3,1280,256]{3,2,1,0:T(8,128)(2,1)} %get-tuple-element.52.first_ref, bf16[10,3,1280,256]{3,2,1,0:T(8,128)(2,1)} %get-tuple-element.53.second_ref, f32[10,3,512]{2,1,0:T(4,128)} %get-tuple-element.58.scales_ref, bf16[12576,1024]{1,0:T(8,128)(2,1)} %table_ref.7, ...), custom_call_target="tpu_custom_call" | custom-call | flops 28521267200 | bytes 64389120 | tf_op jit(solution)/shard_map/vocab_backward/pallas_call | solution.py:327
  278.2 1.5 pad.7.bias_ref
  279.6 52.6 %reduce_gradients.1 = (bf16[256,1024]{1,0:T(8,128)(2,1)}, f32[8,128]{1,0:T(8,128)}, f32[8,8,128]{2,1,0:T(8,128)}) custom-call(bf16[2,8,128,1024]{3,2,1,0:T(8,128)(2,1)} %bitcast.45, f32[8,8,128]{2,1,0:T(8,128)} %pad.7.bias_ref, f32[8,128]{1,0:T(8,128)} %get-tuple-element.63.note_ref), custom_call_target="tpu_custom_call" | custom-call | tf_op jit(solution)/shard_map/reduce_gradients/pallas_call | solution.py:1371
  332.2 0.9 reduce_sum.9
  333.1 0.6 fusion.7
  335.2 1.3 multiply_subtract_fusion.1
  336.5 1.2 convert_multiply_fusion
  337.6 0.1 copy.33
  337.8 2.2 multiply_subtract_fusion
  (22 shorter events, 0.1 us)
Async XLA Ops:
  278.1 57.1 %copy-start.3 = (f32[2,128]{1,0:T(2,128)S(1)}, f32[2,128]{1,0:T(2,128)}, u32[]{:S(2)}) copy-start(f32[2,128]{1,0:T(2,128)} %param.33) | copy-start | bytes 3076
  278.1 57.1 %copy-start.4 = (f32[2,128]{1,0:T(2,128)S(1)}, f32[2,128]{1,0:T(2,128)}, u32[]{:S(2)}) copy-start(f32[2,128]{1,0:T(2,128)} %param.37) | copy-start | bytes 3076
  278.1 57.1 %copy-start.5 = (f32[2,128]{1,0:T(2,128)S(1)}, f32[2,128]{1,0:T(2,128)}, u32[]{:S(2)}) copy-start(f32[2,128]{1,0:T(2,128)} %param.36) | copy-start | bytes 3076
  278.1 59.6 %copy-start = (f32[2,128,1024]{2,1,0:T(8,128)S(1)}, f32[2,128,1024]{2,1,0:T(8,128)}, u32[]{:S(2)}) copy-start(f32[2,128,1024]{2,1,0:T(8,128)} %trans_ref.1) | copy-start | bytes 3145732
  278.1 59.6 %copy-start.1 = (f32[2,128,1024]{2,1,0:T(8,128)S(1)}, f32[2,128,1024]{2,1,0:T(8,128)}, u32[]{:S(2)}) copy-start(f32[2,128,1024]{2,1,0:T(8,128)} %param.35) | copy-start | bytes 3145732
  278.1 59.6 %copy-start.2 = (f32[2,128,1024]{2,1,0:T(8,128)S(1)}, f32[2,128,1024]{2,1,0:T(8,128)}, u32[]{:S(2)}) copy-start(f32[2,128,1024]{2,1,0:T(8,128)} %param.34) | copy-start | bytes 3145732

commit v7 on v6

--- a/solution.py
+++ b/solution.py
@@ -1,4 +1,5 @@
 import functools
+import math
 
 import jax
 import jax.numpy as jnp
@@ -15,7 +16,7 @@
 VOCAB_TILE = 1280
 LANES = 128
 NEGATIVE = -1e30
-VMEM_BYTES = 60 * 1024 * 1024
+VMEM_BYTES = 62 * 1024 * 1024
 norm_eps = 1e-05
 clip_max = 0.001
 beta_one = 0.9
@@ -79,7 +80,7 @@
 
     def multiply(part, target, state, cut):
         place = slice(state * half, (state + 1) * half)
-        at = slice(cut * width // 2, (cut + 1) * width // 2)
+        at = slice(cut * width // 5, (cut + 1) * width // 5)
         target[at, place] = jnp.dot(
             table_ref[at, :], turned[part, :, place], preferred_element_type=jnp.float32
         )
@@ -144,7 +145,7 @@
                     cross_ref[other, :, span] = held["cross"][other]
 
             result.append(tops)
-            cuts = 5
+            cuts = 10
             for cut in range(cuts):
                 result.append(
                     functools.partial(powers, cut * blocks // cuts, (cut + 1) * blocks // cuts)
@@ -154,9 +155,9 @@
 
     def stage(part, target, work):
         done = 0
-        for piece in range(4):
-            multiply(part, target, piece // 2, piece % 2)
-            upto = (piece + 1) * len(work) // 4
+        for piece in range(10):
+            multiply(part, target, piece // 5, piece % 5)
+            upto = (piece + 1) * len(work) // 10
             for unit in work[done:upto]:
                 unit()
             done = upto
@@ -412,11 +413,13 @@
 
 
 class LineSum:
-    def __init__(self, count, size, own, land, held, total, inner_sem, outer_sem, receive_sem):
+    def __init__(self, count, halves, own, land, held, total, inner_sem, outer_sem, receive_sem):
         lines = lax.axis_size("batch")
+        rows, depth = held.shape
+        self.blocks = count // halves
         place = lax.axis_index("batch")
         near = place < lines // 2
-        self.count, self.size = count, size
+        self.count, self.size, self.columns = count, rows // self.blocks, depth // halves
         self.own, self.land, self.held, self.total = own, land, held, total
         self.inner_sem, self.outer_sem, self.receive_sem = inner_sem, outer_sem, receive_sem
         self.middle = (place == lines // 2 - 1) | (place == lines // 2)
@@ -426,13 +429,16 @@
         self.slot = jnp.where(self.middle, 1, 0)
 
     def rows(self, index):
-        return pl.ds(index * self.size, self.size)
+        return (
+            pl.ds(index % self.blocks * self.size, self.size),
+            pl.ds(index // self.blocks * self.columns, self.columns),
+        )
 
     def send_in(self, index):
         rows = self.rows(index)
         push(
-            self.held.at[rows],
-            self.land.at[self.slot, rows],
+            self.held.at[*rows],
+            self.land.at[self.slot, *rows],
             self.inner_sem.at[index],
             self.receive_sem.at[self.slot, index],
             self.inner,
@@ -443,7 +449,7 @@
         def _():
             for index in indices:
                 rows = self.rows(index)
-                self.held[rows, :] = self.own(rows).astype(jnp.bfloat16)
+                self.held[rows] = self.own(rows).astype(jnp.bfloat16)
                 self.send_in(index)
 
     def gather(self, index):
@@ -451,9 +457,9 @@
 
         @pl.when(jnp.logical_not(self.end))
         def _():
-            arrived(self.land.at[0, rows], self.receive_sem.at[0, index], self.outer)
+            arrived(self.land.at[0, *rows], self.receive_sem.at[0, index], self.outer)
             own = self.own(rows).astype(jnp.float32)
-            self.held[rows, :] = (own + self.land[0, rows, :].astype(jnp.float32)).astype(jnp.bfloat16)
+            self.held[rows] = (own + self.land[(0, *rows)].astype(jnp.float32)).astype(jnp.bfloat16)
             self.send_in(index)
 
     def spread(self, index):
@@ -461,19 +467,19 @@
 
         @pl.when(self.middle)
         def _():
-            arrived(self.land.at[1, rows], self.receive_sem.at[1, index], self.inner)
-            both = self.held[rows, :].astype(jnp.float32) + self.land[1, rows, :].astype(jnp.float32)
-            self.total[rows, :] = both.astype(jnp.bfloat16)
+            arrived(self.land.at[1, *rows], self.receive_sem.at[1, index], self.inner)
+            both = self.held[rows].astype(jnp.float32) + self.land[(1, *rows)].astype(jnp.float32)
+            self.total[rows] = both.astype(jnp.bfloat16)
 
         @pl.when(jnp.logical_not(self.middle))
         def _():
-            arrived(self.total.at[rows], self.receive_sem.at[2, index], self.inner)
+            arrived(self.total.at[*rows], self.receive_sem.at[2, index], self.inner)
 
         @pl.when(jnp.logical_not(self.end))
         def _():
             push(
-                self.total.at[rows],
-                self.total.at[rows],
+                self.total.at[*rows],
+                self.total.at[*rows],
                 self.outer_sem.at[index],
                 self.receive_sem.at[2, index],
                 self.outer,
@@ -494,11 +500,11 @@
     def finish(self):
         for index in range(self.count):
             rows = self.rows(index)
-            departed(self.held.at[rows], self.inner_sem.at[index], self.inner)
+            departed(self.held.at[*rows], self.inner_sem.at[index], self.inner)
 
             @pl.when(jnp.logical_not(self.end))
             def _(rows=rows, index=index):
-                departed(self.total.at[rows], self.outer_sem.at[index], self.outer)
+                departed(self.total.at[*rows], self.outer_sem.at[index], self.outer)
 
     @staticmethod
     def scratch(count, rows, depth):
@@ -592,9 +598,9 @@
 
 def front_kernel(
     count,
-    tile_ref, table_ref, joined_ref, fc_ref, proj_ref, out_ref, bias_ref,
-    tiles_out, stream_ref, joined_out, fc_out, proj_out, out_out, bias_out,
-    table, column_ids, chosen, picked,
+    ids_ref, weights_ref, padding_ref, table_ref, joined_ref, fc_ref, trans_ref, out_ref, trans_bias_ref,
+    tiles_out, stream_ref, joined_out, fc_out, trans_out, out_out, bias_out,
+    table, column_ids, chosen, picked, tile_ref, bias_ref, trans_low,
     land, held, inner_sem, outer_sem, receive_sem,
     local_sem, table_sem, tile_send, tile_receive, cross_send, cross_receive, plane_send, plane_receive, bias_send, bias_receive,
 ):
@@ -604,10 +610,11 @@
     spot = lax.axis_index("seq")
     planes = others("batch")
     peers = others("seq")
-    outs = (joined_out, fc_out, proj_out, out_out)
+    outs = (joined_out, fc_out, trans_out, out_out)
     total_rows, depth = stream_ref.shape
-    chunk = total_rows // count
     tokens = tile_ref.shape[1]
+    plane_width = joined_out.shape[3] // 3
+    hidden_rows = fc_out.shape[3] // size
     vocab = table_ref.shape[0]
     number = spot * lines + place
     goal = {"seq": lax.rem(number, size), "batch": number // size}
@@ -622,7 +629,7 @@
         return lambda half, slot: out.at[slot, :, pl.ds(half * (depth // 2), depth // 2)]
 
     plane = PlaneGather([view(array) for array in range(4)], plane_send, plane_receive)
-    width = chosen.shape[1]
+    width = VOCAB_TILE
     cuts = table.shape[0] // width
     table_copies = [
         pltpu.make_async_copy(
@@ -636,21 +643,49 @@
         copy.start()
     if table.shape[0] > vocab:
         table[vocab:, :] = jnp.zeros((table.shape[0] - vocab, depth), table.dtype)
+
+    def joined_cuts(goal):
+        return [
+            (
+                joined_ref.at[:, pl.ds(pl.multiple_of(part * depth + goal * plane_width, LANES), plane_width)],
+                joined_out.at[spot, place, :, pl.ds(part * plane_width, plane_width)],
+            )
+            for part in range(3)
+        ]
+
+    def fc_cuts(goal):
+        if len(fc_ref.shape) == 3:
+            return [(fc_ref.at[goal], fc_out.at[spot, place])]
+        return [
+            (
+                fc_ref.at[:, pl.ds(pl.multiple_of((part * lines + goal) * hidden_rows, LANES), hidden_rows)],
+                fc_out.at[spot, place, :, pl.ds(part * hidden_rows, hidden_rows)],
+            )
+            for part in range(size)
+        ]
+
+    trans_low[...] = trans_ref[0].astype(jnp.bfloat16)
+    tile_ref[...] = jnp.zeros_like(tile_ref)
+    tile_ref[0:1, :] = ids_ref[...]
+    tile_ref[1:2, :] = weights_ref[...]
+    tile_ref[2:3, :] = jnp.full((1, tokens), padding_ref[0], jnp.int32)
+    bias_ref[...] = jnp.zeros_like(bias_ref)
+    bias_ref[0:2, 0 : trans_bias_ref.shape[1]] = trans_bias_ref[...]
     locals_ = [
         pltpu.make_async_copy(source, target, local_sem.at[index])
         for index, (source, target) in enumerate(
-            (
-                (proj_ref, proj_out.at[spot]),
-                (joined_ref.at[place], joined_out.at[spot, place]),
-                (fc_ref.at[place], fc_out.at[spot, place]),
+            [
+                (trans_low, trans_out.at[spot]),
                 (tile_ref, tiles_out.at[place]),
                 (bias_ref, bias_out.at[spot]),
-            )
+            ]
+            + joined_cuts(place)
+            + fc_cuts(place)
         )
     ]
     for copy in locals_:
         copy.start()
-    out_copy = pltpu.make_async_copy(out_ref, out_out.at[spot], local_sem.at[5])
+    out_copy = pltpu.make_async_copy(out_ref, out_out.at[spot], local_sem.at[6 + size])
 
     @pl.when(stays)
     def _():
@@ -672,12 +707,10 @@
     ]
     locals_[0].wait()
     plane.own(2)
-    crossing = []
-    for array, source, out in ((0, joined_ref, joined_out), (1, fc_ref, fc_out)):
+    for array, cuts_of in ((0, joined_cuts), (1, fc_cuts)):
         for index, other in enumerate(planes):
-            crossing.append(
-                push(source.at[other], out.at[spot, place], cross_send.at[array, index], cross_receive.at[array, place], {"batch": other})
-            )
+            for source, target in cuts_of(other):
+                push(source, target, cross_send.at[array, index], cross_receive.at[array, place], {"batch": other})
     out_push = pltpu.make_async_remote_copy(
         src_ref=out_ref, dst_ref=out_out.at[goal["seq"]], send_sem=cross_send.at[2, 0],
         recv_sem=cross_receive.at[2, 0], device_id=goal, device_id_type=pl.DeviceIdType.MESH,
@@ -700,26 +733,30 @@
         column_ids[sequence * tokens : (sequence + 1) * tokens, :] = jnp.broadcast_to(
             turned[:, 0:1] - (place * vocab).astype(jnp.float32), (tokens, LANES)
         )
-    half = total_rows // 2
-    lane = lax.broadcasted_iota(jnp.int32, (half, LANES), 1)
+    lane = lax.broadcasted_iota(jnp.int32, (total_rows, LANES), 1)
+
+    def choose(cut):
+        for block in range(width // LANES):
+            begin = cut * width + block * LANES
+            chosen[:, begin : begin + LANES] = jnp.where(
+                column_ids[...] == (lane + begin).astype(jnp.float32), 1.0, 0.0
+            ).astype(jnp.bfloat16)
 
     def look(part, cut):
-        at = slice(part * half, (part + 1) * half)
+        at = slice(part * (depth // 2), (part + 1) * (depth // 2))
+        span = slice(cut * width, (cut + 1) * width)
         if part == 0:
             table_copies[cut].wait()
-        for block in range(width // LANES):
-            number_ = (lane + (cut * width + block * LANES)).astype(jnp.float32)
-            chosen[:, block * LANES : (block + 1) * LANES] = jnp.where(
-                column_ids[at, :] == number_, 1.0, 0.0
-            ).astype(jnp.bfloat16)
-        found = jnp.dot(chosen[...], table[cut * width : (cut + 1) * width, :], preferred_element_type=jnp.float32)
+        found = jnp.dot(chosen[:, span], table[span, at], preferred_element_type=jnp.float32)
         if cut == 0:
-            picked[at, :] = found
+            picked[:, at] = found
         else:
-            picked[at, :] += found
+            picked[:, at] += found
+        if part == 0 and cut + 1 < cuts:
+            choose(cut + 1)
 
     line_sum = LineSum(
-        count, chunk, lambda at: picked[at, :],
+        count, 2, lambda at: picked[at],
         land, held, stream_ref, inner_sem, outer_sem, receive_sem,
     )
 
@@ -740,12 +777,14 @@
         plane.own(3)
 
     between = {
-        (0, 0): lambda: turn(0),
-        (0, 1): lambda: plane.relay_side(2),
-        (0, 3): lambda: turn(1),
+        (0, 0): lambda: choose(0),
+        (0, 3): lambda: turn(0),
         (0, 4): lambda: turn_out(),
-        (0, 5): lambda: plane.relay_core(2),
-        (0, 7): lambda: plane.relay_side(0),
+        (0, 5): lambda: plane.relay_side(2),
+        (0, 7): lambda: turn(1),
+        (0, 9): lambda: plane.relay_core(2),
+        (1, 4): lambda: plane.relay_side(0),
+        (1, 8): lambda: plane.relay_core(0),
     }
     for part in range(2):
         for cut in range(cuts):
@@ -756,8 +795,6 @@
             work()
         line_sum.begin(range(part * count // 2, (part + 1) * count // 2))
     todo = [
-        lambda: plane.relay_core(0),
-        lambda: None,
         lambda: plane.relay_side(1),
         lambda: plane.relay_side(3),
         lambda: None,
@@ -773,8 +810,11 @@
     line_sum.run(3, todo)
     for peer in peers:
         arrived(bias_out.at[peer], bias_receive.at[peer], {"seq": peer})
-    for copy in crossing + bias_copies + tile_copies:
+    for copy in bias_copies + tile_copies:
         copy.wait_send()
+    for array in range(2):
+        for index, other in enumerate(planes):
+            departed(outs[array].at[spot, place], cross_send.at[array, index], {"batch": other})
 
     @pl.when(jnp.logical_not(stays))
     def _():
@@ -784,38 +824,45 @@
     line_sum.finish()
 
 
-def front(tile, table, joined, fc, proj, out, bias):
+def front(ids, weights, padding, table, joined, fc, trans, out, bias):
     size = lax.axis_size("seq")
     lines = lax.axis_size("batch")
     vocab, depth = table.shape
-    rows = lines * tile.shape[1]
+    tokens = ids.shape[1]
+    rows = lines * tokens
+    own_rows = joined.shape[0]
     count = 16
     vmem = pl.BlockSpec(memory_space=pltpu.VMEM)
+    smem = pl.BlockSpec(memory_space=pltpu.SMEM)
     anywhere = pl.BlockSpec(memory_space=pl.ANY)
     dma = pltpu.SemaphoreType.DMA
     bf16 = jnp.bfloat16
-    spread = lambda part, kind: jax.ShapeDtypeStruct((size,) + part.shape, kind)
+    padded = pl.cdiv(vocab, VOCAB_TILE) * VOCAB_TILE
+    hidden = math.prod(fc.shape) // own_rows // lines
     return pl.pallas_call(
         functools.partial(front_kernel, count),
-        in_specs=[vmem, anywhere, anywhere, anywhere, anywhere, anywhere, vmem],
+        in_specs=[vmem, vmem, smem, anywhere, anywhere, anywhere, vmem, anywhere, vmem],
         out_specs=[vmem, vmem, anywhere, anywhere, anywhere, anywhere, vmem],
         out_shape=[
-            jax.ShapeDtypeStruct((lines,) + tile.shape, tile.dtype),
+            jax.ShapeDtypeStruct((lines, 8, tokens), jnp.int32),
             jax.ShapeDtypeStruct((rows, depth), bf16),
-            spread(joined, bf16),
-            spread(fc, bf16),
-            spread(proj, bf16),
-            spread(out, bf16),
-            spread(bias, jnp.float32),
+            jax.ShapeDtypeStruct((size, lines, own_rows, 3 * depth // lines), bf16),
+            jax.ShapeDtypeStruct((size, lines, own_rows, hidden), bf16),
+            jax.ShapeDtypeStruct((size,) + trans.shape[1:], bf16),
+            jax.ShapeDtypeStruct((size,) + out.shape, bf16),
+            jax.ShapeDtypeStruct((size, 8, LANES), jnp.float32),
         ],
         scratch_shapes=[
-            pltpu.VMEM((pl.cdiv(vocab, VOCAB_TILE) * VOCAB_TILE, depth), bf16),
+            pltpu.VMEM((padded, depth), bf16),
             pltpu.VMEM((rows, LANES), jnp.float32),
-            pltpu.VMEM((rows // 2, VOCAB_TILE), bf16),
+            pltpu.VMEM((rows, padded), bf16),
             pltpu.VMEM((rows, depth), jnp.float32),
+            pltpu.VMEM((8, tokens), jnp.int32),
+            pltpu.VMEM((8, LANES), jnp.float32),
+            pltpu.VMEM(trans.shape[1:], bf16),
         ] + LineSum.scratch(count, rows, depth) + [
-            dma((6,)),
-            dma((pl.cdiv(vocab, VOCAB_TILE),)),
+            dma((7 + size,)),
+            dma((padded // VOCAB_TILE,)),
             dma((lines - 1,)),
             dma((lines,)),
             dma((3, lines - 1)),
@@ -828,7 +875,7 @@
             collective_id=1, has_side_effects=True, vmem_limit_bytes=VMEM_BYTES
         ),
         name="front",
-    )(tile, table, joined, fc, proj, out, bias)
+    )(ids, weights, padding, table, joined, fc, trans, out, bias)
 
 
 def row_norm(values):
@@ -840,10 +887,10 @@
 
 def layer_kernel(
     count, heads,
-    stream_ref, joined_ref, fc_ref, proj_ref, out_ref, trans_ref,
-    gains_ref, offsets_ref, joined_bias, fc_bias, trans_bias, turns_ref, table_ref,
+    stream_ref, joined_ref, fc_ref, proj_ref, out_ref, trans_ref, next_ref,
+    gains_ref, offsets_ref, wide_ref, bias_ref, turns_ref, table_ref,
     states_ref, moved_ref, low_ref, logits_ref,
-    first_trans, second_trans, x_attn, x_mlp, spread, gathered, mixed, returned, part,
+    proj_all, second_trans, trans_bias, fc_bias, hidden, x_attn, x_mlp, spread, gathered, mixed, returned, part,
     land, inner_sem, outer_sem, receive_sem,
     tables, turned, logits, table_sem, logits_sem,
     local_sem, heads_send, heads_receive, rows_send, rows_receive, plane_send, plane_receive,
@@ -862,8 +909,10 @@
     columns = spread.shape[3]
     groups = plane_width // columns
     head_dim = columns // heads
+    hidden_rows = proj_ref.shape[0]
+    own_width = next_ref.shape[1]
     step_rows = 32
-
+    wide_rows = 2 * tokens
     vocab = table_ref.shape[0]
     cut_rows = tables.shape[1]
     cuts = pl.cdiv(vocab, cut_rows)
@@ -896,9 +945,9 @@
         if cut + 2 < cuts:
             loads[cut + 2].start()
 
-    spans = (first_trans, second_trans)
-    for probe in range(2):
-        spans[probe][spot] = trans_ref[probe].astype(bf16)
+    spans = (proj_all, second_trans)
+    proj_all[spot] = proj_ref[...]
+    second_trans[spot] = next_ref[1].astype(bf16)
     greet([{"batch": plane} for plane in planes] + [{"seq": peer} for peer in peers])
     sent = []
 
@@ -916,12 +965,13 @@
 
     lax.fori_loop(0, rows // step_rows, norms, 0, unroll=4)
     half_rot = ROT // 2
-    for sequence in range(lines):
-        at = slice(sequence * tokens, (sequence + 1) * tokens)
-        for kind in range(3):
-            place_ = slice(kind * plane_width, (kind + 1) * plane_width)
-            value = jnp.dot(x_attn[at, :], joined_ref[:, place_], preferred_element_type=f32)
-            value = value + joined_bias[0:1, place_]
+    for kind in range(3):
+        bias = wide_ref[0:1, pl.ds(pl.multiple_of(kind * depth + place * plane_width, LANES), plane_width)]
+        whole = jnp.dot(
+            x_attn[...], joined_ref[:, kind * plane_width : (kind + 1) * plane_width], preferred_element_type=f32
+        )
+        for sequence in range(lines):
+            value = whole[sequence * tokens : (sequence + 1) * tokens] + bias
             if kind < 2:
                 value = (
                     value * turns_ref[0]
@@ -939,15 +989,16 @@
     heads_copy.start()
     plane.own(0)
     plane.own(1)
-
-    def hidden_part(index, carry):
-        at = pl.ds(pl.multiple_of(index * tokens, tokens), tokens)
-        value = jnp.dot(x_mlp[at, :], fc_ref[...], preferred_element_type=f32) + fc_bias[...]
-        value = 0.5 * value * (1.0 + lax.erf(value * (0.5 ** 0.5)))
-        part[at, :] = jnp.dot(value.astype(bf16), proj_ref[...], preferred_element_type=f32)
-        return carry
-
-    lax.fori_loop(0, lines, hidden_part, 0)
+    for source in range(size):
+        at = slice(source * own_width, (source + 1) * own_width)
+        trans_bias[:, at] = bias_ref[source, 0:2, 0:own_width]
+        at = slice(source * hidden_rows, (source + 1) * hidden_rows)
+        if hidden_rows % LANES:
+            begin = wide_ref.shape[1] - fc_ref.shape[1]
+            fc_bias[:, at] = wide_ref[0:1, begin + source * hidden_rows : begin + (source + 1) * hidden_rows]
+        else:
+            begin = pl.multiple_of(3 * depth + (source * lines + place) * hidden_rows, LANES)
+            fc_bias[:, at] = wide_ref[0:1, pl.ds(begin, hidden_rows)]
 
     def translate(probe, stream, low, weights, at):
         moved = stream + jnp.dot(low, weights, preferred_element_type=f32) + trans_bias[probe : probe + 1, :]
@@ -956,13 +1007,17 @@
             row_norm(moved) * gains_ref[2:3, :] + offsets_ref[4:5, :]
         ).astype(bf16)
 
-    def first_probe(sequence):
-        at = slice(sequence * tokens, (sequence + 1) * tokens)
+    for begin in range(0, rows, wide_rows):
+        at = slice(begin, begin + wide_rows)
         low = stream_ref[at, :]
-        translate(0, low.astype(f32), low, first_trans[...].reshape(depth, depth), at)
-
-    plane.relay_side(0)
-    plane.relay_core(0)
+        translate(0, low.astype(f32), low, trans_ref[...], at)
+    turned[...] = jnp.transpose(states_ref[1])
+    for begin in range(0, fc_ref.shape[1], 256):
+        at = slice(begin, begin + 256)
+        for row in range(0, rows, 512):
+            span = slice(row, row + 512)
+            value = jnp.dot(x_mlp[span, :], fc_ref[:, at], preferred_element_type=f32) + fc_bias[:, at]
+            hidden[span, at] = (0.5 * value * (1.0 + lax.erf(value * (0.5 ** 0.5)))).astype(bf16)
     heads_copy.wait()
     for peer in peers:
         arrived(gathered.at[peer], heads_receive.at[peer], {"seq": peer})
@@ -998,11 +1053,18 @@
         )
     rows_copy = pltpu.make_async_copy(mixed.at[spot], returned.at[spot], local_sem.at[1])
     rows_copy.start()
+    plane.relay_side(0)
     plane.relay_side(1)
+    probe_logits(0)
+    probe_logits(1)
+    plane.relay_core(0)
+    probe_logits(2)
     plane.receive_core(0)
-    for sequence in range(lines):
-        first_probe(sequence)
-    turned[...] = jnp.transpose(states_ref[1])
+    for begin in range(0, depth, 256):
+        at = slice(begin, begin + 256)
+        part[:, at] = jnp.dot(
+            hidden[...], proj_all[:, :, at].reshape(size * hidden_rows, 256), preferred_element_type=f32
+        )
     rows_copy.wait()
     for peer in peers:
         arrived(returned.at[peer], rows_receive.at[peer], {"seq": peer})
@@ -1013,27 +1075,22 @@
         )
         part[at, :] += jnp.dot(attended, out_ref[...], preferred_element_type=f32)
     line_sum = LineSum(
-        count, rows // count, lambda at: part[at, :],
+        count, 1, lambda at: part[at],
         land, x_attn, x_mlp, inner_sem, outer_sem, receive_sem,
     )
     line_sum.begin(range(count))
-    todo = [functools.partial(probe_logits, cut) for cut in range(cuts)]
-    todo[3:3] = [lambda: plane.relay_core(1)]
+    todo = [functools.partial(probe_logits, cut) for cut in range(3, cuts)]
+    todo[2:2] = [lambda: plane.relay_core(1)]
     todo[7:7] = [lambda: plane.receive_core(1)]
     line_sum.run(3, todo)
 
-    def second_probe(index, carry):
-        at = pl.ds(pl.multiple_of(index * tokens, tokens), tokens)
-        stream = (
-            stream_ref[at, :].astype(f32) + x_mlp[at, :].astype(f32) + offsets_ref[2:3, :] + offsets_ref[3:4, :]
-        )
+    for begin in range(0, rows, wide_rows):
+        at = slice(begin, begin + wide_rows)
+        stream = stream_ref[at, :].astype(f32) + x_mlp[at, :].astype(f32) + offsets_ref[2:3, :] + offsets_ref[3:4, :]
         states_ref[0, at, :] = (row_norm(stream) * gains_ref[2:3, :] + offsets_ref[4:5, :]).astype(bf16)
         low = stream.astype(bf16)
         low_ref[at, :] = low
         translate(1, stream, low, second_trans[...].reshape(depth, depth), at)
-        return carry
-
-    lax.fori_loop(0, lines, second_probe, 0)
     for copy in sent:
         copy.wait_send()
     for copy in stores[-2:]:
@@ -1042,7 +1099,7 @@
     line_sum.finish()
 
 
-def layer(stream, joined, fc, proj, out, trans, gains, offsets, joined_bias, fc_bias, trans_bias, turns, table):
+def layer(stream, joined, fc, proj, out, trans, next_trans, gains, offsets, wide, bias, turns, table):
     size = lax.axis_size("seq")
     lines = lax.axis_size("batch")
     rows, depth = stream.shape
@@ -1056,6 +1113,7 @@
     vmem = pl.BlockSpec(memory_space=pltpu.VMEM)
     anywhere = pl.BlockSpec(memory_space=pl.ANY)
     dma = pltpu.SemaphoreType.DMA
+    sums = LineSum.scratch(count, rows, depth)
     return pl.pallas_call(
         functools.partial(layer_kernel, count, own_heads),
         in_specs=[vmem] * 12 + [anywhere],
@@ -1067,8 +1125,11 @@
             jax.ShapeDtypeStruct((tiles, VOCAB_TILE, rows), f32),
         ],
         scratch_shapes=[
-            pltpu.VMEM((size,) + trans.shape[1:], bf16),
-            pltpu.VMEM((size,) + trans.shape[1:], bf16),
+            pltpu.VMEM((size,) + proj.shape, bf16),
+            pltpu.VMEM((size,) + next_trans.shape[1:], bf16),
+            pltpu.VMEM((2, depth), f32),
+            pltpu.VMEM((1, fc.shape[1]), f32),
+            pltpu.VMEM((rows, fc.shape[1]), bf16),
             pltpu.VMEM((rows, depth), bf16),
             pltpu.VMEM((rows, depth), bf16),
             pltpu.VMEM((size, 3, tokens, columns), bf16),
@@ -1076,7 +1137,7 @@
             pltpu.VMEM((size, tokens, columns), bf16),
             pltpu.VMEM((size, tokens, columns), bf16),
             pltpu.VMEM((rows, depth), f32),
-        ] + LineSum.scratch(count, rows, depth)[:1] + LineSum.scratch(count, rows, depth)[2:] + [
+        ] + sums[:1] + sums[2:] + [
             pltpu.VMEM((2, VOCAB_TILE // 2, depth), bf16),
             pltpu.VMEM((depth, rows), bf16),
             pltpu.VMEM((2, VOCAB_TILE // 2, rows), f32),
@@ -1092,7 +1153,7 @@
             collective_id=2, has_side_effects=True, vmem_limit_bytes=VMEM_BYTES
         ),
         name="layer",
-    )(stream, joined, fc, proj, out, trans, gains, offsets, joined_bias, fc_bias, trans_bias, turns, table)
+    )(stream, joined, fc, proj, out, trans, next_trans, gains, offsets, wide, bias, turns, table)
 
 
 def stats_kernel(
@@ -1174,8 +1235,9 @@
 
 def reduce_kernel(
     count,
-    grad_ref, bias_ref, note_ref,
-    total_ref, bias_out, note_out,
+    grad_ref, bias_ref, note_ref, trans_ref, mom1_ref, mom2_ref, trans_bias, mom1_bias, mom2_bias,
+    first_out, second_out, weight_out, first_bias, second_bias, weight_bias, result_out,
+    total_ref, note_out, weights, firsts, seconds, adam_sem,
     mine, sibling_land, side_land, line_land, side_sum, line_part, last_land, own_sum,
     land, held, inner_sem, outer_sem, receive_sem,
     tile_land, tile_line, tile_out,
@@ -1214,6 +1276,12 @@
             )
             copy.start()
             loads[chunk, step, index] = copy
+    fetches = [
+        pltpu.make_async_copy(source, target, adam_sem.at[index])
+        for index, (source, target) in enumerate(((trans_ref, weights), (mom1_ref, firsts), (mom2_ref, seconds)))
+    ]
+    for copy in fetches:
+        copy.start()
     tile_land[spot] = bias_ref[spot]
     greet([{"batch": plane} for plane in planes] + [{"seq": peer} for peer in peers])
     for chunk in range(count):
@@ -1229,7 +1297,7 @@
             push(bias_ref.at[peer], tile_land.at[spot], bias_send.at[index], bias_receive.at[spot], {"seq": peer})
         )
     line_sum = LineSum(
-        count, 2 * step_rows, lambda at: own_sum[at, :],
+        count, 1, lambda at: own_sum[at],
         land, held, total_ref, inner_sem, outer_sem, receive_sem,
     )
 
@@ -1341,7 +1409,6 @@
     tile = tile_line[0]
     for source in range(1, lax.axis_size("batch")):
         tile += tile_line[source]
-    bias_out[...] = tile
     head = jnp.sum(squares[0] + tile * tile, axis=0, keepdims=True)
     row8 = lax.broadcasted_iota(jnp.int32, (8, LANES), 0)
     tile_out[...] = jnp.where(row8 == 0, head, note_ref[...])
@@ -1352,12 +1419,33 @@
         )
     for peer in peers:
         arrived(note_out.at[peer], note_receive.at[peer], {"seq": peer})
+    notes = note_out[0]
+    for source in range(1, size):
+        notes += note_out[source]
+    sums = jnp.sum(notes, axis=-1, keepdims=True)
+    norm = jnp.sqrt(sums[0:1]) / sums[2:3]
+    result_out[...] = jnp.broadcast_to(jnp.where(row8[:, 0:1] == 0, norm, sums), (8, LANES))
+    factor = jnp.minimum(1.0, clip_max / (norm + 1e-06)) / sums[2:3]
+    for copy in fetches:
+        copy.wait()
+    for chunk in range(count):
+        for probe in range(2):
+            begin = (2 * chunk + probe) * step_rows
+            at = slice(chunk * step_rows, (chunk + 1) * step_rows)
+            gradient = total_ref[begin : begin + step_rows, :].astype(f32) * factor
+            first_out[probe, at, :], second_out[probe, at, :], weight_out[probe, at, :] = adam_update(
+                weights[probe, at, :], gradient, firsts[probe, at, :], seconds[probe, at, :]
+            )
+    gradient = tile[0:2, 0 : trans_bias.shape[1]] * factor
+    first_bias[...], second_bias[...], weight_bias[...] = adam_update(
+        trans_bias[...], gradient, mom1_bias[...], mom2_bias[...]
+    )
     for copy in sent:
         copy.wait_send()
     line_sum.finish()
 
 
-def reduce_gradients(grad, bias, note):
+def reduce_gradients(grad, bias, note, *optimizer):
     size = lax.axis_size("seq")
     lines = lax.axis_size("batch")
     _, _, width, depth = grad.shape
@@ -1368,16 +1456,22 @@
     vmem = pl.BlockSpec(memory_space=pltpu.VMEM)
     dma = pltpu.SemaphoreType.DMA
     near = max(rows - 1, 1)
-    total, bias_sum, notes = pl.pallas_call(
+    anywhere = pl.BlockSpec(memory_space=pl.ANY)
+    f32 = jnp.float32
+    return pl.pallas_call(
         functools.partial(reduce_kernel, count),
-        in_specs=[pl.BlockSpec(memory_space=pl.ANY), vmem, vmem],
-        out_specs=[vmem, vmem, vmem],
-        out_shape=[
-            jax.ShapeDtypeStruct((2 * width, depth), bf16),
-            jax.ShapeDtypeStruct(bias.shape[1:], jnp.float32),
-            jax.ShapeDtypeStruct((size,) + note.shape, jnp.float32),
-        ],
+        in_specs=[anywhere, vmem, vmem, anywhere, anywhere, anywhere, vmem, vmem, vmem],
+        out_specs=[vmem] * 7,
+        out_shape=[jax.ShapeDtypeStruct((2, width, depth), f32)] * 3
+        + [jax.ShapeDtypeStruct((2, width), f32)] * 3
+        + [jax.ShapeDtypeStruct(note.shape, f32)],
         scratch_shapes=[
+            pltpu.VMEM((2 * width, depth), bf16),
+            pltpu.VMEM((size,) + note.shape, f32),
+            pltpu.VMEM((2, width, depth), f32),
+            pltpu.VMEM((2, width, depth), f32),
+            pltpu.VMEM((2, width, depth), f32),
+            dma((3,)),
             pltpu.VMEM((count, rows, 2, 2, cut, depth), bf16),
             pltpu.VMEM((count, rows, 2, 2, cut, depth), bf16),
             pltpu.VMEM((count, rows, cut, depth), bf16),
@@ -1410,9 +1504,7 @@
             collective_id=6, has_side_effects=True, vmem_limit_bytes=VMEM_BYTES
         ),
         name="reduce_gradients",
-    )(grad, bias, note)
-    total = jnp.transpose(total.reshape(count, 2, cut, depth), (1, 0, 2, 3)).reshape(2, width, depth)
-    return total, bias_sum, notes
+    )(grad, bias, note, *optimizer)
 
 
 def body(
@@ -1466,36 +1558,31 @@
     )
     turns = jnp.tile(turns, (1, 1, plane_heads))
 
-    def plane_part(vector, parts, size):
-        return lax.dynamic_slice_in_dim(vector.reshape(parts, n_batch, size), batch_index, 1, 1).reshape(1, -1)
-
-    joined_bias = plane_part(wide_bias[: 3 * width], 3, plane_width)
-    fc_bias = plane_part(wide_bias[3 * width :], n_seq, hidden_rows)
-    padding = jnp.broadcast_to(pad_lengths[:, None], (1, tok_rows))
-    tile = jnp.concatenate([token_ids, pos_weights, padding, jnp.zeros((5, tok_rows), jnp.int32)], axis=0)
-    own_rows = w_qkv.shape[0]
-    joined_cut = jnp.transpose(w_qkv.reshape(own_rows, 3, n_batch, plane_width), (2, 0, 1, 3))
-    joined_cut = joined_cut.reshape(n_batch, own_rows, 3 * plane_width)
-    fc_cut = jnp.transpose(w_fc.reshape(own_rows, n_seq, n_batch, hidden_rows), (2, 0, 1, 3))
-    fc_cut = fc_cut.reshape(n_batch, own_rows, n_seq * hidden_rows)
+    wide = wide_bias[None, :]
+    fc = w_fc
+    if hidden_rows % LANES:
+        fc = jnp.transpose(w_fc.reshape(-1, n_seq, n_batch, hidden_rows), (2, 0, 1, 3))
+        fc = fc.reshape(n_batch, -1, n_seq * hidden_rows)
+        fc_bias = lax.dynamic_slice_in_dim(
+            wide_bias[3 * width :].reshape(n_seq, n_batch, hidden_rows), batch_index, 1, 1
+        ).reshape(1, -1)
+        wide = jnp.concatenate([wide, fc_bias], axis=1)
     own_width = trans_bias.shape[1]
-    bias_tile = jnp.zeros((8, LANES), f32).at[:2, :own_width].set(trans_bias)
-    tiles, stream_low, joined_w, fc_w, proj_w, out_w, bias_all = front(
-        tile, embed_in, joined_cut, fc_cut, w_proj, w_out, bias_tile
+    tiles, stream_low, joined_w, fc_w, trans_low, out_w, bias_all = front(
+        token_ids, pos_weights, pad_lengths, embed_in, w_qkv, fc, trans_weight, w_out, trans_bias
     )
-    bias_full = jnp.transpose(bias_all[:, :2, :own_width], (1, 0, 2)).reshape(2, width)
     states, translated, low1, probe_logits = layer(
         stream_low,
         joined_w.reshape(width, 3 * plane_width),
         fc_w.reshape(width, n_seq * hidden_rows),
-        proj_w.reshape(n_seq * hidden_rows, width),
+        w_proj,
         out_w.reshape(plane_width, width),
+        trans_low.reshape(width, width),
         trans_weight,
         norm_gains,
         layer_biases,
-        joined_bias,
-        fc_bias,
-        bias_full,
+        wide,
+        bias_all,
         turns,
         unembed,
     )
@@ -1507,17 +1594,10 @@
     bias_grad = jnp.transpose(bias_grad.reshape(2, n_seq, own_width), (1, 0, 2))
     bias_grad = jnp.pad(bias_grad, ((0, 0), (0, 6), (0, LANES - own_width)))
     grad = grad.reshape(2, n_seq, own_width, width)
-    grad_sum, bias_sum, notes = reduce_gradients(grad, bias_grad, note)
-    sums = jnp.sum(notes, axis=(0, 2))
-    loss_sum = sums[1]
-    token_count = jnp.round(sums[2])
-    grad_norm = jnp.sqrt(sums[0]) / token_count
-    factor = jnp.minimum(1.0, clip_max / (grad_norm + 1e-06)) / token_count
-    grad_w = grad_sum.astype(f32) * factor
-    grad_b = bias_sum[:2, : trans_bias.shape[1]] * factor
-    first_w, second_w, new_w = adam_update(trans_weight, grad_w, mom1_weight, mom2_weight)
-    first_b, second_b, new_b = adam_update(trans_bias, grad_b, mom1_bias, mom2_bias)
-    return (loss_sum, token_count, grad_norm, first_w, second_w, new_w, first_b, second_b, new_b)
+    first_w, second_w, new_w, first_b, second_b, new_b, result = reduce_gradients(
+        grad, bias_grad, note, trans_weight, mom1_weight, mom2_weight, trans_bias, mom1_bias, mom2_bias
+    )
+    return (result[1, 0], result[2, 0], result[0, 0], first_w, second_w, new_w, first_b, second_b, new_b)
 
 
 def solution(mesh):

time: 349 us -> 333 us (0.954)
  other arithmetic: 7.05 us -> 0.22 us
  between operations: 5.65 us -> 1.6 us
    pallas_call x2, Pallas kernels: 125 us -> 136 us  [the longest x1 80.2 us: front(): pl.pallas_call(functools.partial(front_kernel, count), in_specs=[vmem, vm...]
    pallas_call x1, Pallas kernels: 87.3 us -> 79.2 us  [layer(): pl.pallas_call(functools.partial(layer_kernel, count, own_heads), in_spec...]
    unnamed x12 -> x14, local copies, waits for them, and re-layouts: 0.03 us -> 7.28 us
    reshape x8 -> x0, local copies, waits for them, and re-layouts: 5.99 us -> none  [the longest x1 1.36 us: body(): jnp.transpose(bias_all[:, :2, :own_width], (1, 0, 2)).reshape(2, width)]
where the time goes in v7:
time: 333 us; the launch traced here: 330 us
  Pallas kernels  317 us (95%)
  local copies, waits for them, and re-layouts  11 us (3%)
    pallas_call x1, Pallas kernels, front(): pl.pallas_call(functools.partial(front_kernel, count), in_specs=[vmem, vm...  80.2 us
    pallas_call x1, Pallas kernels, layer(): pl.pallas_call(functools.partial(layer_kernel, count, own_heads), in_spec...  79.2 us
    pallas_call x1, Pallas kernels, reduce_gradients(): pl.pallas_call(functools.partial(reduce_kernel, count), in_specs=[anywher...  55.5 us
    pallas_call x1, Pallas kernels, vocab_forward(): pl.pallas_call(functools.partial(forward_kernel, vocab), grid=(tiles + 1,...  51.3 us
    pallas_call x1, Pallas kernels, vocab_backward(): pl.pallas_call(functools.partial(backward_kernel, vocab), grid=(tiles + 1...  43.9 us
    unnamed x14, local copies, waits for them, and re-layouts  7.28 us
    pallas_call x1, Pallas kernels, statistics(): pl.pallas_call(stats_kernel, in_specs=[vmem] * 4, out_specs=[vmem] * 2, o...  7.24 us

profile of v7, /device:TPU:0, one launch (start us, length us, event | category | flops | bytes accessed | tf_op | source)
XLA Modules:
  0.0 330.1 jit_solution(13622112178783597865)
XLA Ops:
  1.3 0.1 pad.16.clone
  1.4 0.1 pad.13.clone
  1.5 0.1 multiply_cosine_fusion
  1.6 0.1 maximum_bitcast_fusion.1
  1.7 0.9 copy.27.turns_ref
  2.7 80.2 %front.1 = (s32[4,8,128]{2,1,0:T(8,128)}, bf16[512,1024]{1,0:T(8,128)(2,1)}, bf16[8,4,32,768]{3,2,1,0:T(8,128)(2,1)}, bf16[8,4,32,1024]{3,2,1,0:T(8,128)(2,1)}, ...) custom-call(s32[1,128]{1,0:T(1,128)} %ids_ref.1, s32[1,128]{1,0:T(1,128)} %weights_ref.1, ...), custom_call_target="tpu_custom_call" | custom-call | tf_op jit(solution)/shard_map/front/pallas_call | solution.py:842
  82.8 79.2 %layer.1 = (bf16[3,512,1024]{2,1,0:T(8,128)(2,1)}, f32[2,512,1024]{2,1,0:T(8,128)}, bf16[512,1024]{1,0:T(8,128)(2,1)}, f32[10,1280,512]{2,1,0:T(8,128)}) custom-call(bf16[512,1024]{1,0:T(8,128)(2,1)} %get-tuple-element.36.stream_ref.low0_ref, bf16[1024,768]{1,0:T(8,128)(2,1)} %bitcast.22, bf16[1024,1024]{1,0:T(8,128)(2,1)} %bitcast.20, ...), custom_call_target="tpu_custom_call" | custom-call | tf_op jit(solution)/shard_map/layer/pallas_call | solution.py:1117
  162.0 51.3 %vocab_forward.1 = (bf16[10,3,1280,256]{3,2,1,0:T(8,128)(2,1)}, bf16[10,3,1280,256]{3,2,1,0:T(8,128)(2,1)}, f32[10,3,512]{2,1,0:T(4,128)}, f32[3,8,512]{2,1,0:T(8,128)}, f32[2,8,512]{2,1,0:T(8,128)}) custom-call(bf16[3,512,1024]{2,1,0:T(8,128)(2,1)} %get-tuple-element.42.states_ref, bf16[12576,1024]{1,0:T(8,128)(2,1)} %table_ref.7, ...), custom_call_target="tpu_custom_call" | custom-call | flops 26373783552 | bytes 90144768 | tf_op jit(solution)/shard_map/vocab_forward/pallas_call | solution.py:186
  213.4 7.2 %statistics.1 = (f32[10,3,512]{2,1,0:T(4,128)}, f32[8,128]{1,0:T(8,128)}) custom-call(s32[4,8,128]{2,1,0:T(8,128)} %get-tuple-element.46.tiles_ref, f32[10,3,512]{2,1,0:T(4,128)} %get-tuple-element.47.peaks_ref, f32[3,8,512]{2,1,0:T(8,128)} %get-tuple-element.48.sums_ref, f32[2,8,512]{2,1,0:T(8,128)} %get-tuple-element.49.cross_ref), custom_call_target="tpu_custom_call" | custom-call | tf_op jit(solution)/shard_map/statistics/pallas_call | solution.py:1218
  220.6 43.9 %vocab_backward.1 = (bf16[2,1024,1024]{2,1,0:T(8,128)(2,1)}, f32[2,1024]{1,0:T(2,128)}) custom-call(bf16[10,3,1280,256]{3,2,1,0:T(8,128)(2,1)} %get-tuple-element.44.first_ref, bf16[10,3,1280,256]{3,2,1,0:T(8,128)(2,1)} %get-tuple-element.45.second_ref, f32[10,3,512]{2,1,0:T(4,128)} %get-tuple-element.50.scales_ref, bf16[12576,1024]{1,0:T(8,128)(2,1)} %table_ref.7, ...), custom_call_target="tpu_custom_call" | custom-call | flops 28521267200 | bytes 64389120 | tf_op jit(solution)/shard_map/vocab_backward/pallas_call | solution.py:328
  264.5 1.3 pad.4.bias_ref
  265.8 55.5 %reduce_gradients.1 = (f32[2,128,1024]{2,1,0:T(8,128)}, f32[2,128,1024]{2,1,0:T(8,128)}, f32[2,128,1024]{2,1,0:T(8,128)}, f32[2,128]{1,0:T(2,128)}, f32[2,128]{1...) custom-call(bf16[2,8,128,1024]{3,2,1,0:T(8,128)(2,1)} %bitcast.19, f32[8,8,128]{2,1,0:T(8,128)} %pad.4.bias_ref, ...), custom_call_target="tpu_custom_call" | custom-call | tf_op jit(solution)/shard_map/reduce_gradients/pallas_call | solution.py:1461
  321.3 0.0 copy-start
  321.3 0.0 copy-start.3
  321.3 0.0 copy-start.2
  321.3 0.0 copy-start.1
  321.3 1.3 fusion.1
  322.6 2.3 copy.35
  324.9 2.3 copy.36
  327.2 0.0 copy-done
  327.2 1.0 copy.37
  328.2 0.0 copy-done.3
  328.2 0.6 copy.38
  328.8 0.0 copy-done.2
  328.8 0.6 copy.39
  329.3 0.0 copy-done.1
  329.3 0.6 copy.40
  (7 shorter events, 0.1 us)
Async XLA Ops:
  321.3 5.9 %copy-start = (f32[2,128,1024]{2,1,0:T(8,128)S(1)}, f32[2,128,1024]{2,1,0:T(8,128)}, u32[]{:S(2)}) copy-start(f32[2,128,1024]{2,1,0:T(8,128)} %get-tuple-element.86) | copy-start | bytes 3145732
  321.3 6.9 %copy-start.3 = (f32[2,128]{1,0:T(2,128)S(1)}, f32[2,128]{1,0:T(2,128)}, u32[]{:S(2)}) copy-start(f32[2,128]{1,0:T(2,128)} %get-tuple-element.87) | copy-start | bytes 3076
  321.3 7.5 %copy-start.2 = (f32[2,128]{1,0:T(2,128)S(1)}, f32[2,128]{1,0:T(2,128)}, u32[]{:S(2)}) copy-start(f32[2,128]{1,0:T(2,128)} %get-tuple-element.88) | copy-start | bytes 3076
  321.3 8.0 %copy-start.1 = (f32[2,128]{1,0:T(2,128)S(1)}, f32[2,128]{1,0:T(2,128)}, u32[]{:S(2)}) copy-start(f32[2,128]{1,0:T(2,128)} %get-tuple-element.89) | copy-start | bytes 3076
